TPU v7x, 32 devices: a whole 2x2x4 slice. The times are simulated.
32 devices in a mesh: dp: 8 (over z, y), unit: 4 (over x, core).
Axes of the slice: x: 2, y: 2, z: 4, core: 2. Of those that a mesh axis runs over, the one named last changes fastest.
Arguments:
- layer_input: bfloat16 [32768, 768], P(('dp', 'unit')), may hold values from -18 to 18
- teacher: bfloat16 [32768, 768], P(('dp', 'unit')), may hold values from -18 to 18
- cotangent: bfloat16 [32768, 768], P(('dp', 'unit')), may hold values from -6 to 6
- key_valid: int32 [32768], P(('dp', 'unit')), may hold values 0 or 1
- seg_lengths: int32 [32, 3], P(('dp', 'unit')), may hold values from 1 to 512, 1024 in all within a row
- head_mask: int32 [12], replicated, may hold values from 0 to 1, as said below
- hidden_mask: int32 [768], replicated, may hold values 0 or 1
- inter_mask: int32 [3072], replicated, may hold values 0 or 1
- proj_master: float32 [768, 3840], P(('dp', 'unit')), may hold values from -0.649519 to 0.649519
- proj_first: float32 [768, 3840], P(('dp', 'unit')), may hold values from -0.00061035156 to 0.00061035156
- proj_second: float32 [768, 3840], P(('dp', 'unit')), may hold values from 6.5123705e-11 to 1.0419793e-09
- up_master: float32 [768, 3072], P('dp', 'unit'), may hold values from -0.21875 to 0.21875
- up_first: float32 [768, 3072], P('dp', 'unit'), may hold values from -0.00061035156 to 0.00061035156
- up_second: float32 [768, 3072], P('dp', 'unit'), may hold values from 6.5123705e-11 to 1.0419793e-09
- down_master: float32 [3072, 768], P('unit', 'dp'), may hold values from -0.21875 to 0.21875
- down_first: float32 [3072, 768], P('unit', 'dp'), may hold values from -0.00061035156 to 0.00061035156
- down_second: float32 [3072, 768], P('unit', 'dp'), may hold values from 6.5123705e-11 to 1.0419793e-09
- vector_master: float32 [13, 768], replicated, may hold values from -1 to 2.5
- vector_first: float32 [13, 768], replicated, may hold values from -0.00061035156 to 0.00061035156
- vector_second: float32 [13, 768], replicated, may hold values from 6.5123705e-11 to 1.0419793e-09
Outputs:
- layer_out: bfloat16 [32768, 768], P(('dp', 'unit'))
- input_grad: float32 [32768, 768], P(('dp', 'unit'))
- grad_norm: float32 [], replicated
- distill_loss: float32 [], replicated
- proj_master_new: float32 [768, 3840], P(('dp', 'unit'))
- proj_first_new: float32 [768, 3840], P(('dp', 'unit'))
- proj_second_new: float32 [768, 3840], P(('dp', 'unit'))
- up_master_new: float32 [768, 3072], P('dp', 'unit')
- up_first_new: float32 [768, 3072], P('dp', 'unit')
- up_second_new: float32 [768, 3072], P('dp', 'unit')
- down_master_new: float32 [3072, 768], P('unit', 'dp')
- down_first_new: float32 [3072, 768], P('unit', 'dp')
- down_second_new: float32 [3072, 768], P('unit', 'dp')
- vector_master_new: float32 [13, 768], replicated
- vector_first_new: float32 [13, 768], replicated
- vector_second_new: float32 [13, 768], replicated
Inputs may be any that keep to these rules, and one draw needn't show every extreme that they name: `seg_lengths`: each row holds the lengths of the 3 sequences that fill one pack of 1024 consecutive tokens, in order. `head_mask`: exactly one head is pruned (0), all others are 1.
All inputs are finite; a program needn't handle non-finite values. No bound on the sum of `key_valid` on one device may be relied on, other than what follows from the above.
Results may differ from a plain program's by a relative error of at most 0.017.
Values may be sent and summed in bfloat16 or wider, within the bound.
No kernel may reach another device: no remote copies, remote signals or barrier semaphores. Data moves between devices by JAX's collectives and lax.ppermute only.
A program may use at most 192 MiB of HBM per device.

v0:
```python
from functools import partial

import jax
import jax.numpy as jnp
from jax import lax
from jax.sharding import PartitionSpec as P

SEQ_BLOCK = 1024
STEP = 10


EPS_NORM = 1e-05
BETA_ONE = 0.9
BETA_TWO = 0.999
ADAM_EPS = 1e-08
RATE_MATRIX = 0.1
RATE_VECTOR = 1.0
DECAY_MATRIX = 0.01
CLIP_NORM = 1.0
MASKED = -1000000000.0


def layer_norm(value, gain, shift):
    mean = jnp.mean(value, axis=-1, keepdims=True)
    centred = value - mean
    spread = jnp.mean(centred * centred, axis=-1, keepdims=True)
    return centred * lax.rsqrt(spread + EPS_NORM) * gain + shift


def segment_ids(lengths, count):
    ends = jnp.cumsum(lengths)
    places = jnp.arange(count, dtype=jnp.int32)
    return jnp.sum((places[:, None] >= ends[None, :-1]).astype(jnp.int32), axis=1)


def contract_rows(left, right):
    return lax.dot_general(
        left, right, (((0,), (0,)), ((), ())), preferred_element_type=jnp.float32
    )


def times_transposed(left, right):
    return lax.dot_general(
        left, right, (((1,), (1,)), ((), ())), preferred_element_type=jnp.float32
    )


def gelu_slope(value):
    normal_cdf = 0.5 * (1.0 + lax.erf(value * 0.7071067811865476))
    normal_pdf = jnp.exp(-0.5 * value * value) * 0.3989422804014327
    return normal_cdf + value * normal_pdf


def adamw(master, first, second, grad, rate, decay):
    first_new = BETA_ONE * first + (1.0 - BETA_ONE) * grad
    second_new = BETA_TWO * second + (1.0 - BETA_TWO) * grad * grad
    first_hat = first_new / (1.0 - BETA_ONE**STEP)
    second_hat = second_new / (1.0 - BETA_TWO**STEP)
    master_new = master - rate * (first_hat / (jnp.sqrt(second_hat) + ADAM_EPS) + decay * master)
    return (master_new, first_new, second_new)


def shards(
    layer_input,
    teacher,
    cotangent,
    key_valid,
    seg_lengths,
    head_mask,
    hidden_mask,
    inter_mask,
    proj_master,
    proj_first,
    proj_second,
    up_master,
    up_first,
    up_second,
    down_master,
    down_first,
    down_second,
    vector_master,
    vector_first,
    vector_second,
):
    bf16 = jnp.bfloat16
    f32 = jnp.float32
    rows, width = layer_input.shape
    heads = head_mask.shape[0]
    head_size = width // heads
    scale = head_size ** (-0.5)
    head_gate = head_mask.astype(f32)
    hidden_gate = hidden_mask.astype(f32)
    inter_gate = inter_mask.astype(f32)
    valid = key_valid.astype(f32)
    inner_bias = vector_master[9:].reshape(-1)
    proj_full = lax.all_gather(proj_master.astype(bf16), ("dp", "unit"), axis=0, tiled=True)
    w_query = proj_full[:, : 3 * width]
    w_out = proj_full[:, 3 * width : 4 * width]
    w_dist = proj_full[:, 4 * width :]
    up_local, down_local = (
        lax.all_gather(up_master.astype(bf16), "dp", axis=0, tiled=True),
        lax.all_gather(down_master.astype(bf16), "dp", axis=1, tiled=True),
    )
    ffn_local = up_local.shape[1]
    offset = lax.axis_index("unit") * ffn_local
    up_weight, down_weight = (up_local, down_local)
    unit_bias = lax.dynamic_slice_in_dim(inner_bias, offset, ffn_local, 0)
    unit_gate = lax.dynamic_slice_in_dim(inter_gate, offset, ffn_local, 0)
    bias_qkv = jnp.concatenate(
        [vector_master[0], jnp.zeros_like(vector_master[0]), vector_master[1]]
    )
    qkv = (jnp.dot(layer_input, w_query, preferred_element_type=f32) + bias_qkv).astype(bf16)
    query = qkv[:, :width].reshape(rows, heads, head_size)
    keys = qkv[:, width : 2 * width].reshape(rows, heads, head_size)
    values = qkv[:, 2 * width :].reshape(rows, heads, head_size)
    segments = jax.vmap(partial(segment_ids, count=SEQ_BLOCK))(seg_lengths).reshape(rows)
    block_rows = min(512, SEQ_BLOCK)
    blocks = rows // block_rows

    def block_scores(index):
        start = index * block_rows
        base = start // SEQ_BLOCK * SEQ_BLOCK
        query_block = lax.dynamic_slice_in_dim(query, start, block_rows, 0)
        seg_query = lax.dynamic_slice_in_dim(segments, start, block_rows, 0)
        place_query = start + jnp.arange(block_rows, dtype=jnp.int32)
        place_key = base + jnp.arange(SEQ_BLOCK, dtype=jnp.int32)
        allowed = (seg_query[:, None] == segments[None, :]) & (
            (valid[None, :] > 0.5) | (place_query[:, None] == place_key[None, :])
        )
        scores = jnp.einsum("qhd,khd->hqk", query_block, keys, preferred_element_type=f32) * scale
        scores = jnp.where(allowed[None], scores, MASKED)
        return (scores, query_block, keys, values, start, base)

    def forward_block(index):
        scores, query_block, key_pack, value_pack, start, base = block_scores(index)
        peak = jnp.max(scores, axis=-1, keepdims=True)
        expo = jnp.exp(scores - peak)
        total = jnp.sum(expo, axis=-1, keepdims=True)
        probs = (expo / total).astype(bf16)
        context = jnp.einsum("hqk,khd->qhd", probs, value_pack, preferred_element_type=f32)
        return (context, (peak + jnp.log(total))[..., 0])

    context, log_total = lax.map(forward_block, jnp.arange(blocks))
    context = context.reshape(rows, heads, head_size) * head_gate[None, :, None]
    context_low = context.reshape(rows, width).astype(bf16)
    attn = (
        jnp.dot(context_low, w_out, preferred_element_type=f32) + vector_master[2]
    ) * hidden_gate
    first_sum = layer_input.astype(f32) + attn
    first, first_back = jax.vjp(layer_norm, first_sum, vector_master[3], vector_master[4])
    first_low = first.astype(bf16)
    ffn_input = lax.all_gather(first_low, "unit", axis=0, tiled=True)
    inner = jnp.dot(ffn_input, up_weight, preferred_element_type=f32) + unit_bias
    active = (jax.nn.gelu(inner, approximate=False) * unit_gate).astype(bf16)
    piece = active
    branch_sum = lax.psum_scatter(
        jnp.dot(piece, down_weight, preferred_element_type=f32).astype(jnp.bfloat16),
        "unit",
        scatter_dimension=0,
        tiled=True,
    ).astype(jnp.float32)
    branch = (branch_sum + vector_master[5]) * hidden_gate
    out, out_back = jax.vjp(layer_norm, first + branch, vector_master[6], vector_master[7])
    out_low = out.astype(bf16)
    student = jnp.dot(out_low, w_dist, preferred_element_type=f32) + vector_master[8]
    error = student - teacher.astype(f32)
    half_sq = 0.5 * jnp.sum(valid[:, None] * error * error)
    d_student = (valid[:, None] * error).astype(bf16)
    g_dist = contract_rows(out_low, d_student)
    g_bias_dist = jnp.sum(d_student.astype(f32), axis=0)
    d_out = cotangent.astype(f32) + times_transposed(d_student, w_dist)
    d_second, g_gain_two, g_shift_two = out_back(d_out)
    d_branch = d_second.astype(bf16) * hidden_gate.astype(bf16)
    g_bias_two = jnp.sum(d_branch.astype(f32), axis=0)
    d_rows = lax.all_gather(d_branch, "unit", axis=0, tiled=True)
    d_active = times_transposed(d_rows, down_weight)
    d_inner = (d_active * unit_gate * gelu_slope(inner)).astype(bf16)
    g_down = contract_rows(active, d_rows)
    g_up = contract_rows(ffn_input, d_inner)
    g_inner_bias = jnp.sum(d_inner.astype(f32), axis=0)
    piece = d_inner
    d_first_ffn = lax.psum_scatter(
        times_transposed(piece, up_weight).astype(jnp.bfloat16),
        "unit",
        scatter_dimension=0,
        tiled=True,
    ).astype(jnp.float32)
    bias_full = lax.dynamic_update_slice_in_dim(
        jnp.zeros(inner_bias.shape, f32), g_inner_bias, offset, 0
    )
    g_up, g_down = (
        lax.psum_scatter(g_up.astype(jnp.bfloat16), "dp", scatter_dimension=0, tiled=True).astype(
            jnp.float32
        ),
        lax.psum_scatter(g_down.astype(jnp.bfloat16), "dp", scatter_dimension=1, tiled=True).astype(
            jnp.float32
        ),
    )
    d_first_sum, g_gain_one, g_shift_one = first_back(d_second + d_first_ffn)
    d_attn = d_first_sum.astype(bf16) * hidden_gate.astype(bf16)
    g_bias_out = jnp.sum(d_attn.astype(f32), axis=0)
    g_out = contract_rows(context_low, d_attn)
    d_context = times_transposed(d_attn, w_out).astype(bf16).reshape(rows, heads, head_size)
    d_context = d_context * head_gate.astype(bf16)[None, :, None]

    def backward_block(carry, index):
        d_keys, d_values = carry
        scores, query_block, key_pack, value_pack, start, base = block_scores(index)
        lse = lax.dynamic_index_in_dim(log_total, index, 0, keepdims=False)
        probs = jnp.exp(scores - lse[..., None])
        d_ctx_block = lax.dynamic_slice_in_dim(d_context, start, block_rows, 0)
        d_probs = jnp.einsum("qhd,khd->hqk", d_ctx_block, value_pack, preferred_element_type=f32)
        row_sum = jnp.sum(probs * d_probs, axis=-1, keepdims=True)
        d_scores = (probs * (d_probs - row_sum)).astype(bf16)
        d_query = jnp.einsum("hqk,khd->qhd", d_scores, key_pack, preferred_element_type=f32) * scale
        d_key = (
            jnp.einsum("hqk,qhd->khd", d_scores, query_block, preferred_element_type=f32) * scale
        )
        d_value = jnp.einsum(
            "hqk,qhd->khd", probs.astype(bf16), d_ctx_block, preferred_element_type=f32
        )
        d_keys = d_keys + d_key
        d_values = d_values + d_value
        return ((d_keys, d_values), d_query)

    empty = jnp.zeros((rows, heads, head_size), f32)
    (d_keys, d_values), d_queries = lax.scan(backward_block, (empty, empty), jnp.arange(blocks))
    d_qkv = jnp.concatenate(
        [
            d_queries.reshape(rows, width),
            d_keys.reshape(rows, width),
            d_values.reshape(rows, width),
        ],
        axis=1,
    ).astype(bf16)
    g_bias_query = jnp.sum(d_qkv[:, :width].astype(f32), axis=0)
    g_bias_value = jnp.sum(d_qkv[:, 2 * width :].astype(f32), axis=0)
    g_query = contract_rows(layer_input, d_qkv)
    input_grad = d_first_sum + times_transposed(d_qkv, w_query)
    g_proj = lax.psum_scatter(
        jnp.concatenate([g_query, g_out, g_dist], axis=1),
        ("dp", "unit"),
        scatter_dimension=0,
        tiled=True,
    )
    vector_grad = jnp.concatenate(
        [
            jnp.stack(
                [
                    g_bias_query,
                    g_bias_value,
                    g_bias_out,
                    g_gain_one,
                    g_shift_one,
                    g_bias_two,
                    g_gain_two,
                    g_shift_two,
                    g_bias_dist,
                ]
            ),
            bias_full.reshape(-1, width),
        ],
        axis=0,
    )
    shard_sq = jnp.sum(g_proj * g_proj) + jnp.sum(g_up * g_up) + jnp.sum(g_down * g_down)
    vector_grad, half_total, shard_total = lax.psum(
        (vector_grad, half_sq, shard_sq), ("dp", "unit")
    )
    grad_norm = jnp.sqrt(shard_total + jnp.sum(vector_grad * vector_grad))
    clip = jnp.minimum(1.0, CLIP_NORM / (grad_norm + 1e-06))
    all_tokens = rows * lax.axis_size("dp") * lax.axis_size("unit")
    distill_loss = 2.0 * half_total / (all_tokens * width)
    proj_new = adamw(proj_master, proj_first, proj_second, clip * g_proj, RATE_MATRIX, DECAY_MATRIX)
    up_new = adamw(up_master, up_first, up_second, clip * g_up, RATE_MATRIX, DECAY_MATRIX)
    down_new = adamw(down_master, down_first, down_second, clip * g_down, RATE_MATRIX, DECAY_MATRIX)
    vector_new = adamw(
        vector_master, vector_first, vector_second, clip * vector_grad, RATE_VECTOR, 0.0
    )
    return (
        out_low,
        input_grad,
        grad_norm,
        distill_loss,
        proj_new[0],
        proj_new[1],
        proj_new[2],
        up_new[0],
        up_new[1],
        up_new[2],
        down_new[0],
        down_new[1],
        down_new[2],
        vector_new[0],
        vector_new[1],
        vector_new[2],
    )


def solution(mesh):
    in_specs = (
        P(("dp", "unit"), None),
        P(("dp", "unit"), None),
        P(("dp", "unit"), None),
        P(("dp", "unit")),
        P(("dp", "unit"), None),
        P(),
        P(),
        P(),
        P(("dp", "unit"), None),
        P(("dp", "unit"), None),
        P(("dp", "unit"), None),
        P("dp", "unit"),
        P("dp", "unit"),
        P("dp", "unit"),
        P("unit", "dp"),
        P("unit", "dp"),
        P("unit", "dp"),
        P(),
        P(),
        P(),
    )
    out_specs = (
        P(("dp", "unit"), None),
        P(("dp", "unit"), None),
        P(),
        P(),
        P(("dp", "unit"), None),
        P(("dp", "unit"), None),
        P(("dp", "unit"), None),
        P("dp", "unit"),
        P("dp", "unit"),
        P("dp", "unit"),
        P("unit", "dp"),
        P("unit", "dp"),
        P("unit", "dp"),
        P(),
        P(),
        P(),
    )
    return jax.shard_map(shards, mesh=mesh, in_specs=in_specs, out_specs=out_specs, check_vma=False)
```

profile of v0, /device:TPU:0, one launch (start us, length us, event | category | flops | bytes accessed | tf_op | source)
XLA Modules:
  0.0 979.2 jit_solution(8347069284150351771)
XLA Ops:
  20.0 61.9 %all-gather.6.cloned.1.call-done = bf16[768,3840]{1,0:T(8,128)(2,1)} async-done(((bf16[24,3840]{1,0:T(8,128)(2,1)}), bf16[768,3840]{1,0:T(8,128)(2,1)}) %all-gather.6.cloned.1.call-update) | async-done | bytes 5898256 | tf_op jit(solution)/shard_map/all_gather | solution.py:96
  94.4 138.7 %while.31 = (s32[]{:T(128)}, f32[2,512,12,64]{1,0,3,2:T(2,128)}, f32[2,12,512]{2,1,0:T(8,128)S(1)}, s32[2]{0:T(128)S(1)}, s32[1024]{0:T(1024)S(1)}, /*index=5*/s...) while((s32[]{:T(128)}, f32[2,512,12,64]{1,0,3,2:T(2,128)}, ...), condition=%wide.region_5.6_spmd, body=%wide.region_2.5_spmd.sunk | while | flops 1688203776 | bytes 190304688 | solution.py:143
  96.6 12.1 %fusion.133 = (f32[12,512]{1,0:T(8,128)S(1)}, f32[12,512,1024]{2,1,0:T(8,128)}) fusion(pred[512,1024]{1,0:T(8,128)(4,1)S(1)} %or_and_fusion.4, bf16[1024,12,64]{0,2,1:T(8,128)(2,1)S(1)} %get-tuple-element.756, bf16[1024,12,64]{0,2,1:T(8,128)(2,1)} %get-tuple-element.755, s32[]{:T(128)S(6)} %select_n.96), kind=kOutput, calls=%fused_computation.3.clone.1 | convolution fusion | flops 824174592 | bytes 28073988 | tf_op jit(solution)/shard_map/while/body/eval_jaxpr/qhd,khd->hqk/dot_general | solution.py:130
  108.7 12.4 %fusion.134 = f32[12,512]{1,0:T(8,128)S(1)} fusion(f32[12,512,1024]{2,1,0:T(8,128)} %get-tuple-element.697, f32[12,512]{1,0:T(8,128)S(1)} %get-tuple-element.698, pred[512,1024]{1,0:T(8,128)(4,1)S(1)} %or_and_fusion.4), kind=kLoop, calls=%fused_computation.4.clone.1 | loop fusion | flops 25159680 | bytes 25739264 | tf_op jit(solution)/shard_map/while/body/eval_jaxpr/reduce_sum | solution.py:138
  134.8 28.8 %dynamic_update_slice.31 = f32[2,512,12,64]{1,0,3,2:T(2,128)} dynamic-update-slice(f32[2,512,12,64]{1,0,3,2:T(2,128)} %get-tuple-element.732, f32[1,512,12,64]{1,0,3,2:T(1,128)S(1)} %copy.165, s32[]{:T(128)S(6)} %copy.172, s32[]{:T(128)} %constant.260.clone.1..sunk, s32[]{:T(128)} %constant.260.clone.1..sunk, s32[]{:T(128)} %constant.260.clone.1..sunk) | dynamic-update-slice | bytes 3145732 | tf_op jit(solution)/shard_map/while/body/jit(dynamic_update_index_in_dim)/dynamic_update_slice | solution.py:143
  165.7 12.0 %fusion.133 = (f32[12,512]{1,0:T(8,128)S(1)}, f32[12,512,1024]{2,1,0:T(8,128)}) fusion(pred[512,1024]{1,0:T(8,128)(4,1)S(1)} %or_and_fusion.4, bf16[1024,12,64]{0,2,1:T(8,128)(2,1)S(1)} %get-tuple-element.756, bf16[1024,12,64]{0,2,1:T(8,128)(2,1)} %get-tuple-element.755, s32[]{:T(128)S(6)} %select_n.96), kind=kOutput, calls=%fused_computation.3.clone.1 | convolution fusion | flops 824174592 | bytes 28073988 | tf_op jit(solution)/shard_map/while/body/eval_jaxpr/qhd,khd->hqk/dot_general | solution.py:130
  177.6 12.3 %fusion.134 = f32[12,512]{1,0:T(8,128)S(1)} fusion(f32[12,512,1024]{2,1,0:T(8,128)} %get-tuple-element.697, f32[12,512]{1,0:T(8,128)S(1)} %get-tuple-element.698, pred[512,1024]{1,0:T(8,128)(4,1)S(1)} %or_and_fusion.4), kind=kLoop, calls=%fused_computation.4.clone.1 | loop fusion | flops 25159680 | bytes 25739264 | tf_op jit(solution)/shard_map/while/body/eval_jaxpr/reduce_sum | solution.py:138
  203.7 28.8 %dynamic_update_slice.31 = f32[2,512,12,64]{1,0,3,2:T(2,128)} dynamic-update-slice(f32[2,512,12,64]{1,0,3,2:T(2,128)} %get-tuple-element.732, f32[1,512,12,64]{1,0,3,2:T(1,128)S(1)} %copy.165, s32[]{:T(128)S(6)} %copy.172, s32[]{:T(128)} %constant.260.clone.1..sunk, s32[]{:T(128)} %constant.260.clone.1..sunk, s32[]{:T(128)} %constant.260.clone.1..sunk) | dynamic-update-slice | bytes 3145732 | tf_op jit(solution)/shard_map/while/body/jit(dynamic_update_index_in_dim)/dynamic_update_slice | solution.py:143
  245.5 43.1 %all-gather.8.cloned.1.call-done = bf16[4096,768]{0,1:T(8,128)(2,1)} async-done(((bf16[1024,768]{0,1:T(8,128)(2,1)}), bf16[4096,768]{0,1:T(8,128)(2,1)}) %all-gather.8.cloned.1.call-update) | async-done | bytes 6291472 | tf_op jit(solution)/shard_map/all_gather | solution.py:152
  288.7 35.4 %fusion.30 = (bf16[4096,768]{1,0:T(8,128)(2,1)}, f32[4096,768]{1,0:T(8,128)}) fusion(f32[768]{0:T(1024)S(1)} %dynamic-slice_convert_fusion, f32[768]{0:T(1024)S(1)} %dynamic_slice.56, bf16[4096,768]{0,1:T(8,128)(2,1)} %all-gather.8.cloned.1.call-done, bf16[768,768]{1,0:T(8,128)(2,1)} %all-gather.10.cloned.1.call-done), kind=kOutput, calls=%fused_computation.48 | convolution fusion | flops 5042601984 | bytes 26351616 | tf_op jit(solution)/shard_map/dot_general | solution.py:153
  344.4 54.5 %reduce-scatter.8.cloned.1.call-done = bf16[1024,768]{0,1:T(8,128)(2,1)} async-done(((bf16[4096,768]{0,1:T(8,128)(2,1)}), bf16[1024,768]{0,1:T(8,128)(2,1)}) %reduce-scatter.8.cloned.1.call-update) | async-done | bytes 1572880 | tf_op jit(solution)/shard_map/reduce_scatter | solution.py:156
  416.5 46.5 %all-gather.14.cloned.1.call-done = bf16[4096,768]{0,1:T(8,128)(2,1)} async-done(((bf16[1024,768]{0,1:T(8,128)(2,1)}), bf16[4096,768]{0,1:T(8,128)(2,1)}) %all-gather.14.cloned.1.call-update) | async-done | bytes 6291472 | tf_op jit(solution)/shard_map/all_gather | solution.py:175
  463.0 13.7 %convert_reduce_fusion = (f32[768]{0:T(1024)}, bf16[4096,768]{1,0:T(8,128)(2,1)S(1)}) fusion(f32[4096,768]{1,0:T(8,128)} %get-tuple-element.562, f32[768]{0:T(1024)S(1)} %dynamic_slice.56, f32[768]{0:T(1024)S(1)} %dynamic-slice_convert_fusion, bf16[4096,768]{0,1:T(8,128)(2,1)} %all-gather.14.cloned.1.call-done, ...), kind=kOutput, calls=%fused_computation.55 | convolution fusion | flops 4875877376 | bytes 26354688 | tf_op jit(solution)/shard_map/dot_general | solution.py:43
  511.7 33.1 %reduce-scatter.10.cloned.1.call-done = bf16[1024,768]{0,1:T(8,128)(2,1)} async-done(((bf16[4096,768]{0,1:T(8,128)(2,1)}), bf16[1024,768]{0,1:T(8,128)(2,1)}) %reduce-scatter.10.cloned.1.call-update) | async-done | bytes 1572880 | tf_op jit(solution)/shard_map/reduce_scatter | solution.py:182
  557.3 175.8 %while.32 = (s32[]{:T(128)}, f32[1024,12,64]{0,2,1:T(8,128)}, f32[1024,12,64]{0,2,1:T(8,128)}, bf16[2,512,12,64]{1,3,2,0:T(8,128)(2,1)}, s32[2]{0:T(128)S(1)}, /...) while((s32[]{:T(128)}, f32[1024,12,64]{0,2,1:T(8,128)}, ...), condition=%wide.region_18.19_spmd.clone, body=%wide.region_16.18_spmd.clone.sunk | while | flops 4127322624 | bytes 219361776 | solution.py:227
  573.0 13.5 %bitcast_add_fusion.5 = f32[1024,12,64]{0,2,1:T(8,128)} fusion(f32[1024,12,64]{0,2,1:T(8,128)} %get-tuple-element.788, f32[12,512,1024]{2,1,0:T(8,128)} %fusion.145, f32[12,512]{1,0:T(8,128)S(1)} %dynamic-slice_bitcast_fusion.2, pred[512,1024]{1,0:T(8,128)(4,1)S(1)} %or_and_fusion.5, pred[]{:T(512)S(6)} %compare.11, ...), kind=kOutput, calls=%fused_computation.23.clone.1 | convolution fusion | flops 832045056 | bytes 32800772 | tf_op jit(solution)/shard_map/while/body/eval_jaxpr/hqk,qhd->khd/dot_general | solution.py:219
  586.5 18.1 %multiply_reduce_fusion.10 = (f32[12,512]{1,0:T(8,128)S(1)}, f32[12,512,1024]{2,1,0:T(8,128)}) fusion(f32[12,512,1024]{2,1,0:T(8,128)} %fusion.145, f32[12,512]{1,0:T(8,128)S(1)} %dynamic-slice_bitcast_fusion.2, pred[512,1024]{1,0:T(8,128)(4,1)S(1)} %or_and_fusion.5, bf16[1024,12,64]{0,2,1:T(8,128)(2,1)} %get-tuple-element.819, ...), kind=kOutput, calls=%fused_computation.18.clone.1 | convolution fusion | flops 836757504 | bytes 53264388 | tf_op jit(solution)/shard_map/while/body/eval_jaxpr/qhd,khd->hqk/dot_general | solution.py:212
  604.6 21.8 %multiply_convert_fusion.7 = bf16[12,512,1024]{2,1,0:T(8,128)(2,1)} fusion(f32[12,512,1024]{2,1,0:T(8,128)} %get-tuple-element.712, f32[12,512,1024]{2,1,0:T(8,128)} %fusion.145, f32[12,512]{1,0:T(8,128)S(1)} %get-tuple-element.713, f32[12,512]{1,0:T(8,128)S(1)} %dynamic-slice_bitcast_fusion.2, pred[512,1024]{1,0:T(8,128)(4,1)S(1)} %or_and_fusion.5), kind=kLoop, calls=%fused_computation.17.clone.1 | loop fusion | flops 37748736 | bytes 63488000 | tf_op jit(solution)/shard_map/while/body/eval_jaxpr/convert_element_type | solution.py:214
  660.1 14.4 %bitcast_add_fusion.5 = f32[1024,12,64]{0,2,1:T(8,128)} fusion(f32[1024,12,64]{0,2,1:T(8,128)} %get-tuple-element.788, f32[12,512,1024]{2,1,0:T(8,128)} %fusion.145, f32[12,512]{1,0:T(8,128)S(1)} %dynamic-slice_bitcast_fusion.2, pred[512,1024]{1,0:T(8,128)(4,1)S(1)} %or_and_fusion.5, pred[]{:T(512)S(6)} %compare.11, ...), kind=kOutput, calls=%fused_computation.23.clone.1 | convolution fusion | flops 832045056 | bytes 32800772 | tf_op jit(solution)/shard_map/while/body/eval_jaxpr/hqk,qhd->khd/dot_general | solution.py:219
  674.5 18.1 %multiply_reduce_fusion.10 = (f32[12,512]{1,0:T(8,128)S(1)}, f32[12,512,1024]{2,1,0:T(8,128)}) fusion(f32[12,512,1024]{2,1,0:T(8,128)} %fusion.145, f32[12,512]{1,0:T(8,128)S(1)} %dynamic-slice_bitcast_fusion.2, pred[512,1024]{1,0:T(8,128)(4,1)S(1)} %or_and_fusion.5, bf16[1024,12,64]{0,2,1:T(8,128)(2,1)} %get-tuple-element.819, ...), kind=kOutput, calls=%fused_computation.18.clone.1 | convolution fusion | flops 836757504 | bytes 53264388 | tf_op jit(solution)/shard_map/while/body/eval_jaxpr/qhd,khd->hqk/dot_general | solution.py:212
  692.6 21.2 %multiply_convert_fusion.7 = bf16[12,512,1024]{2,1,0:T(8,128)(2,1)} fusion(f32[12,512,1024]{2,1,0:T(8,128)} %get-tuple-element.712, f32[12,512,1024]{2,1,0:T(8,128)} %fusion.145, f32[12,512]{1,0:T(8,128)S(1)} %get-tuple-element.713, f32[12,512]{1,0:T(8,128)S(1)} %dynamic-slice_bitcast_fusion.2, pred[512,1024]{1,0:T(8,128)(4,1)S(1)} %or_and_fusion.5), kind=kLoop, calls=%fused_computation.17.clone.1 | loop fusion | flops 37748736 | bytes 63488000 | tf_op jit(solution)/shard_map/while/body/eval_jaxpr/convert_element_type | solution.py:214
  751.7 12.4 %copy.135 = f32[768,3840]{1,0:T(8,128)} copy(f32[768,3840]{0,1:T(8,128)} %pad_maximum_fusion) | data formatting | bytes 23592960
  784.0 128.4 %reduce-scatter.16.cloned.1.call-done = f32[24,3840]{1,0:T(8,128)} async-done(((f32[768,3840]{1,0:T(8,128)}), f32[24,3840]{1,0:T(8,128)}) %reduce-scatter.16.cloned.1.call-update) | async-done | bytes 368656 | tf_op jit(solution)/shard_map/reduce_scatter | solution.py:240
  920.8 40.7 %all-reduce = (f32[]{:T(128)}, f32[13,768]{1,0:T(8,128)}, f32[]{:T(128)}) all-reduce(f32[]{:T(128)S(6)} %add.354, f32[13,768]{1,0:T(8,128)} %concatenate.16, f32[]{:T(128)S(6)} %mul.528), channel_id=1, replica_groups=mesh['dp'=8,'unit'=4] {'dp','unit'}, use_global_device_ids=true, to_apply=%region_25.26 | all-reduce | flops 9986 | bytes 79888 | tf_op jit(solution)/shard_map/psum | solution.py:266
  (296 shorter events, 265.8 us)
Async XLA Ops:
  7.2 74.7 %copy-start.15 = (bf16[1024,768]{1,0:T(8,128)(2,1)S(1)}, bf16[1024,768]{1,0:T(8,128)(2,1)}, u32[]{:S(2)}) copy-start(bf16[1024,768]{1,0:T(8,128)(2,1)} %param.24) | copy-start | bytes 4718596
  7.2 74.7 %all-gather.6.cloned.1.call-start = ((), (), s32[]{:S(2)}) async-start(), calls=%async_computation.5 | async-start | bytes 6082560 | tf_op jit(solution)/shard_map/all_gather | solution.py:96
  9.1 236.5 %all-gather.10.cloned.1.call-start = ((), (), s32[]{:S(2)}) async-start(), calls=%async_computation.7 | async-start | bytes 1327104 | tf_op jit(solution)/shard_map/all_gather | solution.py:101
  10.8 277.9 %all-gather.8.cloned.1.call-start = ((), (), s32[]{:S(2)}) async-start(), calls=%async_computation.6 | async-start | bytes 7864320 | tf_op jit(solution)/shard_map/all_gather | solution.py:152
  243.1 89.3 %all-gather.12.cloned.1.call-start = ((), (), s32[]{:S(2)}) async-start(), calls=%async_computation.8 | async-start | bytes 1327104 | tf_op jit(solution)/shard_map/all_gather | solution.py:102
  243.9 155.0 %reduce-scatter.8.cloned.1.call-start = ((), (), s32[]{:S(2)}) async-start(), calls=%async_computation.9 | async-start | bytes 7864320 | tf_op jit(solution)/shard_map/reduce_scatter | solution.py:156
  341.6 57.3 %copy-start.47 = (f32[768]{0:T(1024)S(1)}, f32[768]{0:T(1024)}, u32[]{:S(2)}) copy-start(f32[768]{0:T(1024)} %get-tuple-element.466) | copy-start | bytes 9220
  341.6 121.4 %all-gather.14.cloned.1.call-start = ((), (), s32[]{:S(2)}) async-start(), calls=%async_computation.10 | async-start | bytes 7864320 | tf_op jit(solution)/shard_map/all_gather | solution.py:175
  416.5 128.4 %reduce-scatter.10.cloned.1.call-start = ((), (), s32[]{:S(2)}) async-start(), calls=%async_computation.11 | async-start | bytes 7864320 | tf_op jit(solution)/shard_map/reduce_scatter | solution.py:182
  486.4 281.9 %reduce-scatter.12.cloned.1.call-start = ((), (), s32[]{:S(2)}) async-start(), calls=%async_computation.12 | async-start | bytes 1327104 | tf_op jit(solution)/shard_map/reduce_scatter | solution.py:192
  496.6 273.2 %reduce-scatter.14.cloned.1.call-start = ((), (), s32[]{:S(2)}) async-start(), calls=%async_computation.13 | async-start | bytes 1327104 | tf_op jit(solution)/shard_map/reduce_scatter | solution.py:195
  511.7 400.7 %reduce-scatter.16.cloned.1.call-start = ((), (), s32[]{:S(2)}) async-start(), calls=%async_computation.14 | async-start | bytes 12165120 | tf_op jit(solution)/shard_map/reduce_scatter | solution.py:240
  917.0 49.4 %copy-start.26 = (f32[768,96]{0,1:T(8,128)S(1)}, f32[768,96]{0,1:T(8,128)}, u32[]{:S(2)}) copy-start(f32[768,96]{0,1:T(8,128)} %param.38) | copy-start | bytes 884740
  917.0 49.4 %copy-start.31 = (bf16[768,96]{0,1:T(8,128)(2,1)S(1)}, bf16[768,96]{0,1:T(8,128)(2,1)}, u32[]{:S(2)}) copy-start(bf16[768,96]{0,1:T(8,128)(2,1)} %reduce-scatter.14.cloned.1.call-done) | copy-start | bytes 442372
  917.1 49.4 %copy-start.36 = (f32[768,96]{0,1:T(8,128)S(1)}, f32[768,96]{0,1:T(8,128)}, u32[]{:S(2)}) copy-start(f32[768,96]{0,1:T(8,128)} %param.39) | copy-start | bytes 884740
  917.1 49.4 %copy-start.37 = (f32[768,96]{0,1:T(8,128)S(1)}, f32[768,96]{0,1:T(8,128)}, u32[]{:S(2)}) copy-start(f32[768,96]{0,1:T(8,128)} %param.40) | copy-start | bytes 884740
  917.1 50.5 %copy-start.27 = (f32[96,768]{1,0:T(8,128)S(1)}, f32[96,768]{1,0:T(8,128)}, u32[]{:S(2)}) copy-start(f32[96,768]{1,0:T(8,128)} %param.35) | copy-start | bytes 884740
  917.1 50.5 %copy-start.30 = (bf16[96,768]{1,0:T(8,128)(2,1)S(1)}, bf16[96,768]{1,0:T(8,128)(2,1)}, u32[]{:S(2)}) copy-start(bf16[96,768]{1,0:T(8,128)(2,1)} %reduce-scatter.12.cloned.1.call-done) | copy-start | bytes 442372
  917.1 50.4 %copy-start.38 = (f32[96,768]{1,0:T(8,128)S(1)}, f32[96,768]{1,0:T(8,128)}, u32[]{:S(2)}) copy-start(f32[96,768]{1,0:T(8,128)} %param.36) | copy-start | bytes 884740
  917.1 50.4 %copy-start.39 = (f32[96,768]{1,0:T(8,128)S(1)}, f32[96,768]{1,0:T(8,128)}, u32[]{:S(2)}) copy-start(f32[96,768]{1,0:T(8,128)} %param.37) | copy-start | bytes 884740
  920.8 47.8 %copy-start.23 = (f32[24,3840]{1,0:T(8,128)S(1)}, f32[24,3840]{1,0:T(8,128)}, u32[]{:S(2)}) copy-start(f32[24,3840]{1,0:T(8,128)} %reduce-scatter.16.cloned.1.call-done) | copy-start | bytes 1105924
  920.8 47.8 %copy-start.24 = (f32[24,3840]{1,0:T(8,128)S(1)}, f32[24,3840]{1,0:T(8,128)}, u32[]{:S(2)}) copy-start(f32[24,3840]{1,0:T(8,128)} %param.32) | copy-start | bytes 1105924
  920.8 47.8 %copy-start.34 = (f32[24,3840]{1,0:T(8,128)S(1)}, f32[24,3840]{1,0:T(8,128)}, u32[]{:S(2)}) copy-start(f32[24,3840]{1,0:T(8,128)} %param.33) | copy-start | bytes 1105924
  920.8 47.8 %copy-start.35 = (f32[24,3840]{1,0:T(8,128)S(1)}, f32[24,3840]{1,0:T(8,128)}, u32[]{:S(2)}) copy-start(f32[24,3840]{1,0:T(8,128)} %param.34) | copy-start | bytes 1105924
  (56 other events, 287.0 us)
Sparse Core Ops, SparseCore 0:
  11.5 70.3 all-gather.5
  84.6 40.0 all-gather.9
  243.2 45.3 all-gather.7
  291.3 41.0 all-gather.11
  341.7 57.1 reduce-scatter.7
  416.6 46.3 all-gather.13
  486.5 58.3 reduce-scatter.9
  548.3 63.9 reduce-scatter.11
  615.7 62.9 reduce-scatter.13
  764.3 148.0 reduce-scatter.15
where the time goes:
time: 988 us; the launch traced here: 979 us
  waiting for transfers between devices  376 us (38%)
  matrix products  294 us (30%)
  local copies, waits for them, and re-layouts  122 us (12%)
  other arithmetic  116 us (12%)
  blocking collectives  40.7 us (4%)
  between operations  22.3 us (2%)
    reduce_scatter x1, waiting for transfers between devices, shards(): lax.psum_scatter(jnp.concatenate([g_query, g_out, g_dist], axis=1), ('dp'...  128 us
    all_gather x1, waiting for transfers between devices, shards(): lax.all_gather(proj_master.astype(bf16), ('dp', 'unit'), axis=0, tiled=True)  61.9 us
    dynamic_update_slice x4, local copies, waits for them, and re-layouts, shards(): context, log_total = lax.map(forward_block, jnp.arange(blocks))  60.9 us
    reduce_scatter x1, waiting for transfers between devices, shards(): lax.psum_scatter(jnp.dot(piece, down_weight, preferred_element_type=f32)....  54.5 us
    dot_general x4, matrix products, block_scores(): jnp.einsum('qhd,khd->hqk', query_block, keys, preferred_element_type=f32)  47.1 us
    all_gather x1, waiting for transfers between devices, shards(): d_rows = lax.all_gather(d_branch, 'unit', axis=0, tiled=True)  46.5 us
    all_gather x1, waiting for transfers between devices, shards(): ffn_input = lax.all_gather(first_low, 'unit', axis=0, tiled=True)  43.1 us
    convert_element_type x2, other arithmetic, backward_block(): d_scores = (probs * (d_probs - row_sum)).astype(bf16)  43 us
  transfers between devices with their start and end apart: 10, of which 7 were waited for; matrix products, arithmetic and copies ran while one was open for 47% of the time, Pallas kernels for 0%

commit v1 on v0

v1 whole, which is shorter than its diff:
```python
import jax
import jax.numpy as jnp
from jax import lax
from jax.experimental import pallas as pl
from jax.experimental.pallas import tpu as pltpu
from jax.sharding import PartitionSpec as P

STEP = 10
EPS_NORM = 1e-05
BETA_ONE = 0.9
BETA_TWO = 0.999
ADAM_EPS = 1e-08
RATE_MATRIX = 0.1
RATE_VECTOR = 1.0
DECAY_MATRIX = 0.01
CLIP_NORM = 1.0
HEAD = 64
LANES = 128
QUERY_ROWS = 256
MASKED = -1e30
AXES = ("dp", "unit")
f32 = jnp.float32
bf16 = jnp.bfloat16


def dot(left, right):
    return jnp.dot(left, right, preferred_element_type=f32)


def dot_rows(left, right):
    return lax.dot_general(left, right, (((0,), (0,)), ((), ())), preferred_element_type=f32)


def dot_cols(left, right):
    return lax.dot_general(left, right, (((1,), (1,)), ((), ())), preferred_element_type=f32)


def build_bias(bias_ref, valid_ref, end_one, end_two):
    count = bias_ref.shape[0]
    for start in range(0, count, QUERY_ROWS):
        key = lax.broadcasted_iota(jnp.int32, (count, QUERY_ROWS), 0)
        query = lax.broadcasted_iota(jnp.int32, (count, QUERY_ROWS), 1) + start
        seg_key = (key >= end_one).astype(jnp.int32) + (key >= end_two).astype(jnp.int32)
        seg_query = (query >= end_one).astype(jnp.int32) + (query >= end_two).astype(jnp.int32)
        allowed = (seg_key == seg_query) & ((valid_ref[...] > 0) | (key == query))
        bias_ref[:, start : start + QUERY_ROWS] = jnp.where(allowed, 0.0, MASKED)


def over_window(first_row, end_one, end_two, count, body):
    low = jnp.where(first_row < end_one, 0, jnp.where(first_row < end_two, end_one, end_two))
    last_row = first_row + QUERY_ROWS - 1
    high = jnp.where(last_row < end_one, end_one, jnp.where(last_row < end_two, end_two, count))
    low = (low // 16) * 16
    done = jnp.bool_(False)
    for width in [w for w in (272, 528, 784) if w < count] + [count]:
        start = jnp.minimum(low, count - width)
        fits = (high - start) <= width
        run = fits & jnp.logical_not(done)

        @pl.when(run)
        def _(width=width, start=start):
            body(width, pl.multiple_of(start, 16))

        done = done | fits


def pair_position(heads_ref):
    step = pl.program_id(0)
    head = heads_ref[step]
    fresh = (step == 0) | (heads_ref[jnp.maximum(step - 1, 0)] // 2 != head // 2)
    lane = lax.broadcasted_iota(jnp.int32, (1, LANES), 1)
    return fresh, (lane // HEAD) == (head % 2)


def forward_kernel(
    heads_ref, ends_ref, q_ref, k_ref, v_ref, valid_ref, ctx_ref, lse_ref, bias_ref, qm_ref
):
    count = q_ref.shape[0]
    end_one, end_two = ends_ref[0], ends_ref[1]
    fresh, keep = pair_position(heads_ref)

    @pl.when(pl.program_id(0) == 0)
    def _():
        build_bias(bias_ref, valid_ref, end_one, end_two)

    @pl.when(fresh)
    def _():
        ctx_ref[...] = jnp.zeros_like(ctx_ref)

    qm_ref[...] = jnp.where(keep, q_ref[...] * bf16(HEAD**-0.5), bf16(0))

    def step(index, carry):
        first_row = pl.multiple_of(index * QUERY_ROWS, QUERY_ROWS)
        queries = pl.ds(first_row, QUERY_ROWS)

        def body(width, start):
            window = pl.ds(start, width)
            scores = dot_cols(k_ref[window, :], qm_ref[queries, :]) + bias_ref[window, queries]
            peak = jnp.max(scores, axis=0, keepdims=True)
            expo = jnp.exp(scores - peak)
            total = jnp.sum(expo, axis=0, keepdims=True)
            out = (dot_rows(v_ref[window, :], expo.astype(bf16)) * (1.0 / total)).T
            ctx_ref[queries, :] = jnp.where(keep, out.astype(bf16), ctx_ref[queries, :])
            lse_ref[0, :, queries] = peak + jnp.log(total)

        over_window(first_row, end_one, end_two, count, body)
        return carry

    lax.fori_loop(0, count // QUERY_ROWS, step, 0)


def pair_block(count, offset):
    return pl.BlockSpec((count, LANES), lambda i, heads, ends: (0, heads[i] // 2 + offset))


def attention_forward(qkv, valid_column, ends, heads, all_heads):
    count, width = qkv.shape[0], qkv.shape[1] // 3
    active, pairs = heads.shape[0], width // LANES
    return pl.pallas_call(
        forward_kernel,
        grid_spec=pltpu.PrefetchScalarGridSpec(
            num_scalar_prefetch=2,
            grid=(active,),
            in_specs=[
                pair_block(count, 0),
                pair_block(count, pairs),
                pair_block(count, 2 * pairs),
                pl.BlockSpec((count, 1), lambda i, heads, ends: (0, 0)),
            ],
            out_specs=[
                pair_block(count, 0),
                pl.BlockSpec((1, 1, count), lambda i, heads, ends: (heads[i], 0, 0)),
            ],
            scratch_shapes=[pltpu.VMEM((count, count), f32), pltpu.VMEM((count, LANES), bf16)],
        ),
        out_shape=[
            jax.ShapeDtypeStruct((count, width), bf16),
            jax.ShapeDtypeStruct((all_heads, 1, count), f32),
        ],
        compiler_params=pltpu.CompilerParams(vmem_limit_bytes=40 * 2**20),
        cost_estimate=pl.CostEstimate(
            flops=30 * count * count * HEAD * active,
            bytes_accessed=8 * count * width,
            transcendentals=count * count * active,
        ),
        name="attention_forward",
    )(heads, ends, qkv, qkv, qkv, valid_column)


def backward_kernel(
    heads_ref, ends_ref, q_ref, k_ref, v_ref, do_ref, ctx_ref, lse_ref, valid_ref,
    dq_ref, dk_ref, dv_ref, sums_ref,
    bias_ref, qm_ref, dom_ref, dk_total, dv_total, delta_ref,
):
    count = q_ref.shape[0]
    end_one, end_two = ends_ref[0], ends_ref[1]
    fresh, keep = pair_position(heads_ref)

    @pl.when(pl.program_id(0) == 0)
    def _():
        build_bias(bias_ref, valid_ref, end_one, end_two)

    @pl.when(fresh)
    def _():
        dq_ref[...] = jnp.zeros_like(dq_ref)
        dk_total[...] = jnp.zeros_like(dk_total)
        dv_total[...] = jnp.zeros_like(dv_total)

    qm_ref[...] = jnp.where(keep, q_ref[...] * bf16(HEAD**-0.5), bf16(0))
    dom_ref[...] = jnp.where(keep, do_ref[...], bf16(0))
    product = dom_ref[...].astype(f32) * ctx_ref[...].astype(f32)
    delta_ref[...] = jnp.sum(product.T, axis=0, keepdims=True)

    def step(index, carry):
        first_row = pl.multiple_of(index * QUERY_ROWS, QUERY_ROWS)
        queries = pl.ds(first_row, QUERY_ROWS)

        def body(width, start):
            window = pl.ds(start, width)
            keys, query, grad = k_ref[window, :], qm_ref[queries, :], dom_ref[queries, :]
            scores = dot_cols(keys, query) + bias_ref[window, queries]
            probs = jnp.exp(scores - lse_ref[0, :, queries])
            d_probs = dot_cols(v_ref[window, :], grad)
            d_scores = (probs * (d_probs - delta_ref[:, queries])).astype(bf16)
            dv_total[window, :] += dot(probs.astype(bf16), grad)
            dk_total[window, :] += dot(d_scores, query)
            d_query = (dot_rows(keys, d_scores) * HEAD**-0.5).T
            dq_ref[queries, :] = jnp.where(keep, d_query.astype(bf16), dq_ref[queries, :])

        over_window(first_row, end_one, end_two, count, body)
        return carry

    lax.fori_loop(0, count // QUERY_ROWS, step, 0)
    dk_ref[...] = dk_total[...].astype(bf16)
    d_value = dv_total[...].astype(bf16)
    dv_ref[...] = d_value
    sums_ref[0:1, :] = jnp.sum(dq_ref[...].astype(f32), axis=0, keepdims=True)
    sums_ref[1:2, :] = jnp.sum(d_value.astype(f32), axis=0, keepdims=True)


def attention_backward(qkv, d_ctx, ctx, lse, valid_column, ends, heads):
    count, width = ctx.shape
    active, pairs = heads.shape[0], width // LANES
    part = jax.ShapeDtypeStruct((count, width), bf16)
    return pl.pallas_call(
        backward_kernel,
        grid_spec=pltpu.PrefetchScalarGridSpec(
            num_scalar_prefetch=2,
            grid=(active,),
            in_specs=[
                pair_block(count, 0),
                pair_block(count, pairs),
                pair_block(count, 2 * pairs),
                pair_block(count, 0),
                pair_block(count, 0),
                pl.BlockSpec((1, 1, count), lambda i, heads, ends: (heads[i], 0, 0)),
                pl.BlockSpec((count, 1), lambda i, heads, ends: (0, 0)),
            ],
            out_specs=[pair_block(count, 0)] * 3
            + [pl.BlockSpec((8, LANES), lambda i, heads, ends: (0, heads[i] // 2))],
            scratch_shapes=[
                pltpu.VMEM((count, count), f32),
                pltpu.VMEM((count, LANES), bf16),
                pltpu.VMEM((count, LANES), bf16),
                pltpu.VMEM((count, LANES), f32),
                pltpu.VMEM((count, LANES), f32),
                pltpu.VMEM((1, count), f32),
            ],
        ),
        out_shape=[part, part, part, jax.ShapeDtypeStruct((8, width), f32)],
        compiler_params=pltpu.CompilerParams(vmem_limit_bytes=40 * 2**20),
        cost_estimate=pl.CostEstimate(
            flops=30 * count * count * HEAD * active,
            bytes_accessed=16 * count * width,
            transcendentals=count * count * active,
        ),
        name="attention_backward",
    )(heads, ends, qkv, qkv, qkv, d_ctx, ctx, lse, valid_column)


def normalize(value):
    mean = jnp.mean(value, axis=-1, keepdims=True)
    centred = value - mean
    root = lax.rsqrt(jnp.mean(centred * centred, axis=-1, keepdims=True) + EPS_NORM)
    return centred * root, root


def normalize_back(grad, hat, root, gain):
    scaled = grad * gain
    mean_one = jnp.mean(scaled, axis=-1, keepdims=True)
    mean_two = jnp.mean(scaled * hat, axis=-1, keepdims=True)
    back = root * (scaled - mean_one - hat * mean_two)
    return back, jnp.sum(grad * hat, axis=0), jnp.sum(grad, axis=0)


def adamw(master, first, second, grad, rate, decay):
    first_new = BETA_ONE * first + (1.0 - BETA_ONE) * grad
    second_new = BETA_TWO * second + (1.0 - BETA_TWO) * grad * grad
    first_hat = first_new / (1.0 - BETA_ONE**STEP)
    second_hat = second_new / (1.0 - BETA_TWO**STEP)
    master_new = master - rate * (first_hat / (jnp.sqrt(second_hat) + ADAM_EPS) + decay * master)
    return master_new, first_new, second_new


def gather_rows(shard):
    return lax.all_gather(shard, AXES, axis=0, tiled=True)


def scatter_rows(grad):
    return lax.psum_scatter(grad.astype(bf16), AXES, scatter_dimension=0, tiled=True).astype(f32)


def gather_tiles(shard):
    tiles = lax.all_gather(shard, AXES, axis=0)
    dp, unit = lax.axis_size("dp"), lax.axis_size("unit")
    tiles = tiles.reshape(dp, unit, *shard.shape).transpose(0, 2, 1, 3)
    return tiles.reshape(dp * shard.shape[0], unit * shard.shape[1])


def scatter_tiles(grad):
    dp, unit = lax.axis_size("dp"), lax.axis_size("unit")
    rows, cols = grad.shape[0] // dp, grad.shape[1] // unit
    tiles = grad.astype(bf16).reshape(dp, rows, unit, cols).transpose(0, 2, 1, 3)
    tiles = tiles.reshape(dp * unit * rows, cols)
    return lax.psum_scatter(tiles, AXES, scatter_dimension=0, tiled=True).astype(f32)


def shards(
    layer_input, teacher, cotangent, key_valid, seg_lengths, head_mask, hidden_mask, inter_mask,
    proj_master, proj_first, proj_second, up_master, up_first, up_second,
    down_master, down_first, down_second, vector_master, vector_first, vector_second,
):
    rows, width = layer_input.shape
    all_heads = head_mask.shape[0]
    hidden_gate = hidden_mask.astype(f32)
    unit_gate = inter_mask.astype(f32)
    valid = key_valid.astype(f32)[:, None]
    valid_column = key_valid[:, None]
    ends = jnp.cumsum(seg_lengths[0])
    pruned = jnp.argmin(head_mask).astype(jnp.int32)
    heads = jnp.arange(all_heads - 1, dtype=jnp.int32)
    heads = heads + (heads >= pruned).astype(jnp.int32)
    head_gate = jnp.repeat(head_mask.astype(bf16), HEAD)
    vec = vector_master
    inner_bias = vec[9:].reshape(-1)

    proj_low = proj_master.astype(bf16)
    w_qkv = gather_rows(proj_low[:, : 3 * width])
    w_rest = gather_rows(proj_low[:, 3 * width :])
    w_out, w_dist = w_rest[:, :width], w_rest[:, width:]
    w_up = gather_tiles(up_master.astype(bf16))
    w_down = gather_tiles(down_master.astype(bf16).T)

    bias_qkv = jnp.concatenate([vec[0], jnp.zeros_like(vec[0]), vec[1]])
    qkv = (dot(layer_input, w_qkv) + bias_qkv).astype(bf16)
    ctx, lse = attention_forward(qkv, valid_column, ends, heads, all_heads)
    attn = (dot(ctx, w_out) + vec[2]) * hidden_gate
    hat_one, root_one = normalize(layer_input.astype(f32) + attn)
    first = hat_one * vec[3] + vec[4]
    first_low = first.astype(bf16)

    inner = dot(first_low, w_up) + inner_bias
    cdf = 0.5 * (1.0 + lax.erf(inner * 0.7071067811865476))
    pdf = jnp.exp(-0.5 * inner * inner) * 0.3989422804014327
    active = (inner * cdf * unit_gate).astype(bf16)
    slope = ((cdf + inner * pdf) * unit_gate).astype(bf16)
    branch = (dot_cols(active, w_down) + vec[5]) * hidden_gate
    hat_two, root_two = normalize(first + branch)
    out_low = (hat_two * vec[6] + vec[7]).astype(bf16)
    error = dot(out_low, w_dist) + vec[8] - teacher.astype(f32)
    half_sq = 0.5 * jnp.sum(valid * error * error)
    d_student = (valid * error).astype(bf16)
    g_dist = dot_rows(out_low, d_student)
    g_bias_dist = jnp.sum(d_student.astype(f32), axis=0)
    d_out = cotangent.astype(f32) + dot_cols(d_student, w_dist)
    d_second, g_gain_two, g_shift_two = normalize_back(d_out, hat_two, root_two, vec[6])
    d_branch = (d_second * hidden_gate).astype(bf16)
    g_bias_two = jnp.sum(d_branch.astype(f32), axis=0)

    d_inner = (dot(d_branch, w_down) * slope.astype(f32)).astype(bf16)
    g_down = scatter_tiles(dot_rows(d_branch, active))
    g_up = scatter_tiles(dot_rows(first_low, d_inner))
    g_inner_bias = jnp.sum(d_inner.astype(f32), axis=0)
    d_first = d_second + dot_cols(d_inner, w_up)
    d_first_sum, g_gain_one, g_shift_one = normalize_back(d_first, hat_one, root_one, vec[3])
    d_attn = (d_first_sum * hidden_gate).astype(bf16)
    g_bias_out = jnp.sum(d_attn.astype(f32), axis=0)
    g_out = dot_rows(ctx, d_attn)
    g_rest = scatter_rows(jnp.concatenate([g_out, g_dist], axis=1))
    d_ctx = dot_cols(d_attn, w_out).astype(bf16) * head_gate
    dq, dk, dv, bias_sums = attention_backward(qkv, d_ctx, ctx, lse, valid_column, ends, heads)
    d_qkv = jnp.concatenate([dq, dk, dv], axis=1)
    g_qkv = scatter_rows(dot_rows(layer_input, d_qkv))
    input_grad = d_first_sum + dot_cols(d_qkv, w_qkv)

    g_proj = jnp.concatenate([g_qkv, g_rest], axis=1)
    vector_grad = jnp.concatenate(
        [
            jnp.stack(
                [
                    bias_sums[0], bias_sums[1], g_bias_out, g_gain_one, g_shift_one,
                    g_bias_two, g_gain_two, g_shift_two, g_bias_dist,
                ]
            ),
            g_inner_bias.reshape(-1, width),
        ]
    )
    shard_sq = jnp.sum(g_proj * g_proj) + jnp.sum(g_up * g_up) + jnp.sum(g_down * g_down)
    vector_grad, half_total, shard_total = lax.psum((vector_grad, half_sq, shard_sq), AXES)
    grad_norm = jnp.sqrt(shard_total + jnp.sum(vector_grad * vector_grad))
    clip = jnp.minimum(1.0, CLIP_NORM / (grad_norm + 1e-06))
    all_tokens = rows * lax.axis_size("dp") * lax.axis_size("unit")
    distill_loss = 2.0 * half_total / (all_tokens * width)
    return (
        out_low,
        input_grad,
        grad_norm,
        distill_loss,
        *adamw(proj_master, proj_first, proj_second, clip * g_proj, RATE_MATRIX, DECAY_MATRIX),
        *adamw(up_master, up_first, up_second, clip * g_up, RATE_MATRIX, DECAY_MATRIX),
        *adamw(down_master, down_first, down_second, clip * g_down.T, RATE_MATRIX, DECAY_MATRIX),
        *adamw(vector_master, vector_first, vector_second, clip * vector_grad, RATE_VECTOR, 0.0),
    )


def solution(mesh):
    by_token = P(AXES, None)
    tile, tile_back = P("dp", "unit"), P("unit", "dp")
    in_specs = (
        (by_token, by_token, by_token, P(AXES), by_token, P(), P(), P())
        + (by_token,) * 3
        + (tile,) * 3
        + (tile_back,) * 3
        + (P(),) * 3
    )
    out_specs = (
        (by_token, by_token, P(), P()) + (by_token,) * 3 + (tile,) * 3 + (tile_back,) * 3 + (P(),) * 3
    )
    return jax.shard_map(shards, mesh=mesh, in_specs=in_specs, out_specs=out_specs, check_vma=False)
```

time: 988 us -> 835 us (0.85)
  matrix products: 294 us -> 94.3 us
  waiting for transfers between devices: 376 us -> 476 us
  other arithmetic: 116 us -> 26.5 us
  Pallas kernels: 0 us -> 84.5 us
  local copies, waits for them, and re-layouts: 122 us -> 84.7 us
    dot_general x29 -> x15, matrix products: 294 us -> 94.3 us  [the longest x5 37.4 us: dot(): return jnp.dot(left, right, preferred_element_type=f32)]
    pallas_call x0 -> x2, Pallas kernels: none -> 84.5 us  [the longest x1 44.5 us: attention_backward(): pl.pallas_call(backward_kernel, grid_spec=pltpu.PrefetchScalarGridSpec(nu...]
    reduce_scatter x5 -> x4, waiting for transfers between devices: 216 us -> 297 us  [the longest x2 219 us: scatter_tiles(): lax.psum_scatter(tiles, AXES, scatter_dimension=0, tiled=True).astype(f32)]
    dynamic_update_slice x5 -> x0, local copies, waits for them, and re-layouts: 61.4 us -> none  [the longest x4 60.9 us: shards(): context, log_total = lax.map(forward_block, jnp.arange(blocks))]
    convert_element_type x11 -> x7, other arithmetic: 53.2 us -> 6.01 us  [the longest x1 1.64 us: shards(): w_up = gather_tiles(up_master.astype(bf16))]
    reduce_sum x11 -> x2, other arithmetic: 39 us -> 0.77 us  [normalize(): jnp.mean(centred * centred, axis=-1, keepdims=True) + EPS_NORM]
    reshape x6 -> x5, local copies, waits for them, and re-layouts: 0.04 us -> 31.5 us  [the longest x2 19.5 us: scatter_tiles(): grad.astype(bf16).reshape(dp, rows, unit, cols).transpose(0, 2, 1, 3)]
    all_gather x5 -> x4, waiting for transfers between devices: 160 us -> 179 us  [the longest x2 117 us: gather_tiles(): tiles = lax.all_gather(shard, AXES, axis=0)]
  transfers between devices with their start and end apart: 10 -> 8, of which waited for: 7 -> 7; matrix products, arithmetic and copies ran while one was open for 47% -> 14% of each run, Pallas kernels for 0% -> 10%
where the time goes in v1:
time: 835 us; the launch traced here: 829 us
  waiting for transfers between devices  476 us (57%)
  matrix products  94.3 us (11%)
  local copies, waits for them, and re-layouts  84.7 us (10%)
  Pallas kernels  84.5 us (10%)
  blocking collectives  40.6 us (5%)
  other arithmetic  26.5 us (3%)
  between operations  21.8 us (3%)
    reduce_scatter x2, waiting for transfers between devices, scatter_tiles(): lax.psum_scatter(tiles, AXES, scatter_dimension=0, tiled=True).astype(f32)  219 us
    all_gather x2, waiting for transfers between devices, gather_tiles(): tiles = lax.all_gather(shard, AXES, axis=0)  117 us
    reduce_scatter x2, waiting for transfers between devices, scatter_rows(): lax.psum_scatter(grad.astype(bf16), AXES, scatter_dimension=0, tiled=True)  77.4 us
    all_gather x2, waiting for transfers between devices, gather_rows(): return lax.all_gather(shard, AXES, axis=0, tiled=True)  61.9 us
    pallas_call x1, Pallas kernels, attention_backward(): pl.pallas_call(backward_kernel, grid_spec=pltpu.PrefetchScalarGridSpec(nu...  44.5 us
    psum x1, blocking collectives, shards(): lax.psum((vector_grad, half_sq, shard_sq), AXES)  40.6 us
    pallas_call x1, Pallas kernels, attention_forward(): pl.pallas_call(forward_kernel, grid_spec=pltpu.PrefetchScalarGridSpec(num...  40 us
    unnamed x68, local copies, waits for them, and re-layouts  38.8 us
  transfers between devices with their start and end apart: 8, of which 7 were waited for; matrix products, arithmetic and copies ran while one was open for 14% of the time, Pallas kernels for 10%

profile of v1, /device:TPU:0, one launch (start us, length us, event | category | flops | bytes accessed | tf_op | source)
XLA Modules:
  0.0 828.6 jit_solution(4970498615586408410)
XLA Ops:
  23.9 50.5 %all-gather.7.cloned.1.call-done = bf16[768,2304]{1,0:T(8,128)(2,1)} async-done(((bf16[24,2304]{1,0:T(8,128)(2,1)}), bf16[768,2304]{1,0:T(8,128)(2,1)}) %all-gather.7.cloned.1.call-update) | async-done | bytes 3538960 | tf_op jit(solution)/shard_map/all_gather | solution.py:266
  74.4 6.1 add_convert_fusion.q_ref.k_ref.v_ref
  80.5 40.0 %attention_forward.1 = (bf16[1024,768]{1,0:T(8,128)(2,1)S(1)}, f32[12,1,1024]{2,1,0:T(1,128)S(1)}) custom-call(s32[11]{0:T(128)S(1)} %fusion.29.heads_ref, s32[3]{0:T(128)S(1)} %bitcast.59, bf16[1024,2304]{1,0:T(8,128)(2,1)S(1)} %add_convert_fusion.q_ref.k_ref.v_ref, bf16[1024,2304]{1,0:T(8,128)(2,1)S(1)} %add_convert_fusion.q_ref.k_ref.v_ref, ...), custom_call_target="tpu_custom_call" | custom-call | flops 22145925120 | bytes 6291456 | tf_op jit(solution)/shard_map/attention_forward/pallas_call | solution.py:119
  122.6 11.4 %all-gather.9.cloned.1.call-done = bf16[768,1536]{1,0:T(8,128)(2,1)} async-done(((bf16[24,1536]{1,0:T(8,128)(2,1)}), bf16[768,1536]{1,0:T(8,128)(2,1)}) %all-gather.9.cloned.1.call-update) | async-done | bytes 2359312 | tf_op jit(solution)/shard_map/all_gather | solution.py:266
  139.6 60.4 %all-gather.11.cloned.1.call-done = bf16[3072,768]{1,0:T(8,128)(2,1)} async-done(((bf16[96,768]{1,0:T(8,128)(2,1)}), bf16[3072,768]{1,0:T(8,128)(2,1)}) %all-gather.11.cloned.1.call-update) | async-done | bytes 4718608 | tf_op jit(solution)/shard_map/all_gather | solution.py:274
  200.1 6.0 copy.76
  209.3 56.6 %all-gather.13.cloned.1.call-done = bf16[3072,768]{1,0:T(8,128)(2,1)} async-done(((bf16[96,768]{1,0:T(8,128)(2,1)}), bf16[3072,768]{1,0:T(8,128)(2,1)}) %all-gather.13.cloned.1.call-update) | async-done | bytes 4718608 | tf_op jit(solution)/shard_map/all_gather | solution.py:274
  265.9 6.0 copy.77
  275.1 10.8 %multiply_convert_fusion.1 = (bf16[1024,3072]{1,0:T(8,128)(2,1)S(1)}, f32[1024,3072]{1,0:T(8,128)}) fusion(f32[3072]{0:T(1024)S(1)} %convert_element_type.106, f32[3072]{0:T(1024)S(1)} %add.208, bf16[768,3072]{1,0:T(8,128)(2,1)S(1)} %bitcast.69, f32[1024,768]{0,1:T(8,128)S(1)} %copy-done.3, f32[768]{0:T(1024)S(1)} %get-tuple-element.90, ...), kind=kOutput, calls=%fused_computation.9 | convolution fusion | flops 4857790464 | bytes 26777600 | tf_op jit(solution)/shard_map/dot_general | solution.py:27
  302.1 14.2 %convert_reduce_fusion = (f32[3072]{0:T(1024)S(1)}, bf16[1024,3072]{1,0:T(8,128)(2,1)}) fusion(f32[3072]{0:T(1024)S(1)} %convert_element_type.106, f32[1024,3072]{1,0:T(8,128)} %get-tuple-element.120, f32[3072]{0:T(1024)S(1)} %add.208, bf16[1024,768]{0,1:T(8,128)(2,1)S(1)} %get-tuple-element.113, bf16[768,3072]{1,0:T(8,128)(2,1)S(1)} %bitcast.72), kind=kOutput, calls=%fused_computation.7 | convolution fusion | flops 4882166784 | bytes 25202688 | tf_op jit(solution)/shard_map/dot_general | solution.py:27
  316.3 8.7 %multiply_reduce_fusion.1 = (f32[768]{0:T(1024)S(1)}, f32[1024]{0:T(1024)S(1)}, f32[1024]{0:T(1024)S(1)}, f32[768]{0:T(1024)S(1)}, f32[1024,768]{0,1:T(8,128)S(1)}) fusion(f32[1024,768]{0,1:T(8,128)S(1)} %copy-done.3, f32[1024]{0:T(1024)S(1)} %add_rsqrt_fusion.1, f32[1024]{0:T(1024)S(1)} %broadcast_multiply_fusion.5, f32[768]{0:T(1024)S(1)} %get-tuple-element.91, ...), kind=kOutput, calls=%fused_computation.22 | convolution fusion | flops 4845203456 | bytes 23638016 | tf_op jit(solution)/shard_map/dot_general | solution.py:35
  339.7 44.5 %attention_backward.1 = (bf16[1024,768]{1,0:T(8,128)(2,1)S(1)}, bf16[1024,768]{1,0:T(8,128)(2,1)S(1)}, bf16[1024,768]{1,0:T(8,128)(2,1)S(1)}, f32[8,768]{1,0:T(8,128)S(1)}) custom-call(s32[11]{0:T(128)S(1)} %fusion.29.heads_ref, s32[3]{0:T(128)S(1)} %bitcast.60, bf16[1024,2304]{1,0:T(8,128)(2,1)S(1)} %copy-done.1, bf16[1024,2304]{1,0:T(8,128)(2,1)S(1)} %copy-done.1, ...), custom_call_target="tpu_custom_call" | custom-call | flops 22145925120 | bytes 12582912 | tf_op jit(solution)/shard_map/attention_backward/pallas_call | solution.py:205
  392.0 5.8 copy.94
  397.9 9.9 %convolution_convert_fusion.1 = bf16[768,3072]{1,0:T(8,128)(2,1)} fusion(bf16[1024,3072]{1,0:T(8,128)(2,1)} %get-tuple-element.126, f32[1024,768]{0,1:T(8,128)} %copy-done.2, f32[768]{0:T(1024)S(1)} %get-tuple-element.90, f32[768]{0:T(1024)S(1)} %get-tuple-element.91, f32[1024]{0:T(1024)S(1)} %add_rsqrt_fusion.1, f32[1024]{0:T(1024)S(1)} %broadcast_multiply_fusion.5), kind=kOutput, calls=%fused_computation.13 | convolution fusion | flops 4838129664 | bytes 14170112 | tf_op jit(solution)/shard_map/dot_general | solution.py:31
  407.8 9.8 %reshape.138 = bf16[8,96,4,768]{3,2,1,0:T(4,128)(2,1)} reshape(bf16[768,3072]{1,0:T(8,128)(2,1)} %convolution_convert_fusion.1) | data formatting | bytes 9437184 | tf_op jit(solution)/shard_map/reshape | solution.py:283
  417.6 5.5 copy.86
  424.5 9.7 %convolution_convert_fusion = bf16[768,3072]{1,0:T(8,128)(2,1)} fusion(bf16[1024,768]{0,1:T(8,128)(2,1)S(1)} %copy-done.13, bf16[1024,3072]{1,0:T(8,128)(2,1)} %copy-done.28), kind=kOutput, calls=%fused_computation.12 | convolution fusion | flops 4834197504 | bytes 12582912 | tf_op jit(solution)/shard_map/dot_general | solution.py:31
  434.1 9.8 %reshape.140 = bf16[8,96,4,768]{3,2,1,0:T(4,128)(2,1)} reshape(bf16[768,3072]{1,0:T(8,128)(2,1)} %convolution_convert_fusion) | data formatting | bytes 9437184 | tf_op jit(solution)/shard_map/reshape | solution.py:283
  443.9 5.6 copy.87
  453.3 9.6 %convolution_add_fusion.1 = f32[1024,768]{0,1:T(8,128)S(1)} fusion(bf16[1024,2304]{1,0:T(8,128)(2,1)} %copy-done.17, bf16[768,2304]{1,0:T(8,128)(2,1)} %all-gather.7.cloned.1.call-done, f32[1024]{0:T(1024)S(1)} %broadcast_multiply_fusion, f32[1024,768]{0,1:T(8,128)} %copy-done.2, f32[1024]{0:T(1024)S(1)} %broadcast_multiply_fusion.5, ...), kind=kOutput, calls=%fused_computation.45 | convolution fusion | flops 3630170112 | bytes 17714176 | tf_op jit(solution)/shard_map/dot_general | solution.py:35
  462.9 77.3 %reduce-scatter.13.cloned.1.call-done = bf16[24,2304]{1,0:T(8,128)(2,1)} async-done(((bf16[768,2304]{1,0:T(8,128)(2,1)}), bf16[24,2304]{1,0:T(8,128)(2,1)}) %reduce-scatter.13.cloned.1.call-update) | async-done | bytes 110608 | tf_op jit(solution)/shard_map/reduce_scatter | solution.py:270
  541.9 110.7 %reduce-scatter.9.cloned.1.call-done = bf16[96,768]{1,0:T(8,128)(2,1)} async-done(((bf16[3072,768]{1,0:T(8,128)(2,1)}), bf16[96,768]{1,0:T(8,128)(2,1)}) %reduce-scatter.9.cloned.1.call-update) | async-done | bytes 147472 | tf_op jit(solution)/shard_map/reduce_scatter | solution.py:285
  655.5 108.7 %reduce-scatter.11.cloned.1.call-done = bf16[96,768]{1,0:T(8,128)(2,1)} async-done(((bf16[3072,768]{1,0:T(8,128)(2,1)}), bf16[96,768]{1,0:T(8,128)(2,1)}) %reduce-scatter.11.cloned.1.call-update) | async-done | bytes 147472 | tf_op jit(solution)/shard_map/reduce_scatter | solution.py:285
  768.8 40.6 %all-reduce = (f32[]{:T(128)}, f32[13,768]{1,0:T(8,128)S(1)}, f32[]{:T(128)}) all-reduce(f32[]{:T(128)S(6)} %add.229, f32[13,768]{1,0:T(8,128)S(1)} %concatenate.25, f32[]{:T(128)S(6)} %mul.421), channel_id=1, replica_groups=mesh['dp'=8,'unit'=4] {'dp','unit'}, use_global_device_ids=true, to_apply=%region_17.18 | all-reduce | flops 9986 | bytes 79888 | tf_op jit(solution)/shard_map/psum | solution.py:369
  (144 shorter events, 88.7 us)
Async XLA Ops:
  7.2 10.7 %copy-start.8 = (bf16[1024,768]{1,0:T(8,128)(2,1)S(1)}, bf16[1024,768]{1,0:T(8,128)(2,1)}, u32[]{:S(2)}) copy-start(bf16[1024,768]{1,0:T(8,128)(2,1)} %param.22) | copy-start | bytes 4718596
  7.2 67.2 %all-gather.7.cloned.1.call-start = ((), (), s32[]{:S(2)}) async-start(), calls=%async_computation.4 | async-start | bytes 3649536 | tf_op jit(solution)/shard_map/all_gather | solution.py:266
  9.0 125.0 %all-gather.9.cloned.1.call-start = ((), (), s32[]{:S(2)}) async-start(), calls=%async_computation.5 | async-start | bytes 2433024 | tf_op jit(solution)/shard_map/all_gather | solution.py:266
  9.8 190.3 %all-gather.11.cloned.1.call-start = ((), (), s32[]{:S(2)}) async-start(), calls=%async_computation.8 | async-start | bytes 4866048 | tf_op jit(solution)/shard_map/all_gather | solution.py:274
  11.5 254.3 %all-gather.13.cloned.1.call-start = ((), (), s32[]{:S(2)}) async-start(), calls=%async_computation.9 | async-start | bytes 4866048 | tf_op jit(solution)/shard_map/all_gather | solution.py:274
  13.2 449.7 %reduce-scatter.15.cloned.1.call-start = ((), (), s32[]{:S(2)}) async-start(), calls=%async_computation.11 | async-start | bytes 2433024 | tf_op jit(solution)/shard_map/reduce_scatter | solution.py:270
  17.9 4.4 copy-start.26
  17.9 4.6 copy-start.27
  17.9 5.9 copy-start.22
  19.6 54.8 %copy-start.9 = (bf16[1024,768]{1,0:T(8,128)(2,1)S(1)}, bf16[1024,768]{1,0:T(8,128)(2,1)}, u32[]{:S(2)}) copy-start(bf16[1024,768]{1,0:T(8,128)(2,1)} %param.20) | copy-start | bytes 4718596
  271.8 3.3 copy-start.6
  286.0 5.4 copy-start.28
  292.3 4.9 copy-start.4
  302.1 14.2 %copy-start.12 = (bf16[1024,768]{0,1:T(8,128)(2,1)}, bf16[1024,768]{0,1:T(8,128)(2,1)S(1)}, u32[]{:S(2)}) copy-start(bf16[1024,768]{0,1:T(8,128)(2,1)S(1)} %get-tuple-element.113) | copy-start | bytes 4718596
  334.0 206.2 %reduce-scatter.13.cloned.1.call-start = ((), (), s32[]{:S(2)}) async-start(), calls=%async_computation.10 | async-start | bytes 3649536 | tf_op jit(solution)/shard_map/reduce_scatter | solution.py:270
  397.9 254.8 %reduce-scatter.9.cloned.1.call-start = ((), (), s32[]{:S(2)}) async-start(), calls=%async_computation.6 | async-start | bytes 4866048 | tf_op jit(solution)/shard_map/reduce_scatter | solution.py:285
  423.1 341.1 %reduce-scatter.11.cloned.1.call-start = ((), (), s32[]{:S(2)}) async-start(), calls=%async_computation.7 | async-start | bytes 4866048 | tf_op jit(solution)/shard_map/reduce_scatter | solution.py:285
  766.4 45.6 %copy-start.23 = (f32[13,768]{1,0:T(8,128)S(1)}, f32[13,768]{1,0:T(8,128)}, u32[]{:S(2)}) copy-start(f32[13,768]{1,0:T(8,128)} %param.37) | copy-start | bytes 119812
  766.5 47.1 %copy-start.16 = (f32[768,96]{0,1:T(8,128)S(1)}, f32[768,96]{0,1:T(8,128)}, u32[]{:S(2)}) copy-start(f32[768,96]{0,1:T(8,128)} %param.34) | copy-start | bytes 884740
  768.8 49.2 %copy-start.15 = (f32[24,3840]{1,0:T(8,128)S(1)}, f32[24,3840]{1,0:T(8,128)}, u32[]{:S(2)}) copy-start(f32[24,3840]{1,0:T(8,128)} %param.28) | copy-start | bytes 1105924
  768.8 49.2 %copy-start.18 = (bf16[24,2304]{1,0:T(8,128)(2,1)S(1)}, bf16[24,2304]{1,0:T(8,128)(2,1)}, u32[]{:S(2)}) copy-start(bf16[24,2304]{1,0:T(8,128)(2,1)} %reduce-scatter.13.cloned.1.call-done) | copy-start | bytes 331780
  768.8 49.2 %copy-start.19 = (f32[24,3840]{1,0:T(8,128)S(1)}, f32[24,3840]{1,0:T(8,128)}, u32[]{:S(2)}) copy-start(f32[24,3840]{1,0:T(8,128)} %param.29) | copy-start | bytes 1105924
  768.8 49.2 %copy-start.20 = (f32[24,3840]{1,0:T(8,128)S(1)}, f32[24,3840]{1,0:T(8,128)}, u32[]{:S(2)}) copy-start(f32[24,3840]{1,0:T(8,128)} %param.30) | copy-start | bytes 1105924
  768.8 49.2 %copy-start.21 = (bf16[24,1536]{1,0:T(8,128)(2,1)S(1)}, bf16[24,1536]{1,0:T(8,128)(2,1)}, u32[]{:S(2)}) copy-start(bf16[24,1536]{1,0:T(8,128)(2,1)} %reduce-scatter.15.cloned.1.call-done) | copy-start | bytes 221188
  (13 other events, 24.8 us)
Sparse Core Ops, SparseCore 0:
  11.5 62.8 all-gather.6
  77.9 56.1 all-gather.8
  137.5 62.5 all-gather.10
  203.4 62.4 all-gather.12
  334.2 97.8 reduce-scatter.14
  438.2 102.0 reduce-scatter.12
  546.7 105.9 reduce-scatter.8
  658.1 106.0 reduce-scatter.10

commit v2 on v1

v2 whole, which is shorter than its diff:
```python
from functools import partial

import jax
import jax.numpy as jnp
from jax import lax
from jax.experimental import pallas as pl
from jax.experimental.pallas import tpu as pltpu
from jax.sharding import PartitionSpec as P

STEP = 10
EPS_NORM = 1e-05
BETA_ONE = 0.9
BETA_TWO = 0.999
ADAM_EPS = 1e-08
RATE_MATRIX = 0.1
RATE_VECTOR = 1.0
DECAY_MATRIX = 0.01
CLIP_NORM = 1.0
HEAD = 64
LANES = 128
HEADS_PER_CHUNK = 4
QUERY_ROWS = 256
MASKED = -1e30
AXES = ("dp", "unit")
f32 = jnp.float32
bf16 = jnp.bfloat16


def dot(left, right):
    return jnp.dot(left, right, preferred_element_type=f32)


def dot_rows(left, right):
    return lax.dot_general(left, right, (((0,), (0,)), ((), ())), preferred_element_type=f32)


def dot_cols(left, right):
    return lax.dot_general(left, right, (((1,), (1,)), ((), ())), preferred_element_type=f32)


def build_bias(bias_ref, valid_ref, end_one, end_two):
    count = bias_ref.shape[0]
    for start in range(0, count, QUERY_ROWS):
        key = lax.broadcasted_iota(jnp.int32, (count, QUERY_ROWS), 0)
        query = lax.broadcasted_iota(jnp.int32, (count, QUERY_ROWS), 1) + start
        seg_key = (key >= end_one).astype(jnp.int32) + (key >= end_two).astype(jnp.int32)
        seg_query = (query >= end_one).astype(jnp.int32) + (query >= end_two).astype(jnp.int32)
        allowed = (seg_key == seg_query) & ((valid_ref[...] > 0) | (key == query))
        bias_ref[:, start : start + QUERY_ROWS] = jnp.where(allowed, 0.0, MASKED)


def over_window(first_row, end_one, end_two, count, body):
    low = jnp.where(first_row < end_one, 0, jnp.where(first_row < end_two, end_one, end_two))
    last_row = first_row + QUERY_ROWS - 1
    high = jnp.where(last_row < end_one, end_one, jnp.where(last_row < end_two, end_two, count))
    low = (low // 16) * 16
    done = jnp.bool_(False)
    for width in [w for w in (272, 528, 784) if w < count] + [count]:
        start = jnp.minimum(low, count - width)
        fits = (high - start) <= width
        run = fits & jnp.logical_not(done)

        @pl.when(run)
        def _(width=width, start=start):
            body(width, pl.multiple_of(start, 16))

        done = done | fits


def lanes_of(head):
    lane = lax.broadcasted_iota(jnp.int32, (1, LANES), 1)
    return (lane // HEAD) == (head % 2)


def forward_kernel(
    chunk, gate_ref, ends_ref, q_ref, k_ref, v_ref, valid_ref, *refs
):
    ctx_ref, lse_ref, bias_ref, qm_ref = refs[-4:]
    count = q_ref.shape[0]
    end_one, end_two = ends_ref[0], ends_ref[1]
    head = pl.program_id(0)
    keep = lanes_of(head)

    @pl.when(head == 0)
    def _():
        build_bias(bias_ref, valid_ref, end_one, end_two)

    @pl.when(head % 2 == 0)
    def _():
        ctx_ref[...] = jnp.zeros_like(ctx_ref)

    def step(index, carry):
        first_row = pl.multiple_of(index * QUERY_ROWS, QUERY_ROWS)
        queries = pl.ds(first_row, QUERY_ROWS)

        def body(width, start):
            window = pl.ds(start, width)
            scores = dot_cols(k_ref[window, :], qm_ref[queries, :]) + bias_ref[window, queries]
            peak = jnp.max(scores, axis=0, keepdims=True)
            expo = jnp.exp(scores - peak)
            total = jnp.sum(expo, axis=0, keepdims=True)
            out = (dot_rows(v_ref[window, :], expo.astype(bf16)) * (1.0 / total)).T
            ctx_ref[queries, :] = jnp.where(keep, out.astype(bf16), ctx_ref[queries, :])
            lse_ref[0, :, queries] = peak + jnp.log(total)

        over_window(first_row, end_one, end_two, count, body)
        return carry

    @pl.when(gate_ref[chunk * HEADS_PER_CHUNK + head] > 0)
    def _():
        qm_ref[...] = jnp.where(keep, q_ref[...] * bf16(HEAD**-0.5), bf16(0))
        lax.fori_loop(0, count // QUERY_ROWS, step, 0)


def pair_block(count, offset):
    return pl.BlockSpec((count, LANES), lambda i, gate, ends: (0, i // 2 + offset))


def attention_forward(chunk, qkv, valid_column, ends, gate, ctx_before, width):
    count, pairs = qkv.shape[0], HEADS_PER_CHUNK // 2
    in_specs = [
        pair_block(count, 0),
        pair_block(count, pairs),
        pair_block(count, 2 * pairs),
        pl.BlockSpec((count, 1), lambda i, gate, ends: (0, 0)),
    ]
    operands = [gate, ends, qkv, qkv, qkv, valid_column]
    aliases = {}
    if ctx_before is not None:
        in_specs.append(pl.BlockSpec(memory_space=pl.ANY))
        operands.append(ctx_before)
        aliases = {6: 0}
    return pl.pallas_call(
        partial(forward_kernel, chunk),
        grid_spec=pltpu.PrefetchScalarGridSpec(
            num_scalar_prefetch=2,
            grid=(HEADS_PER_CHUNK,),
            in_specs=in_specs,
            out_specs=[
                pair_block(count, chunk * pairs),
                pl.BlockSpec((1, 1, count), lambda i, gate, ends: (i, 0, 0)),
            ],
            scratch_shapes=[pltpu.VMEM((count, count), f32), pltpu.VMEM((count, LANES), bf16)],
        ),
        out_shape=[
            jax.ShapeDtypeStruct((count, width), bf16),
            jax.ShapeDtypeStruct((HEADS_PER_CHUNK, 1, count), f32),
        ],
        input_output_aliases=aliases,
        compiler_params=pltpu.CompilerParams(vmem_limit_bytes=32 * 2**20),
        cost_estimate=pl.CostEstimate(
            flops=45 * count * count * HEAD * HEADS_PER_CHUNK,
            bytes_accessed=8 * count * LANES * pairs,
            transcendentals=count * count * HEADS_PER_CHUNK,
        ),
        name="attention_forward",
    )(*operands)


def backward_kernel(
    chunk, gate_ref, ends_ref, q_ref, k_ref, v_ref, do_ref, ctx_ref, lse_ref, valid_ref,
    grad_ref, sums_ref,
    bias_ref, qm_ref, dom_ref, dq_total, dk_total, dv_total, delta_ref,
):
    count = q_ref.shape[0]
    pairs = HEADS_PER_CHUNK // 2
    end_one, end_two = ends_ref[0], ends_ref[1]
    head = pl.program_id(0)
    keep = lanes_of(head)

    @pl.when(head == 0)
    def _():
        build_bias(bias_ref, valid_ref, end_one, end_two)

    @pl.when(head % 2 == 0)
    def _():
        dq_total[...] = jnp.zeros_like(dq_total)
        dk_total[...] = jnp.zeros_like(dk_total)
        dv_total[...] = jnp.zeros_like(dv_total)

    def step(index, carry):
        first_row = pl.multiple_of(index * QUERY_ROWS, QUERY_ROWS)
        queries = pl.ds(first_row, QUERY_ROWS)

        def body(width, start):
            window = pl.ds(start, width)
            keys, query, grad = k_ref[window, :], qm_ref[queries, :], dom_ref[queries, :]
            scores = dot_cols(keys, query) + bias_ref[window, queries]
            probs = jnp.exp(scores - lse_ref[0, :, queries])
            d_probs = dot_cols(v_ref[window, :], grad)
            d_scores = (probs * (d_probs - delta_ref[:, queries])).astype(bf16)
            dv_total[window, :] += dot(probs.astype(bf16), grad)
            dk_total[window, :] += dot(d_scores, query)
            d_query = (dot_rows(keys, d_scores) * HEAD**-0.5).T
            dq_total[queries, :] = jnp.where(keep, d_query, dq_total[queries, :])

        over_window(first_row, end_one, end_two, count, body)
        return carry

    @pl.when(gate_ref[chunk * HEADS_PER_CHUNK + head] > 0)
    def _():
        qm_ref[...] = jnp.where(keep, q_ref[...] * bf16(HEAD**-0.5), bf16(0))
        dom_ref[...] = jnp.where(keep, do_ref[...], bf16(0))
        product = dom_ref[...].astype(f32) * ctx_ref[...].astype(f32)
        delta_ref[...] = jnp.sum(product.T, axis=0, keepdims=True)
        lax.fori_loop(0, count // QUERY_ROWS, step, 0)

    @pl.when(head % 2 == 1)
    def _():
        for part, total in enumerate((dq_total, dk_total, dv_total)):
            low = total[...].astype(bf16)
            lanes = pl.ds(pl.multiple_of((part * pairs + head // 2) * LANES, LANES), LANES)
            grad_ref[:, lanes] = low
            if part != 1:
                sums_ref[part // 2 : part // 2 + 1, :] = jnp.sum(low.astype(f32), axis=0, keepdims=True)


def attention_backward(chunk, qkv, d_ctx, ctx, lse, valid_column, ends, gate):
    count, pairs = qkv.shape[0], HEADS_PER_CHUNK // 2
    return pl.pallas_call(
        partial(backward_kernel, chunk),
        grid_spec=pltpu.PrefetchScalarGridSpec(
            num_scalar_prefetch=2,
            grid=(HEADS_PER_CHUNK,),
            in_specs=[
                pair_block(count, 0),
                pair_block(count, pairs),
                pair_block(count, 2 * pairs),
                pair_block(count, chunk * pairs),
                pair_block(count, chunk * pairs),
                pl.BlockSpec((1, 1, count), lambda i, gate, ends: (i, 0, 0)),
                pl.BlockSpec((count, 1), lambda i, gate, ends: (0, 0)),
            ],
            out_specs=[
                pl.BlockSpec(qkv.shape, lambda i, gate, ends: (0, 0)),
                pl.BlockSpec((8, LANES), lambda i, gate, ends: (0, i // 2)),
            ],
            scratch_shapes=[
                pltpu.VMEM((count, count), f32),
                pltpu.VMEM((count, LANES), bf16),
                pltpu.VMEM((count, LANES), bf16),
                pltpu.VMEM((count, LANES), f32),
                pltpu.VMEM((count, LANES), f32),
                pltpu.VMEM((count, LANES), f32),
                pltpu.VMEM((1, count), f32),
            ],
        ),
        out_shape=[
            jax.ShapeDtypeStruct(qkv.shape, bf16),
            jax.ShapeDtypeStruct((8, pairs * LANES), f32),
        ],
        compiler_params=pltpu.CompilerParams(vmem_limit_bytes=40 * 2**20),
        cost_estimate=pl.CostEstimate(
            flops=45 * count * count * HEAD * HEADS_PER_CHUNK,
            bytes_accessed=16 * count * LANES * pairs,
            transcendentals=count * count * HEADS_PER_CHUNK,
        ),
        name="attention_backward",
    )(gate, ends, qkv, qkv, qkv, d_ctx, ctx, lse, valid_column)


def bits(size):
    return [1 << k for k in reversed(range(size.bit_length() - 1))]


def add_low(left, right):
    return (left.astype(f32) + right.astype(f32)).astype(bf16)


def hold(*values):
    return lax.optimization_barrier(values)


class Fabric:
    def __init__(self):
        self.dp, self.unit = lax.axis_size("dp"), lax.axis_size("unit")
        self.size = self.dp * self.unit
        self.at_unit = lax.axis_index("unit")
        self.at_dp = lax.axis_index("dp")
        self.me = self.at_dp * self.unit + self.at_unit
        dp_bits, unit_bits = [bit * self.unit for bit in bits(self.dp)], bits(self.unit)
        self.top, self.near, self.far, self.core = dp_bits[:-1], dp_bits[-1], unit_bits[:-1], unit_bits[-1]
        self.offsets = [0]
        for bit in self.far:
            self.offsets = self.offsets + [u ^ bit for u in self.offsets]

    def swap(self, value, bit):
        return lax.ppermute(value, AXES, [(i, i ^ bit) for i in range(self.size)])

    def assemble(self, parts, places):
        flat = jnp.stack([place for rows in places for place in rows]).astype(jnp.int32)

        def kernel(place_ref, *refs):
            index = 0
            for source in refs[:-1]:
                for row in range(source.shape[0]):
                    refs[-1][place_ref[index]] = source[row]
                    index += 1

        count, shape = flat.shape[0], parts[0].shape[1:]
        whole = pl.BlockSpec(memory_space=pltpu.VMEM)
        out = pl.pallas_call(
            kernel,
            in_specs=[pl.BlockSpec(memory_space=pltpu.SMEM)] + [whole] * len(parts),
            out_specs=whole,
            out_shape=jax.ShapeDtypeStruct((count, *shape), parts[0].dtype),
            compiler_params=pltpu.CompilerParams(vmem_limit_bytes=16 * 2**20),
            name="assemble",
        )(flat, *parts)
        return out.reshape(count * shape[0], shape[1])

    def split(self, value, bit, left):
        if bit in left:
            lower = 1 << sorted(left).index(bit)
            value = value.reshape(value.shape[0] // (2 * lower), 2, lower, *value.shape[1:])
            mine = (self.me // bit) % 2
            out = []
            for choice in (1 - mine, mine):
                half = lax.dynamic_index_in_dim(value, choice, 1, keepdims=False)
                out.append(half.reshape(-1, *half.shape[2:]))
            return tuple(out)
        half = value.shape[-1] // 2
        return value[..., half:], value[..., :half]

    def total(self, value):
        for bit in bits(self.size):
            value = value + self.swap(value, bit)
        return value

    def total_soon(self, value):
        steps = bits(self.size)[::-1]
        while steps:
            now, steps = steps[:3], steps[3:]
            masks = [0]
            for bit in now:
                masks = masks + [mask ^ bit for mask in masks]
            terms = [value if mask == 0 else self.swap(value, mask) for mask in masks]
            while len(terms) > 1:
                terms = [a + b for a, b in zip(terms[::2], terms[1::2])]
            value = terms[0]
        return value


class Gather:
    def __init__(self, fabric, block, masks):
        self.fabric, self.state, self.masks = fabric, block, masks

    def rows(self, bit):
        self.state = jnp.concatenate([self.state, self.fabric.swap(self.state, bit)])
        self.masks = self.masks + [mask ^ bit for mask in self.masks]

    def columns(self, bit):
        self.state = jnp.concatenate([self.state, self.fabric.swap(self.state, bit)], axis=-1)

    def place(self, shift, base):
        places = [base ^ (mask // shift) for mask in self.masks]
        self.state = self.fabric.assemble([self.state], [places])


class Scatter:
    def __init__(self, fabric, send, keep, bit, steps, rows):
        self.fabric, self.state, self.bit, self.steps = fabric, (send, keep), bit, list(steps)
        self.rows = [r for r in rows if r != bit]

    @classmethod
    def of(cls, fabric, grad, steps, rows):
        send, keep = fabric.split(grad, steps[0], rows)
        return cls(fabric, send, keep, steps[0], steps[1:], rows)

    def tick(self):
        send, keep = self.state
        other = self.fabric.swap(send, self.bit)
        if not self.steps:
            self.state = keep.astype(f32) + other.astype(f32)
            return
        self.bit = self.steps.pop(0)
        mine, theirs = (self.fabric.split(v, self.bit, self.rows) for v in (keep, other))
        self.rows = [r for r in self.rows if r != self.bit]
        self.state = tuple(add_low(a, b) for a, b in zip(mine, theirs))

    @classmethod
    def merge(cls, chains):
        first = chains[0]
        send, keep = (jnp.concatenate([c.state[i] for c in chains], axis=-1) for i in range(2))
        return cls(first.fabric, send, keep, first.bit, first.steps, first.rows)


def hold_all(values, chains):
    values, states = hold(values, [c.state for c in chains])
    for chain, state in zip(chains, states):
        chain.state = state
    return values


def normalize(value):
    mean = jnp.mean(value, axis=-1, keepdims=True)
    centred = value - mean
    root = lax.rsqrt(jnp.mean(centred * centred, axis=-1, keepdims=True) + EPS_NORM)
    return centred * root, root


def normalize_back(grad, hat, root, gain):
    scaled = grad * gain
    mean_one = jnp.mean(scaled, axis=-1, keepdims=True)
    mean_two = jnp.mean(scaled * hat, axis=-1, keepdims=True)
    back = root * (scaled - mean_one - hat * mean_two)
    return back, jnp.sum(grad * hat, axis=0), jnp.sum(grad, axis=0)


def adamw(master, first, second, grad, rate, decay):
    first_new = BETA_ONE * first + (1.0 - BETA_ONE) * grad
    second_new = BETA_TWO * second + (1.0 - BETA_TWO) * grad * grad
    first_hat = first_new / (1.0 - BETA_ONE**STEP)
    second_hat = second_new / (1.0 - BETA_TWO**STEP)
    master_new = master - rate * (first_hat / (jnp.sqrt(second_hat) + ADAM_EPS) + decay * master)
    return master_new, first_new, second_new


def shards(
    layer_input, teacher, cotangent, key_valid, seg_lengths, head_mask, hidden_mask, inter_mask,
    proj_master, proj_first, proj_second, up_master, up_first, up_second,
    down_master, down_first, down_second, vector_master, vector_first, vector_second,
):
    fabric = Fabric()
    top, near, far, core = fabric.top, fabric.near, fabric.far, fabric.core
    all_bits = top + [near] + far + [core]
    dp_bits = top + [near]
    rows, width = layer_input.shape
    chunks = head_mask.shape[0] // HEADS_PER_CHUNK
    span = HEADS_PER_CHUNK * HEAD
    hidden_gate = hidden_mask.astype(f32)
    valid = key_valid.astype(f32)[:, None]
    valid_column = key_valid[:, None]
    ends = jnp.cumsum(seg_lengths[0])
    head_gate = jnp.repeat(head_mask.astype(bf16), HEAD)
    vec = vector_master
    units = up_master.shape[1]

    def by_offset(values, offsets):
        return [
            lax.dynamic_index_in_dim(values, fabric.at_unit ^ u, 0, keepdims=False) for u in offsets
        ]

    def halves(values):
        values = values.reshape(fabric.unit, units)
        return [
            jnp.concatenate(by_offset(values, [u ^ flip for u in fabric.offsets]))
            for flip in (0, core)
        ]

    inner_bias = halves(vec[9:])
    unit_gate = halves(inter_mask.astype(f32))

    def by_chunk(matrix):
        return [
            matrix[..., p * width + c * span : p * width + (c + 1) * span]
            for c in range(chunks)
            for p in range(3)
        ]

    def gathered(block):
        return Gather(fabric, block, [0])

    proj_low = proj_master.astype(bf16)
    heads = gathered(jnp.concatenate(by_chunk(proj_low), axis=1)[None])
    ffn = gathered(jnp.concatenate([up_master.astype(bf16), down_master.astype(bf16).T])[None])
    outer = gathered(proj_low[None, :, 3 * width :])
    for bit in top:
        heads.rows(bit)
    for bit in top:
        ffn.rows(bit)
        outer.rows(bit)
    head_one = Gather(fabric, heads.state[:, :, : 3 * span], heads.masks)
    head_two = Gather(fabric, heads.state[:, :, 3 * span :], heads.masks)
    split = up_master.shape[0]
    up = Gather(fabric, ffn.state[:, :split], ffn.masks)
    down = Gather(fabric, ffn.state[:, split:], ffn.masks)
    head_one.rows(near)
    for bit in far:
        head_two.rows(bit)
        head_one.rows(bit)
    head_one.rows(core)
    head_two.rows(near)
    head_two.rows(core)
    head_one.place(1, fabric.me)
    head_two.place(1, fabric.me)
    up.rows(near)
    up.place(fabric.unit, fabric.at_dp)
    for bit in far:
        down.columns(bit)
    outer.rows(near)
    w_qkv = [head_one.state] + [
        head_two.state[:, c * 3 * span : (c + 1) * 3 * span] for c in range(chunks - 1)
    ]

    bias_qkv = jnp.concatenate(
        by_chunk(jnp.concatenate([vec[0], jnp.zeros_like(vec[0]), vec[1]]))
    ).reshape(chunks, 3 * span)

    def project(c):
        return (dot(layer_input, w_qkv[c]) + bias_qkv[c]).astype(bf16)

    def attend(c, ctx):
        return attention_forward(c, qkv[c], valid_column, ends, head_mask, ctx, width)

    qkv, lse, ctx = [project(0)], [], None
    (qkv[0],) = hold_all((qkv[0],), [up, down, outer])
    for bit in far:
        up.columns(bit)
        outer.rows(bit)
    down.rows(near)
    down.place(fabric.unit, fabric.at_dp)
    for c in range(chunks - 1):
        if c:
            qkv.append(project(c))
        ctx, part = attend(c, ctx)
        lse.append(part)
    qkv.append(project(chunks - 1))
    ctx, qkv[-1] = hold_all((ctx, qkv[-1]), [up, down, outer])
    w_up, w_down = [[g.state, fabric.swap(g.state, core)] for g in (up, down)]
    outer.rows(core)
    ctx, part = attend(chunks - 1, ctx)
    lse.append(part)
    outer.place(1, fabric.me)
    w_out, w_dist = outer.state[:, :width], outer.state[:, width:]

    attn = (dot(ctx, w_out) + vec[2]) * hidden_gate
    hat_one, root_one = normalize(layer_input.astype(f32) + attn)
    first = hat_one * vec[3] + vec[4]
    first_low = first.astype(bf16)
    branch, active, slope = vec[5], [], []
    for u in range(2):
        inner = dot(first_low, w_up[u]) + inner_bias[u]
        cdf = 0.5 * (1.0 + lax.erf(inner * 0.7071067811865476))
        pdf = jnp.exp(-0.5 * inner * inner) * 0.3989422804014327
        active.append((inner * cdf * unit_gate[u]).astype(bf16))
        slope.append(((cdf + inner * pdf) * unit_gate[u]).astype(bf16))
        branch = branch + dot_cols(active[u], w_down[u])
    hat_two, root_two = normalize(first + branch * hidden_gate)
    out_low = (hat_two * vec[6] + vec[7]).astype(bf16)
    error = dot(out_low, w_dist) + vec[8] - teacher.astype(f32)
    half_sq = 0.5 * jnp.sum(valid * error * error)
    d_student = (valid * error).astype(bf16)
    g_dist = dot_rows(out_low, d_student).astype(bf16)
    g_bias_dist = jnp.sum(d_student.astype(f32), axis=0)

    d_out = cotangent.astype(f32) + dot_cols(d_student, w_dist)
    d_second, g_gain_two, g_shift_two = normalize_back(d_out, hat_two, root_two, vec[6])
    d_branch = (d_second * hidden_gate).astype(bf16)
    g_bias_two = jnp.sum(d_branch.astype(f32), axis=0)
    d_first = d_second
    g_up, g_down, g_inner_bias = [None] * 2, [None] * 2, [None] * 2

    def tiles(grad):
        return grad.astype(bf16).reshape(fabric.dp, -1, grad.shape[1])

    for u in (1, 0):
        g_down[u] = tiles(dot_rows(d_branch, active[u]))
        d_inner = (dot(d_branch, w_down[u]) * slope[u].astype(f32)).astype(bf16)
        g_up[u] = tiles(dot_rows(first_low, d_inner))
        g_inner_bias[u] = jnp.sum(d_inner.astype(f32), axis=0)
        d_first = d_first + dot_cols(d_inner, w_up[u])
        if u:
            d_branch, d_first, g_up[1], g_down[1] = hold(d_branch, d_first, g_up[1], g_down[1])
    r_up = Scatter(fabric, g_up[1], g_up[0], core, far[::-1] + [near] + top[::-1], dp_bits)
    r_down = Scatter(fabric, g_down[1], g_down[0], core, [near] + far[::-1] + top[::-1], dp_bits)
    r_up.tick()
    r_down.tick()
    (d_first,) = hold_all((d_first,), [r_up, r_down])

    d_first_sum, g_gain_one, g_shift_one = normalize_back(d_first, hat_one, root_one, vec[3])
    d_attn = (d_first_sum * hidden_gate).astype(bf16)
    g_bias_out = jnp.sum(d_attn.astype(f32), axis=0)
    g_out = dot_rows(ctx, d_attn).astype(bf16)
    d_ctx = dot_cols(d_attn, w_out).astype(bf16) * head_gate
    input_grad, bias_sums = d_first_sum, []

    first_order = [core] + far[::-1] + [near] + top[::-1]
    second_order = [core, near] + far[::-1] + top[::-1]

    def scatter(grad, order):
        return Scatter.of(fabric, grad.reshape(fabric.size, -1, grad.shape[1]), order, all_bits)

    r_outer = scatter(jnp.concatenate([g_out, g_dist], axis=1), second_order)
    early = [r_up, r_down]
    r_qkv = []
    for c in range(chunks):
        for chain in early + r_qkv:
            if len(chain.steps) >= len(top):
                chain.tick()
        if c == 0:
            early.append(r_outer)
        d_qkv, sums = attention_backward(c, qkv[c], d_ctx, ctx, lse[c], valid_column, ends, head_mask)
        bias_sums.append(sums[:2])
        d_qkv, d_ctx = hold_all((d_qkv, d_ctx), early + r_qkv)
        grad = dot_rows(layer_input, d_qkv).astype(bf16)
        r_qkv.append(scatter(grad, second_order if c % 2 else first_order))
        input_grad = input_grad + dot_cols(d_qkv, w_qkv[c])
    r_ffn = Scatter.merge([r_up, r_down])
    last = r_qkv + [r_outer]
    while any(len(chain.steps) >= len(top) for chain in last):
        for chain in last:
            if len(chain.steps) >= len(top):
                chain.tick()
    r_proj = Scatter.merge(last)
    for _ in range(len(top)):
        r_ffn.tick()
        r_proj.tick()
    g_proj, g_ffn = r_proj.state[0], r_ffn.state[0]
    g_proj = jnp.concatenate(
        [
            g_proj[:, (c * 3 + p) * span : (c * 3 + p + 1) * span]
            for p in range(3)
            for c in range(chunks)
        ]
        + [g_proj[:, 3 * width :]],
        axis=1,
    )
    g_up, g_down = g_ffn[:, :units], g_ffn[:, units:]

    pieces = {}
    for flip, value in zip((0, core), g_inner_bias):
        for u, piece in zip(fabric.offsets, value.reshape(-1, units)):
            pieces[u ^ flip] = piece
    g_inner_bias = by_offset(jnp.stack([pieces[u] for u in range(fabric.unit)]), range(fabric.unit))
    vector_grad = jnp.concatenate(
        [
            jnp.concatenate(bias_sums, axis=1),
            jnp.stack(
                [g_bias_out, g_gain_one, g_shift_one, g_bias_two, g_gain_two, g_shift_two, g_bias_dist]
            ),
            jnp.stack(g_inner_bias).reshape(-1, width),
            jnp.full((1, width), half_sq),
        ]
    )
    vector_grad = fabric.total(vector_grad)
    half_total, vector_grad = vector_grad[-1, 0], vector_grad[:-1]
    shard_sq = jnp.sum(g_proj * g_proj) + jnp.sum(g_ffn * g_ffn)
    shard_total = fabric.total_soon(jnp.full((8, LANES), shard_sq))[0, 0]
    grad_norm = jnp.sqrt(shard_total + jnp.sum(vector_grad * vector_grad))
    clip = jnp.minimum(1.0, CLIP_NORM / (grad_norm + 1e-06))
    distill_loss = 2.0 * half_total / (rows * fabric.size * width)
    return (
        out_low,
        input_grad,
        grad_norm,
        distill_loss,
        *adamw(proj_master, proj_first, proj_second, clip * g_proj, RATE_MATRIX, DECAY_MATRIX),
        *adamw(up_master, up_first, up_second, clip * g_up, RATE_MATRIX, DECAY_MATRIX),
        *adamw(down_master, down_first, down_second, clip * g_down.T, RATE_MATRIX, DECAY_MATRIX),
        *adamw(vector_master, vector_first, vector_second, clip * vector_grad, RATE_VECTOR, 0.0),
    )


def solution(mesh):
    by_token = P(AXES, None)
    tile, tile_back = P("dp", "unit"), P("unit", "dp")
    in_specs = (
        (by_token, by_token, by_token, P(AXES), by_token, P(), P(), P())
        + (by_token,) * 3
        + (tile,) * 3
        + (tile_back,) * 3
        + (P(),) * 3
    )
    out_specs = (
        (by_token, by_token, P(), P()) + (by_token,) * 3 + (tile,) * 3 + (tile_back,) * 3 + (P(),) * 3
    )
    return jax.shard_map(shards, mesh=mesh, in_specs=in_specs, out_specs=out_specs, check_vma=False)
```

time: 835 us -> 421 us (0.50)
  waiting for transfers between devices: 476 us -> 97.1 us
  starting transfers between devices: 0.33 us -> 55.2 us
  local copies, waits for them, and re-layouts: 84.7 us -> 29.9 us
  blocking collectives: 40.6 us -> 0 us
  other arithmetic: 26.5 us -> 43.2 us
  between operations: 21.8 us -> 9.23 us
    reduce_scatter x4 -> x0, waiting for transfers between devices: 297 us -> none  [the longest x2 219 us: scatter_tiles(): lax.psum_scatter(tiles, AXES, scatter_dimension=0, tiled=True).astype(f32)]
    all_gather x4 -> x0, waiting for transfers between devices: 179 us -> none  [the longest x2 117 us: gather_tiles(): tiles = lax.all_gather(shard, AXES, axis=0)]
    ppermute x0 -> x58, waiting for transfers between devices: none -> 97.1 us  [swap(): return lax.ppermute(value, AXES, [(i, i ^ bit) for i in range(self.size)])]
    ppermute x0 -> x58, starting transfers between devices: none -> 55.2 us  [swap(): return lax.ppermute(value, AXES, [(i, i ^ bit) for i in range(self.size)])]
    psum x1 -> x0, blocking collectives: 40.6 us -> none  [shards(): lax.psum((vector_grad, half_sq, shard_sq), AXES)]
    reshape x5 -> x2, local copies, waits for them, and re-layouts: 31.5 us -> 0.19 us  [the longest x1 0.18 us: split(): out.append(half.reshape(-1, *half.shape[2:]))]
    unnamed x68 -> x167, local copies, waits for them, and re-layouts: 38.8 us -> 21.8 us
    convert_element_type x2 -> x26, other arithmetic: 2.35 us -> 18.2 us  [the longest x23 16.7 us: add_low(): return (left.astype(f32) + right.astype(f32)).astype(bf16)]
  transfers between devices with their start and end apart: 8 -> 58, of which waited for: 7 -> 23; matrix products, arithmetic and copies ran while one was open for 14% -> 22% of each run, Pallas kernels for 10% -> 18%
where the time goes in v2:
time: 421 us; the launch traced here: 420 us
  waiting for transfers between devices  97.1 us (23%)
  matrix products  93.1 us (22%)
  Pallas kernels  91.9 us (22%)
  starting transfers between devices  55.2 us (13%)
  other arithmetic  43.2 us (10%)
  local copies, waits for them, and re-layouts  29.9 us (7%)
  between operations  9.23 us (2%)
    ppermute x58, waiting for transfers between devices, swap(): return lax.ppermute(value, AXES, [(i, i ^ bit) for i in range(self.size)])  97.1 us
    ppermute x58, starting transfers between devices, swap(): return lax.ppermute(value, AXES, [(i, i ^ bit) for i in range(self.size)])  55.2 us
    pallas_call x3, Pallas kernels, attention_backward(): pl.pallas_call(partial(backward_kernel, chunk), grid_spec=pltpu.PrefetchS...  45.4 us
    pallas_call x3, Pallas kernels, attention_forward(): pl.pallas_call(partial(forward_kernel, chunk), grid_spec=pltpu.PrefetchSc...  43.2 us
    dot_general x9, matrix products, dot_cols(): lax.dot_general(left, right, (((1,), (1,)), ((), ())), preferred_element_...  34.3 us
    dot_general x9, matrix products, dot(): return jnp.dot(left, right, preferred_element_type=f32)  31.7 us
    dot_general x9, matrix products, dot_rows(): lax.dot_general(left, right, (((0,), (0,)), ((), ())), preferred_element_...  27.1 us
    unnamed x167, local copies, waits for them, and re-layouts  21.8 us
  transfers between devices with their start and end apart: 58, of which 23 were waited for; matrix products, arithmetic and copies ran while one was open for 22% of the time, Pallas kernels for 18%

profile of v2, /device:TPU:0, one launch (start us, length us, event | category | flops | bytes accessed | tf_op | source)
XLA Modules:
  0.0 419.6 jit_solution(15390686168135098601)
XLA Ops:
  12.0 8.1 %collective-permute-done = bf16[1,24,2304]{2,1,0:T(8,128)(2,1)S(1)} collective-permute-done((bf16[1,24,2304]{2,1,0:T(8,128)(2,1)S(1)}, bf16[1,24,2304]{2,1,0:T(8,128)(2,1)S(1)}, u32[]{:S(2)}, u32[]{:S(2)}) %collective-permute-start) | collective-permute-done | bytes 110624 | tf_op jit(solution)/shard_map/ppermute | solution.py:288
  22.3 9.7 %collective-permute-done.1 = bf16[2,24,2304]{2,1,0:T(8,128)(2,1)S(1)} collective-permute-done((bf16[2,24,2304]{2,1,0:T(8,128)(2,1)S(1)}, bf16[2,24,2304]{2,1,0:T(8,128)(2,1)S(1)}, u32[]{:S(2)}, u32[]{:S(2)}) %collective-permute-start.1) | collective-permute-done | bytes 221216 | tf_op jit(solution)/shard_map/ppermute | solution.py:288
  39.4 4.3 %collective-permute-done.2 = bf16[4,24,1536]{2,1,0:T(8,128)(2,1)S(1)} collective-permute-done((bf16[4,24,1536]{2,1,0:T(8,128)(2,1)S(1)}, bf16[4,24,1536]{2,1,0:T(8,128)(2,1)S(1)}, u32[]{:S(2)}, u32[]{:S(2)}) %collective-permute-start.2) | collective-permute-done | bytes 294944 | tf_op jit(solution)/shard_map/ppermute | solution.py:288
  44.4 4.3 %collective-permute-done.6 = bf16[8,24,768]{2,1,0:T(8,128)(2,1)S(1)} collective-permute-done((bf16[8,24,768]{2,1,0:T(8,128)(2,1)S(1)}, bf16[8,24,768]{2,1,0:T(8,128)(2,1)S(1)}, u32[]{:S(2)}, u32[]{:S(2)}) %collective-permute-start.6) | collective-permute-done | bytes 294944 | tf_op jit(solution)/shard_map/ppermute | solution.py:288
  54.1 5.8 %collective-permute-done.3 = bf16[8,24,1536]{2,1,0:T(8,128)(2,1)S(1)} collective-permute-done((bf16[8,24,1536]{2,1,0:T(8,128)(2,1)S(1)}, bf16[8,24,1536]{2,1,0:T(8,128)(2,1)S(1)}, u32[]{:S(2)}, u32[]{:S(2)}) %collective-permute-start.3) | collective-permute-done | bytes 589856 | tf_op jit(solution)/shard_map/ppermute | solution.py:288
  62.8 6.6 %collective-permute-done.10 = bf16[4,96,768]{2,1,0:T(8,128)(2,1)S(1)} collective-permute-done((bf16[4,96,768]{2,1,0:T(8,128)(2,1)S(1)}, bf16[4,96,768]{2,1,0:T(8,128)(2,1)S(1)}, u32[]{:S(2)}, u32[]{:S(2)}) %collective-permute-start.10) | collective-permute-done | bytes 589856 | tf_op jit(solution)/shard_map/ppermute | solution.py:288
  73.9 12.4 %attention_forward.3 = (bf16[1024,768]{1,0:T(8,128)(2,1)S(1)}, f32[4,1,1024]{2,1,0:T(1,128)S(1)}) custom-call(s32[12]{0:T(128)S(1)} %copy-done.8, s32[3]{0:T(128)S(1)} %bitcast.278, bf16[1024,768]{1,0:T(8,128)(2,1)S(1)} %fusion.16.q_ref.k_ref.v_ref, bf16[1024,768]{1,0:T(8,128)(2,1)S(1)} %fusion.16.q_ref.k_ref.v_ref, ...), custom_call_target="tpu_custom_call" | custom-call | flops 12079595520 | bytes 2097152 | tf_op jit(solution)/shard_map/attention_forward/pallas_call | solution.py:133
  92.6 15.3 %attention_forward.4 = (bf16[1024,768]{1,0:T(8,128)(2,1)S(1)}, f32[4,1,1024]{2,1,0:T(1,128)S(1)}) custom-call(s32[12]{0:T(128)S(1)} %copy-done.8, s32[3]{0:T(128)S(1)} %bitcast.279, bf16[1024,768]{1,0:T(8,128)(2,1)S(1)} %fusion.15.q_ref.k_ref.v_ref, bf16[1024,768]{1,0:T(8,128)(2,1)S(1)} %fusion.15.q_ref.k_ref.v_ref, ...), custom_call_target="tpu_custom_call", output_to_operand_aliasing={{0}: (6, {})} | custom-call | flops 12079595520 | bytes 2097152 | tf_op jit(solution)/shard_map/attention_forward/pallas_call | solution.py:133
  120.2 15.5 %attention_forward.5 = (bf16[1024,768]{1,0:T(8,128)(2,1)S(1)}, f32[4,1,1024]{2,1,0:T(1,128)S(1)}) custom-call(s32[12]{0:T(128)S(1)} %copy-done.8, s32[3]{0:T(128)S(1)} %bitcast.280, bf16[1024,768]{1,0:T(8,128)(2,1)S(1)} %copy-done.16, bf16[1024,768]{1,0:T(8,128)(2,1)S(1)} %copy-done.16, ...), custom_call_target="tpu_custom_call", output_to_operand_aliasing={{0}: (6, {})} | custom-call | flops 12079595520 | bytes 2097152 | tf_op jit(solution)/shard_map/attention_forward/pallas_call | solution.py:133
  147.8 4.3 %fusion.79 = f32[1024,768]{0,1:T(8,128)} fusion(bf16[1024,1536]{1,0:T(8,128)(2,1)S(1)} %get-tuple-element.301, bf16[768,1536]{1,0:T(8,128)(2,1)S(1)} %bitcast.270), kind=kOutput, calls=%fused_computation.278 | convolution fusion | flops 2415919104 | bytes 8650752 | tf_op jit(solution)/shard_map/dot_general | solution.py:38
  152.2 5.7 %multiply_convert_fusion.2 = (bf16[1024,1536]{1,0:T(8,128)(2,1)}, f32[1024,1536]{1,0:T(8,128)S(1)}) fusion(f32[1536]{0:T(1024)S(1)} %pad_maximum_fusion.28, f32[1536]{0:T(1024)S(1)} %pad_maximum_fusion.27, bf16[1024,768]{0,1:T(8,128)(2,1)S(1)} %fusion.13, bf16[768,1536]{1,0:T(8,128)(2,1)S(1)} %collective-permute-done.19), kind=kOutput, calls=%fused_computation.18 | convolution fusion | flops 2426929152 | bytes 13381632 | tf_op jit(solution)/shard_map/dot_general | solution.py:30
  157.8 5.9 %fusion.78 = (f32[1024]{0:T(1024)S(1)}, f32[1024,768]{0,1:T(8,128)S(1)}) fusion(f32[768]{0:T(1024)S(1)} %convert_element_type.773, bf16[1024,1536]{1,0:T(8,128)(2,1)} %get-tuple-element.303, bf16[768,1536]{1,0:T(8,128)(2,1)S(1)} %collective-permute-done.20, f32[1024,768]{0,1:T(8,128)} %fusion.79, f32[768]{0:T(1024)S(1)} %get-tuple-element.209, ...), kind=kOutput, calls=%fused_computation.277 | convolution fusion | flops 2422995968 | bytes 14966784 | tf_op jit(solution)/shard_map/dot_general | solution.py:38
  172.0 6.3 %convolution_convert_fusion.2 = bf16[768,1536]{1,0:T(8,128)(2,1)} fusion(bf16[1024,768]{0,1:T(8,128)(2,1)S(1)} %get-tuple-element.88, bf16[1024,1536]{1,0:T(8,128)(2,1)} %get-tuple-element.303), kind=kOutput, calls=%fused_computation.26 | convolution fusion | flops 2417098752 | bytes 7077888 | tf_op jit(solution)/shard_map/dot_general | solution.py:34
  178.3 6.0 %convert_reduce_fusion = (f32[1536]{0:T(1024)S(1)}, bf16[1024,1536]{1,0:T(8,128)(2,1)S(1)}) fusion(f32[1536]{0:T(1024)S(1)} %pad_maximum_fusion.28, f32[1024,1536]{1,0:T(8,128)S(1)} %get-tuple-element.304, f32[1536]{0:T(1024)S(1)} %pad_maximum_fusion.27, bf16[1024,768]{0,1:T(8,128)(2,1)S(1)} %get-tuple-element.88, ...), kind=kOutput, calls=%fused_computation.14 | convolution fusion | flops 2441083392 | bytes 13387776 | tf_op jit(solution)/shard_map/dot_general | solution.py:30
  191.2 6.4 %convert_reduce_fusion.1 = (f32[1536]{0:T(1024)S(1)}, bf16[1024,1536]{1,0:T(8,128)(2,1)S(1)}) fusion(f32[1536]{0:T(1024)S(1)} %pad_maximum_fusion.26, f32[1024,1536]{1,0:T(8,128)S(1)} %get-tuple-element.302, f32[1536]{0:T(1024)S(1)} %pad_maximum_fusion.25, bf16[1024,768]{0,1:T(8,128)(2,1)S(1)} %get-tuple-element.88, bf16[768,1536]{1,0:T(8,128)(2,1)S(1)} %bitcast.271), kind=kOutput, calls=%fused_computation.15 | convolution fusion | flops 2441083392 | bytes 13387776 | tf_op jit(solution)/shard_map/dot_general | solution.py:30
  228.0 4.4 %copy.127 = bf16[768,1536]{1,0:T(8,128)(2,1)} copy(bf16[768,1536]{0,1:T(8,128)(2,1)} %pad_maximum_fusion.4) | data formatting | bytes 4718592 | tf_op jit(solution)/shard_map/concatenate | solution.py:584
  237.8 13.0 %attention_backward.3 = (bf16[1024,768]{1,0:T(8,128)(2,1)S(1)}, f32[8,256]{1,0:T(8,128)S(1)}) custom-call(s32[12]{0:T(128)S(1)} %copy-done.8, s32[3]{0:T(128)S(1)} %bitcast.281, bf16[1024,768]{1,0:T(8,128)(2,1)S(1)} %copy-done.21, bf16[1024,768]{1,0:T(8,128)(2,1)S(1)} %copy-done.21, bf16[1024,768]{1,0:T(8,128)(2,1)S(1)} %copy-done.21, ...), custom_call_target="tpu_custom_call" | custom-call | flops 12079595520 | bytes 4194304 | tf_op jit(solution)/shard_map/attention_backward/pallas_call | solution.py:220
  251.1 10.8 %collective-permute-done.23 = bf16[8,96,768]{2,1,0:T(8,128)(2,1)S(1)} collective-permute-done((bf16[8,96,768]{2,1,0:T(8,128)(2,1)}, bf16[8,96,768]{2,1,0:T(8,128)(2,1)S(1)}, u32[]{:S(2)}, u32[]{:S(2)}) %collective-permute-start.23) | collective-permute-done | bytes 1179680 | tf_op jit(solution)/shard_map/ppermute | solution.py:288
  267.8 16.1 %attention_backward.4 = (bf16[1024,768]{1,0:T(8,128)(2,1)S(1)}, f32[8,256]{1,0:T(8,128)S(1)}) custom-call(s32[12]{0:T(128)S(1)} %copy-done.8, s32[3]{0:T(128)S(1)} %bitcast.282, bf16[1024,768]{1,0:T(8,128)(2,1)S(1)} %copy-done.19, bf16[1024,768]{1,0:T(8,128)(2,1)S(1)} %copy-done.19, bf16[1024,768]{1,0:T(8,128)(2,1)S(1)} %copy-done.19, ...), custom_call_target="tpu_custom_call" | custom-call | flops 12079595520 | bytes 4194304 | tf_op jit(solution)/shard_map/attention_backward/pallas_call | solution.py:220
  288.9 16.3 %attention_backward.5 = (bf16[1024,768]{1,0:T(8,128)(2,1)S(1)}, f32[8,256]{1,0:T(8,128)S(1)}) custom-call(s32[12]{0:T(128)S(1)} %copy-done.8, s32[3]{0:T(128)S(1)} %bitcast.283, bf16[1024,768]{1,0:T(8,128)(2,1)S(1)} %copy-done.17, bf16[1024,768]{1,0:T(8,128)(2,1)S(1)} %copy-done.17, bf16[1024,768]{1,0:T(8,128)(2,1)S(1)} %copy-done.17, ...), custom_call_target="tpu_custom_call" | custom-call | flops 12079595520 | bytes 4194304 | tf_op jit(solution)/shard_map/attention_backward/pallas_call | solution.py:220
  323.5 4.5 %fusion.81 = f32[1024,768]{0,1:T(8,128)} fusion(bf16[1024,768]{1,0:T(8,128)(2,1)} %copy-done.10, bf16[768,768]{1,0:T(8,128)(2,1)S(1)} %bitcast.277), kind=kOutput, calls=%fused_computation.280 | convolution fusion | flops 1207959552 | bytes 5898240 | tf_op jit(solution)/shard_map/dot_general | solution.py:38
  363.6 10.7 %collective-permute-done.39 = bf16[2,24,3840]{2,1,0:T(8,128)(2,1)S(1)} collective-permute-done((bf16[2,24,3840]{2,1,0:T(8,128)(2,1)S(1)}, bf16[2,24,3840]{2,1,0:T(8,128)(2,1)S(1)}, u32[]{:S(2)}, u32[]{:S(2)}) %collective-permute-start.39) | collective-permute-done | bytes 368672 | tf_op jit(solution)/shard_map/ppermute | solution.py:288
  375.2 7.3 %collective-permute-done.40 = bf16[1,24,3840]{2,1,0:T(8,128)(2,1)S(1)} collective-permute-done((bf16[1,24,3840]{2,1,0:T(8,128)(2,1)S(1)}, bf16[1,24,3840]{2,1,0:T(8,128)(2,1)S(1)}, u32[]{:S(2)}, u32[]{:S(2)}) %collective-permute-start.40) | collective-permute-done | bytes 184352 | tf_op jit(solution)/shard_map/ppermute | solution.py:288
  401.7 5.6 %add_add_fusion = f32[1024,768]{0,1:T(8,128)} fusion(f32[1024,768]{0,1:T(8,128)S(1)} %fusion.27, f32[1024,768]{0,1:T(8,128)} %fusion.81, bf16[1024,768]{1,0:T(8,128)(2,1)S(1)} %copy-done.5, bf16[768,1536]{1,0:T(8,128)(2,1)S(1)} %bitcast.266, f32[1024]{0:T(1024)S(1)} %broadcast_multiply_fusion, f32[1024,768]{0,1:T(8,128)S(1)} %copy-done.24, ...), kind=kOutput, calls=%fused_computation.34 | convolution fusion | flops 1215823872 | bytes 18501632 | tf_op jit(solution)/shard_map/dot_general | solution.py:38
  (436 shorter events, 205.2 us)
Async XLA Ops:
  1.8 18.3 %collective-permute-start = (bf16[1,24,2304]{2,1,0:T(8,128)(2,1)S(1)}, bf16[1,24,2304]{2,1,0:T(8,128)(2,1)S(1)}, u32[]{:S(2)}, u32[]{:S(2)}) collective-permute-start(bf16[1,24,2304]{2,1,0:T(8,128)(2,1)S(1)} %bitcast.307), channel_id=1, source_target_pairs={{0,16},{1,17},{2,18},{3,19},{4,20},{5,21},{6,22},{7,23},{8,24},{9,... | collective-permute-start | bytes 331784 | tf_op jit(solution)/shard_map/ppermute | solution.py:288
  5.9 15.8 %collective-permute-start.12 = (bf16[1,24,1536]{2,1,0:T(8,128)(2,1)S(1)}, bf16[1,24,1536]{2,1,0:T(8,128)(2,1)S(1)}, u32[]{:S(2)}, u32[]{:S(2)}) collective-permute-start(bf16[1,24,1536]{2,1,0:T(8,128)(2,1)S(1)} %slice_bitcast_fusion), channel_id=1, source_target_pairs={{0,16},{1,17},{2,18},{3,19},{4,20},{5,21},{6,22},{7,23},{8,24},{9,... | collective-permute-start | bytes 221192 | tf_op jit(solution)/shard_map/ppermute | solution.py:288
  8.0 28.7 %collective-permute-start.8 = (bf16[1,192,768]{2,1,0:T(8,128)(2,1)S(1)}, bf16[1,192,768]{2,1,0:T(8,128)(2,1)S(1)}, u32[]{:S(2)}, u32[]{:S(2)}) collective-permute-start(bf16[1,192,768]{2,1,0:T(8,128)(2,1)S(1)} %maximum_bitcast_fusion), channel_id=1, source_target_pairs={{0,16},{1,17},{2,18},{3,19},{4,20},{5,21},{6,22},{7,23},{8,24},{9,... | collective-permute-start | bytes 884744 | tf_op jit(solution)/shard_map/ppermute | solution.py:288
  43.8 16.1 %collective-permute-start.3 = (bf16[8,24,1536]{2,1,0:T(8,128)(2,1)S(1)}, bf16[8,24,1536]{2,1,0:T(8,128)(2,1)S(1)}, u32[]{:S(2)}, u32[]{:S(2)}) collective-permute-start(bf16[8,24,1536]{2,1,0:T(8,128)(2,1)S(1)} %pad_maximum_fusion.11), channel_id=1, source_target_pairs={{0,4},{1,5},{2,6},{3,7},{4,0},{5,1},{6,2},{7,3},{8,12},{9,13},{10,... | collective-permute-start | bytes 1769480 | tf_op jit(solution)/shard_map/ppermute | solution.py:288
  52.0 17.3 %collective-permute-start.10 = (bf16[4,96,768]{2,1,0:T(8,128)(2,1)S(1)}, bf16[4,96,768]{2,1,0:T(8,128)(2,1)S(1)}, u32[]{:S(2)}, u32[]{:S(2)}) collective-permute-start(bf16[4,96,768]{2,1,0:T(8,128)(2,1)S(1)} %get-tuple-element.269), channel_id=1, source_target_pairs={{0,4},{1,5},{2,6},{3,7},{4,0},{5,1},{6,2},{7,3},{8,12},{9,13},{10,... | collective-permute-start | bytes 1769480 | tf_op jit(solution)/shard_map/ppermute | solution.py:288
  52.6 17.6 %collective-permute-start.11 = (bf16[4,96,768]{2,1,0:T(8,128)(2,1)S(1)}, bf16[4,96,768]{2,1,0:T(8,128)(2,1)S(1)}, u32[]{:S(2)}, u32[]{:S(2)}) collective-permute-start(bf16[4,96,768]{2,1,0:T(8,128)(2,1)S(1)} %get-tuple-element.268), channel_id=1, source_target_pairs={{0,2},{1,3},{2,0},{3,1},{4,6},{5,7},{6,4},{7,5},{8,10},{9,11},{10,... | collective-permute-start | bytes 1769480 | tf_op jit(solution)/shard_map/ppermute | solution.py:288
  60.0 27.7 %collective-permute-start.4 = (bf16[16,24,1536]{2,1,0:T(8,128)(2,1)S(1)}, bf16[16,24,1536]{2,1,0:T(8,128)(2,1)S(1)}, u32[]{:S(2)}, u32[]{:S(2)}) collective-permute-start(bf16[16,24,1536]{2,1,0:T(8,128)(2,1)S(1)} %pad_maximum_fusion.5), channel_id=1, source_target_pairs={{0,1},{1,0},{2,3},{3,2},{4,5},{5,4},{6,7},{7,6},{8,9},{9,8},{10,11... | collective-permute-start | bytes 3538952 | tf_op jit(solution)/shard_map/ppermute | solution.py:288
  70.2 16.3 %collective-permute-start.17 = (bf16[8,24,1536]{2,1,0:T(8,128)(2,1)S(1)}, bf16[8,24,1536]{2,1,0:T(8,128)(2,1)S(1)}, u32[]{:S(2)}, u32[]{:S(2)}) collective-permute-start(bf16[8,24,1536]{2,1,0:T(8,128)(2,1)S(1)} %pad_maximum_fusion.14), channel_id=1, source_target_pairs={{0,2},{1,3},{2,0},{3,1},{4,6},{5,7},{6,4},{7,5},{8,10},{9,11},{10,... | collective-permute-start | bytes 1769480 | tf_op jit(solution)/shard_map/ppermute | solution.py:288
  71.8 36.1 %collective-permute-start.16 = (bf16[4,96,1536]{2,1,0:T(8,128)(2,1)S(1)}, bf16[4,96,1536]{2,1,0:T(8,128)(2,1)S(1)}, u32[]{:S(2)}, u32[]{:S(2)}) collective-permute-start(bf16[4,96,1536]{2,1,0:T(8,128)(2,1)S(1)} %pad_maximum_fusion.9), channel_id=1, source_target_pairs={{0,4},{1,5},{2,6},{3,7},{4,0},{5,1},{6,2},{7,3},{8,12},{9,13},{10,... | collective-permute-start | bytes 3538952 | tf_op jit(solution)/shard_map/ppermute | solution.py:288
  73.4 36.4 %collective-permute-start.15 = (bf16[768,768]{1,0:T(8,128)(2,1)S(1)}, bf16[768,768]{1,0:T(8,128)(2,1)S(1)}, u32[]{:S(2)}, u32[]{:S(2)}) collective-permute-start(bf16[768,768]{1,0:T(8,128)(2,1)S(1)} %bitcast.267), channel_id=1, source_target_pairs={{0,2},{1,3},{2,0},{3,1},{4,6},{5,7},{6,4},{7,5},{8,10},{9,11},{10,... | collective-permute-start | bytes 3538952 | tf_op jit(solution)/shard_map/ppermute | solution.py:288
  111.4 24.3 %collective-permute-start.18 = (bf16[16,24,1536]{2,1,0:T(8,128)(2,1)}, bf16[16,24,1536]{2,1,0:T(8,128)(2,1)}, u32[]{:S(2)}, u32[]{:S(2)}) collective-permute-start(bf16[16,24,1536]{2,1,0:T(8,128)(2,1)} %pad_maximum_fusion.10), channel_id=1, source_target_pairs={{0,1},{1,0},{2,3},{3,2},{4,5},{5,4},{6,7},{7,6},{8,9},{9,8},{10,11... | collective-permute-start | bytes 3538952 | tf_op jit(solution)/shard_map/ppermute | solution.py:288
  116.7 35.4 %collective-permute-start.19 = (bf16[768,1536]{1,0:T(8,128)(2,1)}, bf16[768,1536]{1,0:T(8,128)(2,1)S(1)}, u32[]{:S(2)}, u32[]{:S(2)}) collective-permute-start(bf16[768,1536]{1,0:T(8,128)(2,1)} %pad_maximum_fusion.1), channel_id=1, source_target_pairs={{0,1},{1,0},{2,3},{3,2},{4,5},{5,4},{6,7},{7,6},{8,9},{9,8},{10,11... | collective-permute-start | bytes 7077896 | tf_op jit(solution)/shard_map/ppermute | solution.py:288
  117.3 40.6 %collective-permute-start.20 = (bf16[768,1536]{1,0:T(8,128)(2,1)S(1)}, bf16[768,1536]{1,0:T(8,128)(2,1)S(1)}, u32[]{:S(2)}, u32[]{:S(2)}) collective-permute-start(bf16[768,1536]{1,0:T(8,128)(2,1)S(1)} %bitcast.269), channel_id=1, source_target_pairs={{0,1},{1,0},{2,3},{3,2},{4,5},{5,4},{6,7},{7,6},{8,9},{9,8},{10,11... | collective-permute-start | bytes 7077896 | tf_op jit(solution)/shard_map/ppermute | solution.py:288
  197.7 15.6 %collective-permute-start.22 = (bf16[8,96,1536]{2,1,0:T(8,128)(2,1)}, bf16[8,96,1536]{2,1,0:T(8,128)(2,1)}, u32[]{:S(2)}, u32[]{:S(2)}) collective-permute-start(bf16[8,96,1536]{2,1,0:T(8,128)(2,1)} %bitcast.62), channel_id=1, source_target_pairs={{0,1},{1,0},{2,3},{3,2},{4,5},{5,4},{6,7},{7,6},{8,9},{9,8},{10,11... | collective-permute-start | bytes 7077896 | tf_op jit(solution)/shard_map/ppermute | solution.py:288
  198.2 20.2 %collective-permute-start.21 = (bf16[8,96,1536]{2,1,0:T(8,128)(2,1)}, bf16[8,96,1536]{2,1,0:T(8,128)(2,1)}, u32[]{:S(2)}, u32[]{:S(2)}) collective-permute-start(bf16[8,96,1536]{2,1,0:T(8,128)(2,1)} %bitcast.61), channel_id=1, source_target_pairs={{0,1},{1,0},{2,3},{3,2},{4,5},{5,4},{6,7},{7,6},{8,9},{9,8},{10,11... | collective-permute-start | bytes 7077896 | tf_op jit(solution)/shard_map/ppermute | solution.py:288
  232.4 29.8 %collective-permute-start.24 = (bf16[4,96,1536]{2,1,0:T(8,128)(2,1)}, bf16[4,96,1536]{2,1,0:T(8,128)(2,1)S(1)}, u32[]{:S(2)}, u32[]{:S(2)}) collective-permute-start(bf16[4,96,1536]{2,1,0:T(8,128)(2,1)} %fusion.18), channel_id=1, source_target_pairs={{0,4},{1,5},{2,6},{3,7},{4,0},{5,1},{6,2},{7,3},{8,12},{9,13},{10,... | collective-permute-start | bytes 3538952 | tf_op jit(solution)/shard_map/ppermute | solution.py:288
  234.0 27.9 %collective-permute-start.23 = (bf16[8,96,768]{2,1,0:T(8,128)(2,1)}, bf16[8,96,768]{2,1,0:T(8,128)(2,1)S(1)}, u32[]{:S(2)}, u32[]{:S(2)}) collective-permute-start(bf16[8,96,768]{2,1,0:T(8,128)(2,1)} %get-tuple-element.95), channel_id=1, source_target_pairs={{0,2},{1,3},{2,0},{3,1},{4,6},{5,7},{6,4},{7,5},{8,10},{9,11},{10,... | collective-permute-start | bytes 3538952 | tf_op jit(solution)/shard_map/ppermute | solution.py:288
  265.2 21.3 %collective-permute-start.28 = (bf16[16,24,768]{2,1,0:T(8,128)(2,1)S(1)}, bf16[16,24,768]{2,1,0:T(8,128)(2,1)S(1)}, u32[]{:S(2)}, u32[]{:S(2)}) collective-permute-start(bf16[16,24,768]{2,1,0:T(8,128)(2,1)S(1)} %get-tuple-element.265), channel_id=1, source_target_pairs={{0,1},{1,0},{2,3},{3,2},{4,5},{5,4},{6,7},{7,6},{8,9},{9,8},{10,11... | collective-permute-start | bytes 1769480 | tf_op jit(solution)/shard_map/ppermute | solution.py:288
  265.2 22.2 %collective-permute-start.27 = (bf16[16,24,1536]{2,1,0:T(8,128)(2,1)S(1)}, bf16[16,24,1536]{2,1,0:T(8,128)(2,1)S(1)}, u32[]{:S(2)}, u32[]{:S(2)}) collective-permute-start(bf16[16,24,1536]{2,1,0:T(8,128)(2,1)S(1)} %get-tuple-element.107), channel_id=1, source_target_pairs={{0,1},{1,0},{2,3},{3,2},{4,5},{5,4},{6,7},{7,6},{8,9},{9,8},{10,11... | collective-permute-start | bytes 3538952 | tf_op jit(solution)/shard_map/ppermute | solution.py:288
  265.7 19.8 %collective-permute-start.26 = (bf16[4,96,768]{2,1,0:T(8,128)(2,1)S(1)}, bf16[4,96,768]{2,1,0:T(8,128)(2,1)S(1)}, u32[]{:S(2)}, u32[]{:S(2)}) collective-permute-start(bf16[4,96,768]{2,1,0:T(8,128)(2,1)S(1)} %get-tuple-element.105), channel_id=1, source_target_pairs={{0,2},{1,3},{2,0},{3,1},{4,6},{5,7},{6,4},{7,5},{8,10},{9,11},{10,... | collective-permute-start | bytes 1769480 | tf_op jit(solution)/shard_map/ppermute | solution.py:288
  267.0 16.8 %collective-permute-start.25 = (bf16[4,96,768]{2,1,0:T(8,128)(2,1)S(1)}, bf16[4,96,768]{2,1,0:T(8,128)(2,1)S(1)}, u32[]{:S(2)}, u32[]{:S(2)}) collective-permute-start(bf16[4,96,768]{2,1,0:T(8,128)(2,1)S(1)} %get-tuple-element.103), channel_id=1, source_target_pairs={{0,4},{1,5},{2,6},{3,7},{4,0},{5,1},{6,2},{7,3},{8,12},{9,13},{10,... | collective-permute-start | bytes 1769480 | tf_op jit(solution)/shard_map/ppermute | solution.py:288
  310.2 19.5 %collective-permute-start.31 = (bf16[16,24,768]{2,1,0:T(8,128)(2,1)}, bf16[16,24,768]{2,1,0:T(8,128)(2,1)}, u32[]{:S(2)}, u32[]{:S(2)}) collective-permute-start(bf16[16,24,768]{2,1,0:T(8,128)(2,1)} %get-tuple-element.259), channel_id=1, source_target_pairs={{0,1},{1,0},{2,3},{3,2},{4,5},{5,4},{6,7},{7,6},{8,9},{9,8},{10,11... | collective-permute-start | bytes 1769480 | tf_op jit(solution)/shard_map/ppermute | solution.py:288
  329.5 59.1 %collective-permute-start.57 = (f32[14,768]{1,0:T(8,128)S(1)}, f32[14,768]{1,0:T(8,128)}, u32[]{:S(2)}, u32[]{:S(2)}) collective-permute-start(f32[14,768]{1,0:T(8,128)S(1)} %add.764), channel_id=1, source_target_pairs={{0,1},{1,0},{2,3},{3,2},{4,5},{5,4},{6,7},{7,6},{8,9},{9,8},{10,11... | collective-permute-start | bytes 129032 | tf_op jit(solution)/shard_map/ppermute | solution.py:288
  358.4 16.1 %collective-permute-start.42 = (bf16[1,96,1536]{2,1,0:T(8,128)(2,1)S(1)}, bf16[1,96,1536]{2,1,0:T(8,128)(2,1)S(1)}, u32[]{:S(2)}, u32[]{:S(2)}) collective-permute-start(bf16[1,96,1536]{2,1,0:T(8,128)(2,1)S(1)} %add_convert_fusion.14), channel_id=1, source_target_pairs={{0,16},{1,17},{2,18},{3,19},{4,20},{5,21},{6,22},{7,23},{8,24},{9,... | collective-permute-start | bytes 884744 | tf_op jit(solution)/shard_map/ppermute | solution.py:288
  (107 other events, 830.0 us)

commit v3 on v1

v3 whole, which is shorter than its diff:
```python
from functools import partial

import jax
import jax.numpy as jnp
from jax import lax
from jax.experimental import pallas as pl
from jax.experimental.pallas import tpu as pltpu
from jax.sharding import PartitionSpec as P

STEP = 10
EPS_NORM = 1e-05
BETA_ONE = 0.9
BETA_TWO = 0.999
ADAM_EPS = 1e-08
RATE_MATRIX = 0.1
RATE_VECTOR = 1.0
DECAY_MATRIX = 0.01
CLIP_NORM = 1.0
HEAD = 64
LANES = 128
PAIRS_PER_CHUNK = 2
VMEM_BYTES = 24 * 2**20
BRIEF = pl.CostEstimate(flops=1000, bytes_accessed=1000, transcendentals=0)
QUERY_ROWS = 512
WIDTHS = (528, 656, 784, 912)
MASKED = -1e30
AXES = ("dp", "unit")
f32 = jnp.float32
bf16 = jnp.bfloat16


def dot(left, right):
    return jnp.dot(left, right, preferred_element_type=f32)


def dot_rows(left, right):
    return lax.dot_general(left, right, (((0,), (0,)), ((), ())), preferred_element_type=f32)


def dot_cols(left, right):
    return lax.dot_general(left, right, (((1,), (1,)), ((), ())), preferred_element_type=f32)


def build_bias(bias_ref, valid_ref, end_one, end_two):
    count = bias_ref.shape[0]
    for start in range(0, count, QUERY_ROWS):
        key = lax.broadcasted_iota(jnp.int32, (count, QUERY_ROWS), 0)
        query = lax.broadcasted_iota(jnp.int32, (count, QUERY_ROWS), 1) + start
        seg_key = (key >= end_one).astype(jnp.int32) + (key >= end_two).astype(jnp.int32)
        seg_query = (query >= end_one).astype(jnp.int32) + (query >= end_two).astype(jnp.int32)
        allowed = (seg_key == seg_query) & ((valid_ref[...] > 0) | (key == query))
        bias_ref[:, start : start + QUERY_ROWS] = jnp.where(allowed, 0.0, MASKED)


def over_window(first_row, end_one, end_two, count, body):
    low = jnp.where(first_row < end_one, 0, jnp.where(first_row < end_two, end_one, end_two))
    last_row = first_row + QUERY_ROWS - 1
    high = jnp.where(last_row < end_one, end_one, jnp.where(last_row < end_two, end_two, count))
    low = (low // 16) * 16
    done = jnp.bool_(False)
    for width in [w for w in WIDTHS if w < count] + [count]:
        start = jnp.minimum(low, count - width)
        fits = (high - start) <= width
        run = fits & jnp.logical_not(done)

        @pl.when(run)
        def _(width=width, start=start):
            body(width, pl.multiple_of(start, 16))

        done = done | fits


def lanes_of(member):
    return lax.broadcasted_iota(jnp.int32, (1, LANES), 1) // HEAD == member


def only(value, member):
    return jnp.where(lanes_of(member), value, bf16(0))


def by_member(upper, lower):
    row = lax.broadcasted_iota(jnp.int32, (LANES, 1), 0)
    return jnp.where(row < HEAD, upper, lower).T


def forward_kernel(chunk, gate_ref, ends_ref, q_ref, k_ref, v_ref, valid_ref, *refs):
    ctx_ref, lse_ref, bias_ref = refs[-3:]
    count = q_ref.shape[0]
    end_one, end_two = ends_ref[0], ends_ref[1]
    pair = pl.program_id(0)

    @pl.when(pair == 0)
    def _():
        build_bias(bias_ref, valid_ref, end_one, end_two)

    place = 2 * (chunk * PAIRS_PER_CHUNK + pair)
    gates = [gate_ref[place + member].astype(f32) for member in range(2)]
    gate = jnp.where(lanes_of(0), gates[0], gates[1])

    def step(index, carry):
        first_row = pl.multiple_of(index * QUERY_ROWS, QUERY_ROWS)
        queries = pl.ds(first_row, QUERY_ROWS)

        def body(width, start):
            window = pl.ds(start, width)
            query = q_ref[queries, :] * bf16(HEAD**-0.5)
            keys, bias, value = k_ref[window, :], bias_ref[window, queries], v_ref[window, :]
            outs = []
            for member in range(2):
                scores = dot_cols(keys, only(query, member)) + bias
                peak = jnp.max(scores, axis=0, keepdims=True)
                expo = jnp.exp(scores - peak)
                total = jnp.sum(expo, axis=0, keepdims=True)
                outs.append(dot_rows(value, expo.astype(bf16)) * (1.0 / total))
                lse_ref[member, :, queries] = peak + jnp.log(total)
            ctx_ref[queries, :] = (by_member(*outs) * gate).astype(bf16)

        over_window(first_row, end_one, end_two, count, body)
        return carry

    lax.fori_loop(0, count // QUERY_ROWS, step, 0)


def pair_block(count, offset):
    return pl.BlockSpec((count, LANES), lambda i, gate, ends: (0, i + offset))


def attention_forward(chunk, qkv, valid_column, ends, gate, ctx_before, width):
    count, pairs = qkv.shape[0], PAIRS_PER_CHUNK
    in_specs = [
        pair_block(count, 0),
        pair_block(count, pairs),
        pair_block(count, 2 * pairs),
        pl.BlockSpec((count, 1), lambda i, gate, ends: (0, 0)),
    ]
    operands = [gate, ends, qkv, qkv, qkv, valid_column]
    aliases = {}
    if ctx_before is not None:
        in_specs.append(pl.BlockSpec(memory_space=pl.ANY))
        operands.append(ctx_before)
        aliases = {6: 0}
    return pl.pallas_call(
        partial(forward_kernel, chunk),
        grid_spec=pltpu.PrefetchScalarGridSpec(
            num_scalar_prefetch=2,
            grid=(pairs,),
            in_specs=in_specs,
            out_specs=[
                pair_block(count, chunk * pairs),
                pl.BlockSpec((2, 1, count), lambda i, gate, ends: (i, 0, 0)),
            ],
            scratch_shapes=[pltpu.VMEM((count, count), f32)],
        ),
        out_shape=[
            jax.ShapeDtypeStruct((count, width), bf16),
            jax.ShapeDtypeStruct((2 * pairs, 1, count), f32),
        ],
        input_output_aliases=aliases,
        compiler_params=pltpu.CompilerParams(vmem_limit_bytes=VMEM_BYTES),
        cost_estimate=BRIEF,
        name="attention_forward",
    )(*operands)


def backward_kernel(
    chunk, ends_ref, q_ref, k_ref, v_ref, do_ref, ctx_ref, lse_ref, valid_ref,
    grad_ref, sums_ref,
    bias_ref, dq_low, dk_total, dv_total, delta_ref,
):
    count = q_ref.shape[0]
    end_one, end_two = ends_ref[0], ends_ref[1]
    pair = pl.program_id(0)

    @pl.when(pair == 0)
    def _():
        build_bias(bias_ref, valid_ref, end_one, end_two)

    dk_total[...] = jnp.zeros_like(dk_total)
    dv_total[...] = jnp.zeros_like(dv_total)
    product = (do_ref[...].astype(f32) * ctx_ref[...].astype(f32)).T
    for member in range(2):
        rows = product[member * HEAD : (member + 1) * HEAD]
        delta_ref[member : member + 1, :] = jnp.sum(rows, axis=0, keepdims=True)

    def step(index, carry):
        first_row = pl.multiple_of(index * QUERY_ROWS, QUERY_ROWS)
        queries = pl.ds(first_row, QUERY_ROWS)

        def body(width, start):
            window = pl.ds(start, width)
            keys, value, bias = k_ref[window, :], v_ref[window, :], bias_ref[window, queries]
            query, grad = q_ref[queries, :] * bf16(HEAD**-0.5), do_ref[queries, :]
            d_queries, all_probs, all_scores, all_query, all_grad = [], [], [], [], []
            for member in range(2):
                own_query, own_grad = only(query, member), only(grad, member)
                probs = jnp.exp(dot_cols(keys, own_query) + bias - lse_ref[member, :, queries])
                d_probs = dot_cols(value, own_grad)
                d_scores = (probs * (d_probs - delta_ref[member : member + 1, queries])).astype(bf16)
                all_probs.append(probs.astype(bf16))
                all_scores.append(d_scores)
                all_query.append(own_query)
                all_grad.append(own_grad)
                d_queries.append(dot_rows(keys, d_scores))
            dv_total[window, :] += dot(
                jnp.concatenate(all_probs, axis=1), jnp.concatenate(all_grad, axis=0)
            )
            dk_total[window, :] += dot(
                jnp.concatenate(all_scores, axis=1), jnp.concatenate(all_query, axis=0)
            )
            dq_low[queries, :] = (by_member(*d_queries) * HEAD**-0.5).astype(bf16)

        over_window(first_row, end_one, end_two, count, body)
        return carry

    lax.fori_loop(0, count // QUERY_ROWS, step, 0)
    parts = (dq_low[...], dk_total[...].astype(bf16), dv_total[...].astype(bf16))
    for part, low in enumerate(parts):
        at = (part * PAIRS_PER_CHUNK + pair) * LANES
        grad_ref[:, pl.ds(pl.multiple_of(at, LANES), LANES)] = low
        if part != 1:
            sums_ref[part // 2 : part // 2 + 1, :] = jnp.sum(low.astype(f32), axis=0, keepdims=True)


def attention_backward(chunk, qkv, d_ctx, ctx, lse, valid_column, ends):
    count, pairs = qkv.shape[0], PAIRS_PER_CHUNK

    def block(offset):
        return pl.BlockSpec((count, LANES), lambda i, ends: (0, i + offset))

    return pl.pallas_call(
        partial(backward_kernel, chunk),
        grid_spec=pltpu.PrefetchScalarGridSpec(
            num_scalar_prefetch=1,
            grid=(pairs,),
            in_specs=[
                block(0),
                block(pairs),
                block(2 * pairs),
                block(chunk * pairs),
                block(chunk * pairs),
                pl.BlockSpec((2, 1, count), lambda i, ends: (i, 0, 0)),
                pl.BlockSpec((count, 1), lambda i, ends: (0, 0)),
            ],
            out_specs=[
                pl.BlockSpec(qkv.shape, lambda i, ends: (0, 0)),
                pl.BlockSpec((8, LANES), lambda i, ends: (0, i)),
            ],
            scratch_shapes=[
                pltpu.VMEM((count, count), f32),
                pltpu.VMEM((count, LANES), bf16),
                pltpu.VMEM((count, LANES), f32),
                pltpu.VMEM((count, LANES), f32),
                pltpu.VMEM((8, count), f32),
            ],
        ),
        out_shape=[
            jax.ShapeDtypeStruct(qkv.shape, bf16),
            jax.ShapeDtypeStruct((8, pairs * LANES), f32),
        ],
        compiler_params=pltpu.CompilerParams(vmem_limit_bytes=VMEM_BYTES),
        cost_estimate=BRIEF,
        name="attention_backward",
    )(ends, qkv, qkv, qkv, d_ctx, ctx, lse, valid_column)


def bits(size):
    return [1 << k for k in reversed(range(size.bit_length() - 1))]


def add_low(left, right):
    return (left.astype(f32) + right.astype(f32)).astype(bf16)


def hold(*values):
    return lax.optimization_barrier(values)


def hold(*values):
    return lax.optimization_barrier(values)


class Fabric:
    def __init__(self):
        self.dp, self.unit = lax.axis_size("dp"), lax.axis_size("unit")
        self.size = self.dp * self.unit
        self.at_unit = lax.axis_index("unit")
        self.at_dp = lax.axis_index("dp")
        self.me = self.at_dp * self.unit + self.at_unit
        dp_bits, unit_bits = [bit * self.unit for bit in bits(self.dp)], bits(self.unit)
        self.top, self.near, self.far, self.core = dp_bits[:-1], dp_bits[-1], unit_bits[:-1], unit_bits[-1]
        self.offsets = [0]
        for bit in self.far:
            self.offsets = self.offsets + [u ^ bit for u in self.offsets]

    def swap(self, value, bit):
        return lax.ppermute(value, AXES, [(i, i ^ bit) for i in range(self.size)])

    def assemble(self, block, places):
        flat = jnp.stack(places).astype(jnp.int32)

        def kernel(place_ref, source, out):
            for row in range(source.shape[0]):
                out[place_ref[row]] = source[row]

        whole = pl.BlockSpec(memory_space=pltpu.VMEM)
        out = pl.pallas_call(
            kernel,
            in_specs=[pl.BlockSpec(memory_space=pltpu.SMEM), whole],
            out_specs=whole,
            out_shape=jax.ShapeDtypeStruct(block.shape, block.dtype),
            compiler_params=pltpu.CompilerParams(vmem_limit_bytes=16 * 2**20),
            name="assemble",
        )(flat, block)
        return out.reshape(-1, block.shape[2])

    def by_device(self, block, masks):
        return self.assemble(block, [self.me ^ mask for mask in masks])

    def split(self, value, bit, left):
        own = bit if bit in left else -bit
        lower = 1 << (len(left) - 1 - left.index(own))
        value = value.reshape(value.shape[0] // (2 * lower), 2, lower, *value.shape[1:])
        mine = (self.me // bit) % 2 if own > 0 else 0
        out = []
        for choice in (1 - mine, mine):
            half = lax.dynamic_index_in_dim(value, choice, 1, keepdims=False)
            out.append(half.reshape(-1, *half.shape[2:]))
        return tuple(out)

    def total(self, value):
        for bit in bits(self.size)[::-1]:
            value = value + self.swap(value, bit)
        return value


def doubled(fabric, block, masks, bit):
    return jnp.concatenate([block, fabric.swap(block, bit)]), masks + [mask ^ bit for mask in masks]


class Scatter:
    def __init__(self, fabric, send, keep, steps, left):
        self.fabric, self.send, self.keep, self.steps = fabric, send, keep, list(steps)
        self.left = [r for r in left if abs(r) != steps[0]]

    @classmethod
    def of(cls, fabric, grad, steps, left):
        return cls(fabric, *fabric.split(grad, steps[0], left), steps, left)

    def start(self):
        self.other = self.fabric.swap(self.send, self.steps.pop(0))

    def finish(self):
        if not self.steps:
            self.result = (self.keep.astype(f32) + self.other.astype(f32))[0]
            return
        bit = self.steps[0]
        mine, theirs = (self.fabric.split(v, bit, self.left) for v in (self.keep, self.other))
        self.left = [r for r in self.left if abs(r) != bit]
        self.send, self.keep = (
            (a.astype(f32) + b.astype(f32)).astype(bf16) for a, b in zip(mine, theirs)
        )

    @classmethod
    def merge(cls, chains):
        first = chains[0]
        send, keep = (
            jnp.concatenate([getattr(c, name) for c in chains], axis=-1) for name in ("send", "keep")
        )
        return cls(first.fabric, send, keep, first.steps, first.left + first.steps[:1])


def beside(chains, compute):
    for chain in chains:
        chain.start()
    values, others = hold(compute(), [chain.other for chain in chains])
    for chain, other in zip(chains, others):
        chain.other = other
        chain.finish()
    return values


ROWS = 256


def row_call(kernel, count, blocks, constants, outs, sums, scratch, name):
    steps = count // ROWS

    def by_row(a):
        return pl.BlockSpec((ROWS, a.shape[1]), lambda i: (i, 0))

    def whole(a):
        return pl.BlockSpec(a.shape, lambda i: (0,) * len(a.shape))

    return pl.pallas_call(
        partial(kernel, steps),
        grid=(steps,),
        in_specs=[by_row(a) for a in blocks] + [whole(a) for a in constants],
        out_specs=[by_row(a) for a in outs] + [whole(a) for a in sums],
        out_shape=list(outs) + list(sums),
        scratch_shapes=scratch,
        compiler_params=pltpu.CompilerParams(vmem_limit_bytes=VMEM_BYTES),
        cost_estimate=BRIEF,
        name=name,
    )(*blocks, *constants)


def column_sums(value):
    return jnp.sum(value, axis=0, keepdims=True)


def normalize(value):
    mean = jnp.mean(value, axis=-1, keepdims=True)
    centred = value - mean
    root = lax.rsqrt(jnp.mean(centred * centred, axis=-1, keepdims=True) + EPS_NORM)
    return centred * root, root


def normalize_back(grad, hat, root, gain):
    scaled = grad * gain
    mean_one = jnp.mean(scaled, axis=-1, keepdims=True)
    mean_two = jnp.mean(scaled * hat, axis=-1, keepdims=True)
    return root * (scaled - mean_one - hat * mean_two)


def attention_out_kernel(steps, ctx, x, w_out, vec, gate, hat_out, root_out, low_out):
    attn = (dot(ctx[...], w_out[...]) + vec[2:3, :]) * gate[...]
    hat, root = normalize(x[...].astype(f32) + attn)
    hat_out[...] = hat
    root_out[...] = root
    low_out[...] = (hat * vec[3:4, :] + vec[4:5, :]).astype(bf16)


def head_kernel(
    steps, branch, hat_one, teacher, cotangent, valid, w_dist, vec, gate,
    low_out, d_second_out, d_branch_out, sums, g_dist, total,
):
    step = pl.program_id(0)

    @pl.when(step == 0)
    def _():
        sums[...] = jnp.zeros_like(sums)
        total[...] = jnp.zeros_like(total)

    keep = (valid[...] > 0).astype(f32)
    first = hat_one[...] * vec[3:4, :] + vec[4:5, :]
    hat, root = normalize(first + (branch[...] + vec[5:6, :]) * gate[...])
    low = (hat * vec[6:7, :] + vec[7:8, :]).astype(bf16)
    low_out[...] = low
    error = dot(low, w_dist[...]) + vec[8:9, :] - teacher[...].astype(f32)
    kept = keep * error
    d_student = kept.astype(bf16)
    d_out = cotangent[...].astype(f32) + dot_cols(d_student, w_dist[...])
    d_second = normalize_back(d_out, hat, root, vec[6:7, :])
    d_second_out[...] = d_second
    d_branch = (d_second * gate[...]).astype(bf16)
    d_branch_out[...] = d_branch
    sums[0:1, :] += column_sums(d_student.astype(f32))
    sums[1:2, :] += column_sums(d_out * hat)
    sums[2:3, :] += column_sums(d_out)
    sums[3:4, :] += column_sums(d_branch.astype(f32))
    sums[4:5, :] += column_sums(kept * error)
    total[...] += dot_rows(low, d_student)

    @pl.when(step == steps - 1)
    def _():
        g_dist[...] = total[...].astype(bf16)


def attention_out_back_kernel(
    steps, d_first, hat_one, root_one, ctx, w_out, vec, gate, head_gate,
    d_sum_out, d_ctx_out, sums, g_out, total,
):
    step = pl.program_id(0)

    @pl.when(step == 0)
    def _():
        sums[...] = jnp.zeros_like(sums)
        total[...] = jnp.zeros_like(total)

    hat, grad = hat_one[...], d_first[...]
    d_sum = normalize_back(grad, hat, root_one[...], vec[3:4, :])
    d_sum_out[...] = d_sum
    d_attn = (d_sum * gate[...]).astype(bf16)
    d_ctx_out[...] = (dot_cols(d_attn, w_out[...]) * head_gate[...]).astype(bf16)
    sums[0:1, :] += column_sums(d_attn.astype(f32))
    sums[1:2, :] += column_sums(grad * hat)
    sums[2:3, :] += column_sums(grad)
    total[...] += dot_rows(ctx[...], d_attn)

    @pl.when(step == steps - 1)
    def _():
        g_out[...] = total[...].astype(bf16)


def input_grad_kernel(steps, before, d_qkv, weight, out):
    out[...] = before[...] + dot_cols(d_qkv[...], weight[...])


def adamw(master, first, second, grad, rate, decay):
    first_new = BETA_ONE * first + (1.0 - BETA_ONE) * grad
    second_new = BETA_TWO * second + (1.0 - BETA_TWO) * grad * grad
    first_hat = first_new / (1.0 - BETA_ONE**STEP)
    second_hat = second_new / (1.0 - BETA_TWO**STEP)
    master_new = master - rate * (first_hat / (jnp.sqrt(second_hat) + ADAM_EPS) + decay * master)
    return master_new, first_new, second_new


def shards(
    layer_input, teacher, cotangent, key_valid, seg_lengths, head_mask, hidden_mask, inter_mask,
    proj_master, proj_first, proj_second, up_master, up_first, up_second,
    down_master, down_first, down_second, vector_master, vector_first, vector_second,
):
    fabric = Fabric()
    top, near, far, core = fabric.top, fabric.near, fabric.far, fabric.core
    all_bits = top + [near] + far + [core]
    rows, width = layer_input.shape
    span = PAIRS_PER_CHUNK * LANES
    chunks = width // span
    hidden_gate = hidden_mask.astype(f32)[None]
    valid_column = key_valid[:, None]
    ends = jnp.cumsum(seg_lengths[0])
    head_gate = jnp.repeat(head_mask.astype(f32), HEAD)[None]
    vec = vector_master
    tile_rows, units = up_master.shape

    offsets = fabric.offsets + [u ^ core for u in fabric.offsets]

    def by_offset(values, order):
        return [lax.dynamic_index_in_dim(values, fabric.at_unit ^ u, 0, keepdims=False) for u in order]

    inner_bias = by_offset(vec[9:].reshape(fabric.unit, units), offsets)
    unit_gate = by_offset(inter_mask.astype(f32).reshape(fabric.unit, units), offsets)

    def by_chunk(matrix):
        return [
            matrix[..., p * width + c * span : p * width + (c + 1) * span]
            for c in range(chunks)
            for p in range(3)
        ]

    proj_low = proj_master.astype(bf16)
    block, masks = jnp.concatenate(by_chunk(proj_low), axis=1)[None], [0]
    for bit in top:
        block, masks = doubled(fabric, block, masks, bit)
    ones, ones_masks, twos, twos_masks = block[..., : 3 * span], masks, block[..., 3 * span :], masks
    for bit in [near] + far + [core]:
        ones, ones_masks = doubled(fabric, ones, ones_masks, bit)
    for bit in far + [near]:
        twos, twos_masks = doubled(fabric, twos, twos_masks, bit)
    w_qkv = [fabric.by_device(ones, ones_masks)]

    rest = jnp.concatenate(
        [
            up_master.astype(bf16),
            down_master.astype(bf16).T,
            proj_low[:, 3 * width : 4 * width].reshape(-1, units),
            proj_low[:, 4 * width :].reshape(-1, units),
        ]
    )
    rest = lax.all_gather(rest, ("unit", "dp"), axis=0).reshape(fabric.unit, fabric.dp, -1, units)
    count = (rest.shape[2] - 2 * tile_rows) // 2


    def tile(u, at):
        size = (1, fabric.dp, tile_rows, units)
        return lax.dynamic_slice(rest, (fabric.at_unit ^ u, 0, at, 0), size).reshape(width, units)

    w_up, w_down = ([tile(u, at) for u in offsets] for at in (0, tile_rows))
    w_out, w_dist = (
        rest[:, :, at : at + count].transpose(1, 0, 2, 3).reshape(width, width)
        for at in (2 * tile_rows, 2 * tile_rows + count)
    )

    bias_qkv = jnp.concatenate(
        by_chunk(jnp.concatenate([vec[0], jnp.zeros_like(vec[0]), vec[1]]))
    ).reshape(chunks, 3 * span)

    def project(c):
        return (dot(layer_input, w_qkv[c]) + bias_qkv[c]).astype(bf16)

    qkv, lse, ctx = [project(0)], [], None

    def attend(ctx):
        c = len(lse)
        ctx, part = attention_forward(c, qkv[c], valid_column, ends, head_mask, ctx, width)
        lse.append(part)
        return ctx

    qkv[0], twos = hold(qkv[0], twos)
    other = fabric.swap(twos, core)
    ctx, other = hold(attend(ctx), other)
    late = fabric.by_device(
        jnp.concatenate([twos, other]), twos_masks + [mask ^ core for mask in twos_masks]
    )
    w_qkv += [late[:, c * 3 * span : (c + 1) * 3 * span] for c in range(chunks - 1)]
    for c in range(1, chunks):
        qkv.append(project(c))
        ctx = attend(ctx)

    def like(kind, *shape):
        return jax.ShapeDtypeStruct(shape or (rows, width), kind)

    hat_one, root_one, first_low = row_call(
        attention_out_kernel, rows, [ctx, layer_input], [w_out, vec, hidden_gate],
        [like(f32), like(f32, rows, 1), like(bf16)], [], [], "attention_out",
    )
    branch, active, slope = 0.0, [], []
    for u in range(fabric.unit):
        inner = dot(first_low, w_up[u]) + inner_bias[u]
        cdf = 0.5 * (1.0 + lax.erf(inner * 0.7071067811865476))
        pdf = jnp.exp(-0.5 * inner * inner) * 0.3989422804014327
        active.append((inner * cdf * unit_gate[u]).astype(bf16))
        slope.append((cdf + inner * pdf) * unit_gate[u])
        branch = branch + dot_cols(active[u], w_down[u])
    out_low, d_second, d_branch, head_sums, g_dist = row_call(
        head_kernel, rows, [branch, hat_one, teacher, cotangent, valid_column],
        [w_dist, vec, hidden_gate], [like(bf16), like(f32), like(bf16)],
        [like(f32, 8, width), like(bf16, width, width)],
        [pltpu.VMEM((width, width), f32)], "head",
    )

    unit_bits, dp_bits = far + [core], top + [near]
    blocks = len(fabric.offsets)
    block_bits = [-bit for bit in far[::-1]] + dp_bits

    def stacked(grads):
        return jnp.stack(grads).reshape(blocks * fabric.dp, tile_rows, units)

    def g_blocks(make):
        return [stacked([make(u) for u in side]) for side in (range(blocks, 2 * blocks), range(blocks))]

    g_down = g_blocks(lambda u: dot_rows(d_branch, active[u]).astype(bf16))
    r_down = Scatter(fabric, *g_down, [core, near] + far[::-1] + top[::-1], [core] + block_bits)
    r_down.start()
    d_inner = [(dot(d_branch, w_down[u]) * slope[u]).astype(bf16) for u in range(2 * blocks)]
    g_up = g_blocks(lambda u: dot_rows(first_low, d_inner[u]).astype(bf16))
    g_inner_bias = [jnp.sum(d.astype(f32), axis=0) for d in d_inner]
    *g_up, r_down.other = hold(*g_up, r_down.other)
    r_down.finish()
    r_up = Scatter(fabric, *g_up, [core] + far[::-1] + [near] + top[::-1], [core] + block_bits)
    order = [core] + far[::-1] + [near] + top[::-1]

    def feed_forward_back():
        return sum((dot_cols(d_inner[u], w_up[u]) for u in range(2 * blocks)), d_second)

    def attention_out_back():
        return row_call(
            attention_out_back_kernel, rows, [d_first, hat_one, root_one, ctx],
            [w_out, vec, hidden_gate, head_gate], [like(f32), like(bf16)],
            [like(f32, 8, width), like(bf16, width, width)],
            [pltpu.VMEM((width, width), f32)], "attention_out_back",
        )

    def attend_back(c):
        return attention_backward(c, qkv[c], d_ctx, ctx, lse[c], valid_column, ends)

    def add_input_grad(c):
        if c >= chunks:
            return [input_grad]
        return row_call(
            input_grad_kernel, rows, [input_grad, d_qkv[c]], [w_qkv[c]], [like(f32)], [], [], "input_grad"
        )

    def scatter(grad):
        grad = grad.reshape(fabric.size, -1, grad.shape[1])
        return Scatter.of(fabric, grad, order, dp_bits + unit_bits)

    r_down.start()
    d_first = beside([r_up], feed_forward_back)
    d_qkv, bias_sums, chains = [], [], []
    for c in range(chunks):
        if c == 0:

            def compute():
                global_parts = attention_out_back()
                return global_parts, attention_backward(
                    0, qkv[0], global_parts[1], ctx, lse[0], valid_column, ends
                )

            r_up.start()
            (d_first_sum, d_ctx, out_sums, g_out), (grad, sums) = compute()
            grad, d_ctx, r_up.other, r_down.other = hold(grad, d_ctx, r_up.other, r_down.other)
            r_up.finish()
            r_down.finish()
            rings = [r_up, r_down]
        else:
            while len(rings[0].steps) > len(top) + 1:
                beside(rings, lambda: 0)
            grad, sums = beside(rings + chains, lambda: attend_back(c))
            if len(rings) > 1 and len(rings[0].steps) == len(top):
                rings = [Scatter.merge(rings)]
        d_qkv.append(grad)
        bias_sums.append(sums[:2])
        mine = dot_rows(layer_input, grad).astype(bf16)
        if c == 0:
            mine = jnp.concatenate([mine, g_out, g_dist], axis=1)
        chains.append(scatter(mine))
    input_grad, c = d_first_sum, 0
    while len(chains[-1].steps) > len(top):
        busy = [chain for chain in rings + chains if chain.steps]
        (input_grad,) = beside(busy, lambda: add_input_grad(c))
        c += 1
    while c < chunks:
        (input_grad,) = add_input_grad(c)
        c += 1
    late = [chain for chain in chains if len(chain.steps) == len(top)]
    done = [chain for chain in chains if len(chain.steps) < len(top)]
    last = Scatter.merge(late)
    while last.steps:
        beside([chain for chain in rings + [last] + done if chain.steps], lambda: 0)
    results, at = [chain.result for chain in done], 0
    for chain in late:
        size = chain.keep.shape[-1]
        results.append(last.result[:, at : at + size])
        at += size
    g_proj = jnp.concatenate(
        [result[:, p * span : (p + 1) * span] for p in range(3) for result in results]
        + [results[0][:, 3 * span :]],
        axis=1,
    )
    g_up, g_down = rings[0].result[:, :units], rings[0].result[:, units:]
    g_inner_bias = dict(zip(offsets, g_inner_bias))
    g_inner_bias = by_offset(jnp.stack([g_inner_bias[u] for u in range(fabric.unit)]), range(fabric.unit))

    squares = sum(jnp.sum(g * g) for g in (g_proj, g_up, g_down))
    table = jnp.concatenate(
        [
            jnp.concatenate(bias_sums, axis=1),
            out_sums[:3],
            head_sums[3:4],
            head_sums[1:3],
            head_sums[:1],
            jnp.stack(g_inner_bias).reshape(-1, width),
            head_sums[4:5],
            jnp.full((1, width), squares),
        ]
    )
    table = fabric.total(table)
    vector_grad, error_total, square_total = table[:-2], jnp.sum(table[-2]), table[-1, 0]
    grad_norm = jnp.sqrt(square_total + jnp.sum(vector_grad * vector_grad))
    clip = jnp.minimum(1.0, CLIP_NORM / (grad_norm + 1e-06))
    distill_loss = error_total / (rows * fabric.size * width)
    return (
        out_low,
        input_grad,
        grad_norm,
        distill_loss,
        *adamw(proj_master, proj_first, proj_second, clip * g_proj, RATE_MATRIX, DECAY_MATRIX),
        *adamw(up_master, up_first, up_second, clip * g_up, RATE_MATRIX, DECAY_MATRIX),
        *adamw(down_master, down_first, down_second, clip * g_down.T, RATE_MATRIX, DECAY_MATRIX),
        *adamw(vector_master, vector_first, vector_second, clip * vector_grad, RATE_VECTOR, 0.0),
    )


def solution(mesh):
    by_token = P(AXES, None)
    tile, tile_back = P("dp", "unit"), P("unit", "dp")
    in_specs = (
        (by_token, by_token, by_token, P(AXES), by_token, P(), P(), P())
        + (by_token,) * 3
        + (tile,) * 3
        + (tile_back,) * 3
        + (P(),) * 3
    )
    out_specs = (
        (by_token, by_token, P(), P()) + (by_token,) * 3 + (tile,) * 3 + (tile_back,) * 3 + (P(),) * 3
    )
    return jax.shard_map(shards, mesh=mesh, in_specs=in_specs, out_specs=out_specs, check_vma=False)
```

time: 835 us -> 367 us (0.44)
  waiting for transfers between devices: 476 us -> 98.2 us
  local copies, waits for them, and re-layouts: 84.7 us -> 32.4 us
  blocking collectives: 40.6 us -> 0 us
  starting transfers between devices: 0.33 us -> 38.3 us
  matrix products: 94.3 us -> 59.8 us
    reduce_scatter x4 -> x0, waiting for transfers between devices: 297 us -> none  [the longest x2 219 us: scatter_tiles(): lax.psum_scatter(tiles, AXES, scatter_dimension=0, tiled=True).astype(f32)]
    all_gather x4 -> x1, waiting for transfers between devices: 179 us -> 22.1 us  [shards(): lax.all_gather(rest, ('unit', 'dp'), axis=0)]
    ppermute x0 -> x36, waiting for transfers between devices: none -> 76.1 us  [swap(): return lax.ppermute(value, AXES, [(i, i ^ bit) for i in range(self.size)])]
    psum x1 -> x0, blocking collectives: 40.6 us -> none  [shards(): lax.psum((vector_grad, half_sq, shard_sq), AXES)]
    ppermute x0 -> x36, starting transfers between devices: none -> 38.3 us  [swap(): return lax.ppermute(value, AXES, [(i, i ^ bit) for i in range(self.size)])]
    reshape x5 -> x1, local copies, waits for them, and re-layouts: 31.5 us -> 0.01 us  [shards(): inter_mask.astype(f32).reshape(fabric.unit, units)]
    unnamed x68 -> x165, local copies, waits for them, and re-layouts: 38.8 us -> 21.3 us
    dot_general x5 -> x8, matrix products: 29.1 us -> 13.4 us  [dot_cols(): lax.dot_general(left, right, (((1,), (1,)), ((), ())), preferred_element_...]
  transfers between devices with their start and end apart: 8 -> 37, of which waited for: 7 -> 23; matrix products, arithmetic and copies ran while one was open for 14% -> 15% of each run, Pallas kernels for 10% -> 19%
where the time goes in v3:
time: 367 us; the launch traced here: 363 us
  waiting for transfers between devices  98.2 us (27%)
  Pallas kernels  80.5 us (22%)
  matrix products  59.8 us (16%)
  starting transfers between devices  38.3 us (10%)
  local copies, waits for them, and re-layouts  32.4 us (9%)
  other arithmetic  31.2 us (9%)
  between operations  22.1 us (6%)
    ppermute x36, waiting for transfers between devices, swap(): return lax.ppermute(value, AXES, [(i, i ^ bit) for i in range(self.size)])  76.1 us
    ppermute x36, starting transfers between devices, swap(): return lax.ppermute(value, AXES, [(i, i ^ bit) for i in range(self.size)])  38.3 us
    pallas_call x3, Pallas kernels, attention_backward(): pl.pallas_call(partial(backward_kernel, chunk), grid_spec=pltpu.PrefetchS...  32.2 us
    dot_general x11, matrix products, dot(): return jnp.dot(left, right, preferred_element_type=f32)  30.3 us
    pallas_call x6, Pallas kernels, row_call(): pl.pallas_call(partial(kernel, steps), grid=(steps,), in_specs=[by_row(a)...  23.8 us
    pallas_call x3, Pallas kernels, attention_forward(): pl.pallas_call(partial(forward_kernel, chunk), grid_spec=pltpu.PrefetchSc...  23.1 us
    all_gather x1, waiting for transfers between devices, shards(): lax.all_gather(rest, ('unit', 'dp'), axis=0)  22.1 us
    unnamed x165, local copies, waits for them, and re-layouts  21.3 us
  transfers between devices with their start and end apart: 37, of which 23 were waited for; matrix products, arithmetic and copies ran while one was open for 15% of the time, Pallas kernels for 19%

profile of v3, /device:TPU:0, one launch (start us, length us, event | category | flops | bytes accessed | tf_op | source)
XLA Modules:
  0.0 362.7 jit_solution(11353039038293051602)
XLA Ops:
  11.1 4.1 %collective-permute-start = (bf16[1,24,2304]{2,1,0:T(8,128)(2,1)S(1)}, bf16[1,24,2304]{2,1,0:T(8,128)(2,1)S(1)}, u32[]{:S(2)}, u32[]{:S(2)}) collective-permute-start(bf16[1,24,2304]{2,1,0:T(8,128)(2,1)S(1)} %bitcast.353), channel_id=1, source_target_pairs={{0,16},{1,17},{2,18},{3,19},{4,20},{5,21},{6,22},{7,23},{8,24},{9,... | collective-permute-start | bytes 331784 | tf_op jit(solution)/shard_map/ppermute | solution.py:296
  15.2 5.4 %collective-permute-done = bf16[1,24,2304]{2,1,0:T(8,128)(2,1)S(1)} collective-permute-done((bf16[1,24,2304]{2,1,0:T(8,128)(2,1)S(1)}, bf16[1,24,2304]{2,1,0:T(8,128)(2,1)S(1)}, u32[]{:S(2)}, u32[]{:S(2)}) %collective-permute-start) | collective-permute-done | bytes 110624 | tf_op jit(solution)/shard_map/ppermute | solution.py:296
  21.5 8.6 %collective-permute-done.1 = bf16[2,24,2304]{2,1,0:T(8,128)(2,1)S(1)} collective-permute-done((bf16[2,24,2304]{2,1,0:T(8,128)(2,1)S(1)}, bf16[2,24,2304]{2,1,0:T(8,128)(2,1)S(1)}, u32[]{:S(2)}, u32[]{:S(2)}) %collective-permute-start.1) | collective-permute-done | bytes 221216 | tf_op jit(solution)/shard_map/ppermute | solution.py:296
  33.0 3.9 %collective-permute-done.2 = bf16[4,24,768]{2,1,0:T(8,128)(2,1)S(1)} collective-permute-done((bf16[4,24,768]{2,1,0:T(8,128)(2,1)S(1)}, bf16[4,24,768]{2,1,0:T(8,128)(2,1)S(1)}, u32[]{:S(2)}, u32[]{:S(2)}) %collective-permute-start.2) | collective-permute-done | bytes 147488 | tf_op jit(solution)/shard_map/ppermute | solution.py:296
  39.4 4.4 %collective-permute-done.3 = bf16[8,24,768]{2,1,0:T(8,128)(2,1)S(1)} collective-permute-done((bf16[8,24,768]{2,1,0:T(8,128)(2,1)S(1)}, bf16[8,24,768]{2,1,0:T(8,128)(2,1)S(1)}, u32[]{:S(2)}, u32[]{:S(2)}) %collective-permute-start.3) | collective-permute-done | bytes 294944 | tf_op jit(solution)/shard_map/ppermute | solution.py:296
  43.9 10.5 %collective-permute-done.6 = bf16[8,24,1536]{2,1,0:T(8,128)(2,1)S(1)} collective-permute-done((bf16[8,24,1536]{2,1,0:T(8,128)(2,1)S(1)}, bf16[8,24,1536]{2,1,0:T(8,128)(2,1)S(1)}, u32[]{:S(2)}, u32[]{:S(2)}) %collective-permute-start.6) | collective-permute-done | bytes 589856 | tf_op jit(solution)/shard_map/ppermute | solution.py:296
  61.3 7.7 %attention_forward.3 = (bf16[1024,768]{1,0:T(8,128)(2,1)S(1)}, f32[4,1,1024]{2,1,0:T(1,128)S(1)}) custom-call(s32[12]{0:T(128)S(1)} %copy-done.36, s32[3]{0:T(128)S(1)} %bitcast.307, bf16[1024,768]{1,0:T(8,128)(2,1)S(1)} %fusion.28.q_ref.k_ref.v_ref, bf16[1024,768]{1,0:T(8,128)(2,1)S(1)} %fusion.28.q_ref.k_ref.v_ref, ...), custom_call_target="tpu_custom_call" | custom-call | flops 1000 | bytes 1000 | tf_op jit(solution)/shard_map/attention_forward/pallas_call | solution.py:142
  73.7 7.9 %attention_forward.4 = (bf16[1024,768]{1,0:T(8,128)(2,1)S(1)}, f32[4,1,1024]{2,1,0:T(1,128)S(1)}) custom-call(s32[12]{0:T(128)S(1)} %copy-done.36, s32[3]{0:T(128)S(1)} %bitcast.308, bf16[1024,768]{1,0:T(8,128)(2,1)S(1)} %fusion.30.q_ref.k_ref.v_ref, bf16[1024,768]{1,0:T(8,128)(2,1)S(1)} %fusion.30.q_ref.k_ref.v_ref, ...), custom_call_target="tpu_custom_call", output_to_operand_aliasing={{0}: (6, {})} | custom-call | flops 1000 | bytes 1000 | tf_op jit(solution)/shard_map/attention_forward/pallas_call | solution.py:142
  83.0 7.6 %attention_forward.5 = (bf16[1024,768]{1,0:T(8,128)(2,1)S(1)}, f32[4,1,1024]{2,1,0:T(1,128)S(1)}) custom-call(s32[12]{0:T(128)S(1)} %copy-done.36, s32[3]{0:T(128)S(1)} %bitcast.309, bf16[1024,768]{1,0:T(8,128)(2,1)S(1)} %fusion.29.q_ref.k_ref.v_ref, bf16[1024,768]{1,0:T(8,128)(2,1)S(1)} %fusion.29.q_ref.k_ref.v_ref, ...), custom_call_target="tpu_custom_call", output_to_operand_aliasing={{0}: (6, {})} | custom-call | flops 1000 | bytes 1000 | tf_op jit(solution)/shard_map/attention_forward/pallas_call | solution.py:142
  90.6 22.1 %all-gather.3.cloned.1.call-done = bf16[7680,768]{1,0:T(8,128)(2,1)} async-done(((bf16[240,768]{1,0:T(8,128)(2,1)}), bf16[7680,768]{1,0:T(8,128)(2,1)}) %all-gather.3.cloned.1.call-update) | async-done | bytes 11796496 | tf_op jit(solution)/shard_map/all_gather | solution.py:560
  114.5 4.7 %constant_dynamic-slice_fusion.7 = (bf16[1,8,96,768]{3,2,1,0:T(8,128)(2,1)S(1)}, bf16[1,8,96,768]{3,2,1,0:T(8,128)(2,1)S(1)}, bf16[1,8,96,768]{3,2,1,0:T(8,128)(...) fusion(bf16[4,8,240,768]{3,2,1,0:T(8,128)(2,1)} %bitcast.315, ...), kind=kLoop, calls=%fused_computation.214 | loop fusion | bytes 18874384 | tf_op jit(solution)/shard_map/dynamic_slice | solution.py:566
  124.9 3.4 multiply_convert_fusion.2
  129.7 3.6 multiply_convert_fusion.3
  139.6 3.5 multiply_convert_fusion
  145.2 8.2 %head.1 = (bf16[1024,768]{1,0:T(8,128)(2,1)}, f32[1024,768]{1,0:T(8,128)S(1)}, bf16[1024,768]{1,0:T(8,128)(2,1)S(1)}, f32[8,768]{1,0:T(8,128)S(1)}, bf16[768,768]{1,0:T(8,128)(2,1)S(1)}) custom-call(f32[1024,768]{1,0:T(8,128)S(1)} %add_add_fusion.1.branch, f32[1024,768]{1,0:T(8,128)S(1)} %get-tuple-element.87.hat_one, bf16[1024,768]{1,0:T(8,128)(2,1)S(1)} %copy-done.22, ...), custom_call_target="tpu_custom_call" | custom-call | flops 1000 | bytes 1000 | tf_op jit(solution)/shard_map/head/pallas_call | solution.py:394
  203.2 5.3 %attention_out_back.1 = (f32[1024,768]{1,0:T(8,128)S(1)}, bf16[1024,768]{1,0:T(8,128)(2,1)S(1)}, f32[8,768]{1,0:T(8,128)S(1)}, bf16[768,768]{1,0:T(8,128)(2,1)S(1)}) custom-call(f32[1024,768]{1,0:T(8,128)S(1)} %copy-done.11, f32[1024,768]{1,0:T(8,128)S(1)} %copy-done.13, f32[1024,1]{1,0:T(8,128)S(1)} %copy-done.35, ...), custom_call_target="tpu_custom_call" | custom-call | flops 1000 | bytes 1000 | tf_op jit(solution)/shard_map/attention_out_back/pallas_call | solution.py:394
  208.6 11.6 %attention_backward.3 = (bf16[1024,768]{1,0:T(8,128)(2,1)S(1)}, f32[8,256]{1,0:T(8,128)S(1)}) custom-call(s32[3]{0:T(128)S(1)} %bitcast.310, bf16[1024,768]{1,0:T(8,128)(2,1)S(1)} %copy-done.3, bf16[1024,768]{1,0:T(8,128)(2,1)S(1)} %copy-done.3, bf16[1024,768]{1,0:T(8,128)(2,1)S(1)} %copy-done.3, bf16[1024,768]{1,0:T(8,128)(2,1)S(1)} %get-tuple-element.103.do_ref, ...), custom_call_target="tpu_custom_call" | custom-call | flops 1000 | bytes 1000 | tf_op jit(solution)/shard_map/attention_backward/pallas_call | solution.py:230
  221.2 3.4 collective-permute-done.10
  239.6 10.4 %attention_backward.4 = (bf16[1024,768]{1,0:T(8,128)(2,1)S(1)}, f32[8,256]{1,0:T(8,128)S(1)}) custom-call(s32[3]{0:T(128)S(1)} %bitcast.311, bf16[1024,768]{1,0:T(8,128)(2,1)S(1)} %copy-done.1, bf16[1024,768]{1,0:T(8,128)(2,1)S(1)} %copy-done.1, bf16[1024,768]{1,0:T(8,128)(2,1)S(1)} %copy-done.1, bf16[1024,768]{1,0:T(8,128)(2,1)S(1)} %copy-done.10, ...), custom_call_target="tpu_custom_call" | custom-call | flops 1000 | bytes 1000 | tf_op jit(solution)/shard_map/attention_backward/pallas_call | solution.py:230
  262.0 10.2 %attention_backward.5 = (bf16[1024,768]{1,0:T(8,128)(2,1)S(1)}, f32[8,256]{1,0:T(8,128)S(1)}) custom-call(s32[3]{0:T(128)S(1)} %bitcast.312, bf16[1024,768]{1,0:T(8,128)(2,1)S(1)} %fusion.29.q_ref.k_ref.v_ref, bf16[1024,768]{1,0:T(8,128)(2,1)S(1)} %fusion.29.q_ref.k_ref.v_ref, bf16[1024,768]{1,0:T(8,128)(2,1)S(1)} %fusion.29.q_ref.k_ref.v_ref, ...), custom_call_target="tpu_custom_call" | custom-call | flops 1000 | bytes 1000 | tf_op jit(solution)/shard_map/attention_backward/pallas_call | solution.py:230
  283.2 3.7 %collective-permute-done.20 = bf16[8,24,768]{2,1,0:T(8,128)(2,1)S(1)} collective-permute-done((bf16[8,24,768]{2,1,0:T(8,128)(2,1)S(1)}, bf16[8,24,768]{2,1,0:T(8,128)(2,1)S(1)}, u32[]{:S(2)}, u32[]{:S(2)}) %collective-permute-start.20) | collective-permute-done | bytes 294944 | tf_op jit(solution)/shard_map/ppermute | solution.py:296
  286.9 9.2 %collective-permute-done.18 = bf16[1,96,1536]{2,1,0:T(8,128)(2,1)S(1)} collective-permute-done((bf16[1,96,1536]{2,1,0:T(8,128)(2,1)S(1)}, bf16[1,96,1536]{2,1,0:T(8,128)(2,1)S(1)}, u32[]{:S(2)}, u32[]{:S(2)}) %collective-permute-start.18) | collective-permute-done | bytes 294944 | tf_op jit(solution)/shard_map/ppermute | solution.py:296
  328.6 3.6 collective-permute-done.32
  332.9 3.4 collective-permute-done.33
  (360 shorter events, 174.0 us)
Async XLA Ops:
  7.2 105.5 %all-gather.3.cloned.1.call-start = ((), (), s32[]{:S(2)}) async-start(), calls=%async_computation | async-start | bytes 12165120 | tf_op jit(solution)/shard_map/all_gather | solution.py:560
  11.1 9.5 %collective-permute-start = (bf16[1,24,2304]{2,1,0:T(8,128)(2,1)S(1)}, bf16[1,24,2304]{2,1,0:T(8,128)(2,1)S(1)}, u32[]{:S(2)}, u32[]{:S(2)}) collective-permute-start(bf16[1,24,2304]{2,1,0:T(8,128)(2,1)S(1)} %bitcast.353), channel_id=1, source_target_pairs={{0,16},{1,17},{2,18},{3,19},{4,20},{5,21},{6,22},{7,23},{8,24},{9,... | collective-permute-start | bytes 331784 | tf_op jit(solution)/shard_map/ppermute | solution.py:296
  20.7 9.3 %collective-permute-start.1 = (bf16[2,24,2304]{2,1,0:T(8,128)(2,1)S(1)}, bf16[2,24,2304]{2,1,0:T(8,128)(2,1)S(1)}, u32[]{:S(2)}, u32[]{:S(2)}) collective-permute-start(bf16[2,24,2304]{2,1,0:T(8,128)(2,1)S(1)} %pad_maximum_fusion.15), channel_id=1, source_target_pairs={{0,8},{1,9},{2,10},{3,11},{4,12},{5,13},{6,14},{7,15},{8,0},{9,1},... | collective-permute-start | bytes 663560 | tf_op jit(solution)/shard_map/ppermute | solution.py:296
  30.0 8.0 %collective-permute-start.5 = (bf16[4,24,1536]{2,1,0:T(8,128)(2,1)S(1)}, bf16[4,24,1536]{2,1,0:T(8,128)(2,1)S(1)}, u32[]{:S(2)}, u32[]{:S(2)}) collective-permute-start(bf16[4,24,1536]{2,1,0:T(8,128)(2,1)S(1)} %pad_maximum_fusion.12), channel_id=1, source_target_pairs={{0,2},{1,3},{2,0},{3,1},{4,6},{5,7},{6,4},{7,5},{8,10},{9,11},{10,... | collective-permute-start | bytes 884744 | tf_op jit(solution)/shard_map/ppermute | solution.py:296
  37.0 6.8 %collective-permute-start.3 = (bf16[8,24,768]{2,1,0:T(8,128)(2,1)S(1)}, bf16[8,24,768]{2,1,0:T(8,128)(2,1)S(1)}, u32[]{:S(2)}, u32[]{:S(2)}) collective-permute-start(bf16[8,24,768]{2,1,0:T(8,128)(2,1)S(1)} %pad_maximum_fusion.14), channel_id=1, source_target_pairs={{0,2},{1,3},{2,0},{3,1},{4,6},{5,7},{6,4},{7,5},{8,10},{9,11},{10,... | collective-permute-start | bytes 884744 | tf_op jit(solution)/shard_map/ppermute | solution.py:296
  38.1 16.3 %collective-permute-start.6 = (bf16[8,24,1536]{2,1,0:T(8,128)(2,1)S(1)}, bf16[8,24,1536]{2,1,0:T(8,128)(2,1)S(1)}, u32[]{:S(2)}, u32[]{:S(2)}) collective-permute-start(bf16[8,24,1536]{2,1,0:T(8,128)(2,1)S(1)} %pad_maximum_fusion.9), channel_id=1, source_target_pairs={{0,4},{1,5},{2,6},{3,7},{4,0},{5,1},{6,2},{7,3},{8,12},{9,13},{10,... | collective-permute-start | bytes 1769480 | tf_op jit(solution)/shard_map/ppermute | solution.py:296
  43.8 11.8 %collective-permute-start.4 = (bf16[16,24,768]{2,1,0:T(8,128)(2,1)S(1)}, bf16[16,24,768]{2,1,0:T(8,128)(2,1)S(1)}, u32[]{:S(2)}, u32[]{:S(2)}) collective-permute-start(bf16[16,24,768]{2,1,0:T(8,128)(2,1)S(1)} %pad_maximum_fusion.8), channel_id=1, source_target_pairs={{0,1},{1,0},{2,3},{3,2},{4,5},{5,4},{6,7},{7,6},{8,9},{9,8},{10,11... | collective-permute-start | bytes 1769480 | tf_op jit(solution)/shard_map/ppermute | solution.py:296
  58.6 10.4 %collective-permute-start.7 = (bf16[16,24,1536]{2,1,0:T(8,128)(2,1)}, bf16[16,24,1536]{2,1,0:T(8,128)(2,1)}, u32[]{:S(2)}, u32[]{:S(2)}) collective-permute-start(bf16[16,24,1536]{2,1,0:T(8,128)(2,1)} %pad_maximum_fusion.7), channel_id=1, source_target_pairs={{0,1},{1,0},{2,3},{3,2},{4,5},{5,4},{6,7},{7,6},{8,9},{9,8},{10,11... | collective-permute-start | bytes 3538952 | tf_op jit(solution)/shard_map/ppermute | solution.py:296
  156.5 24.5 %collective-permute-start.8 = (bf16[16,96,768]{2,1,0:T(8,128)(2,1)S(1)}, bf16[16,96,768]{2,1,0:T(8,128)(2,1)S(1)}, u32[]{:S(2)}, u32[]{:S(2)}) collective-permute-start(bf16[16,96,768]{2,1,0:T(8,128)(2,1)S(1)} %bitcast.328), channel_id=1, source_target_pairs={{0,1},{1,0},{2,3},{3,2},{4,5},{5,4},{6,7},{7,6},{8,9},{9,8},{10,11... | collective-permute-start | bytes 7077896 | tf_op jit(solution)/shard_map/ppermute | solution.py:296
  181.0 13.2 %collective-permute-start.9 = (bf16[16,96,768]{2,1,0:T(8,128)(2,1)S(1)}, bf16[16,96,768]{2,1,0:T(8,128)(2,1)S(1)}, u32[]{:S(2)}, u32[]{:S(2)}) collective-permute-start(bf16[16,96,768]{2,1,0:T(8,128)(2,1)S(1)} %bitcast.329), channel_id=1, source_target_pairs={{0,1},{1,0},{2,3},{3,2},{4,5},{5,4},{6,7},{7,6},{8,9},{9,8},{10,11... | collective-permute-start | bytes 7077896 | tf_op jit(solution)/shard_map/ppermute | solution.py:296
  192.8 28.4 %collective-permute-start.11 = (bf16[8,96,768]{2,1,0:T(8,128)(2,1)}, bf16[8,96,768]{2,1,0:T(8,128)(2,1)}, u32[]{:S(2)}, u32[]{:S(2)}) collective-permute-start(bf16[8,96,768]{2,1,0:T(8,128)(2,1)} %get-tuple-element.175), channel_id=1, source_target_pairs={{0,4},{1,5},{2,6},{3,7},{4,0},{5,1},{6,2},{7,3},{8,12},{9,13},{10,... | collective-permute-start | bytes 3538952 | tf_op jit(solution)/shard_map/ppermute | solution.py:296
  196.5 28.2 %collective-permute-start.10 = (bf16[8,96,768]{2,1,0:T(8,128)(2,1)}, bf16[8,96,768]{2,1,0:T(8,128)(2,1)}, u32[]{:S(2)}, u32[]{:S(2)}) collective-permute-start(bf16[8,96,768]{2,1,0:T(8,128)(2,1)} %get-tuple-element.177), channel_id=1, source_target_pairs={{0,2},{1,3},{2,0},{3,1},{4,6},{5,7},{6,4},{7,5},{8,10},{9,11},{10,... | collective-permute-start | bytes 3538952 | tf_op jit(solution)/shard_map/ppermute | solution.py:296
  228.5 21.5 %collective-permute-start.14 = (bf16[16,24,2304]{2,1,0:T(8,128)(2,1)}, bf16[16,24,2304]{2,1,0:T(8,128)(2,1)}, u32[]{:S(2)}, u32[]{:S(2)}) collective-permute-start(bf16[16,24,2304]{2,1,0:T(8,128)(2,1)} %get-tuple-element.181), channel_id=1, source_target_pairs={{0,1},{1,0},{2,3},{3,2},{4,5},{5,4},{6,7},{7,6},{8,9},{9,8},{10,11... | collective-permute-start | bytes 5308424 | tf_op jit(solution)/shard_map/ppermute | solution.py:296
  231.2 18.8 %collective-permute-start.13 = (bf16[4,96,768]{2,1,0:T(8,128)(2,1)}, bf16[4,96,768]{2,1,0:T(8,128)(2,1)}, u32[]{:S(2)}, u32[]{:S(2)}) collective-permute-start(bf16[4,96,768]{2,1,0:T(8,128)(2,1)} %get-tuple-element.185), channel_id=1, source_target_pairs={{0,2},{1,3},{2,0},{3,1},{4,6},{5,7},{6,4},{7,5},{8,10},{9,11},{10,... | collective-permute-start | bytes 1769480 | tf_op jit(solution)/shard_map/ppermute | solution.py:296
  234.2 15.8 %collective-permute-start.12 = (bf16[4,96,768]{2,1,0:T(8,128)(2,1)}, bf16[4,96,768]{2,1,0:T(8,128)(2,1)}, u32[]{:S(2)}, u32[]{:S(2)}) collective-permute-start(bf16[4,96,768]{2,1,0:T(8,128)(2,1)} %get-tuple-element.187), channel_id=1, source_target_pairs={{0,4},{1,5},{2,6},{3,7},{4,0},{5,1},{6,2},{7,3},{8,12},{9,13},{10,... | collective-permute-start | bytes 1769480 | tf_op jit(solution)/shard_map/ppermute | solution.py:296
  252.0 22.3 %collective-permute-start.16 = (bf16[8,24,2304]{2,1,0:T(8,128)(2,1)S(1)}, bf16[8,24,2304]{2,1,0:T(8,128)(2,1)S(1)}, u32[]{:S(2)}, u32[]{:S(2)}) collective-permute-start(bf16[8,24,2304]{2,1,0:T(8,128)(2,1)S(1)} %get-tuple-element.179), channel_id=1, source_target_pairs={{0,2},{1,3},{2,0},{3,1},{4,6},{5,7},{6,4},{7,5},{8,10},{9,11},{10,... | collective-permute-start | bytes 2654216 | tf_op jit(solution)/shard_map/ppermute | solution.py:296
  257.2 16.0 %collective-permute-start.15 = (bf16[2,96,1536]{2,1,0:T(8,128)(2,1)S(1)}, bf16[2,96,1536]{2,1,0:T(8,128)(2,1)S(1)}, u32[]{:S(2)}, u32[]{:S(2)}) collective-permute-start(bf16[2,96,1536]{2,1,0:T(8,128)(2,1)S(1)} %pad_maximum_fusion.10), channel_id=1, source_target_pairs={{0,8},{1,9},{2,10},{3,11},{4,12},{5,13},{6,14},{7,15},{8,0},{9,1},... | collective-permute-start | bytes 1769480 | tf_op jit(solution)/shard_map/ppermute | solution.py:296
  260.2 13.1 %collective-permute-start.17 = (bf16[16,24,768]{2,1,0:T(8,128)(2,1)S(1)}, bf16[16,24,768]{2,1,0:T(8,128)(2,1)S(1)}, u32[]{:S(2)}, u32[]{:S(2)}) collective-permute-start(bf16[16,24,768]{2,1,0:T(8,128)(2,1)S(1)} %get-tuple-element.197), channel_id=1, source_target_pairs={{0,1},{1,0},{2,3},{3,2},{4,5},{5,4},{6,7},{7,6},{8,9},{9,8},{10,11... | collective-permute-start | bytes 1769480 | tf_op jit(solution)/shard_map/ppermute | solution.py:296
  275.9 20.2 %collective-permute-start.21 = (bf16[16,24,768]{2,1,0:T(8,128)(2,1)S(1)}, bf16[16,24,768]{2,1,0:T(8,128)(2,1)S(1)}, u32[]{:S(2)}, u32[]{:S(2)}) collective-permute-start(bf16[16,24,768]{2,1,0:T(8,128)(2,1)S(1)} %get-tuple-element.193), channel_id=1, source_target_pairs={{0,1},{1,0},{2,3},{3,2},{4,5},{5,4},{6,7},{7,6},{8,9},{9,8},{10,11... | collective-permute-start | bytes 1769480 | tf_op jit(solution)/shard_map/ppermute | solution.py:296
  277.3 9.6 %collective-permute-start.20 = (bf16[8,24,768]{2,1,0:T(8,128)(2,1)S(1)}, bf16[8,24,768]{2,1,0:T(8,128)(2,1)S(1)}, u32[]{:S(2)}, u32[]{:S(2)}) collective-permute-start(bf16[8,24,768]{2,1,0:T(8,128)(2,1)S(1)} %get-tuple-element.195), channel_id=1, source_target_pairs={{0,2},{1,3},{2,0},{3,1},{4,6},{5,7},{6,4},{7,5},{8,10},{9,11},{10,... | collective-permute-start | bytes 884744 | tf_op jit(solution)/shard_map/ppermute | solution.py:296
  279.5 16.7 %collective-permute-start.19 = (bf16[4,24,2304]{2,1,0:T(8,128)(2,1)S(1)}, bf16[4,24,2304]{2,1,0:T(8,128)(2,1)S(1)}, u32[]{:S(2)}, u32[]{:S(2)}) collective-permute-start(bf16[4,24,2304]{2,1,0:T(8,128)(2,1)S(1)} %get-tuple-element.189), channel_id=1, source_target_pairs={{0,4},{1,5},{2,6},{3,7},{4,0},{5,1},{6,2},{7,3},{8,12},{9,13},{10,... | collective-permute-start | bytes 1327112 | tf_op jit(solution)/shard_map/ppermute | solution.py:296
  280.0 16.1 %collective-permute-start.18 = (bf16[1,96,1536]{2,1,0:T(8,128)(2,1)S(1)}, bf16[1,96,1536]{2,1,0:T(8,128)(2,1)S(1)}, u32[]{:S(2)}, u32[]{:S(2)}) collective-permute-start(bf16[1,96,1536]{2,1,0:T(8,128)(2,1)S(1)} %add_convert_fusion.20), channel_id=1, source_target_pairs={{0,16},{1,17},{2,18},{3,19},{4,20},{5,21},{6,22},{7,23},{8,24},{9,... | collective-permute-start | bytes 884744 | tf_op jit(solution)/shard_map/ppermute | solution.py:296
  296.3 9.0 %collective-permute-start.24 = (bf16[8,24,768]{2,1,0:T(8,128)(2,1)S(1)}, bf16[8,24,768]{2,1,0:T(8,128)(2,1)S(1)}, u32[]{:S(2)}, u32[]{:S(2)}) collective-permute-start(bf16[8,24,768]{2,1,0:T(8,128)(2,1)S(1)} %get-tuple-element.191), channel_id=1, source_target_pairs={{0,2},{1,3},{2,0},{3,1},{4,6},{5,7},{6,4},{7,5},{8,10},{9,11},{10,... | collective-permute-start | bytes 884744 | tf_op jit(solution)/shard_map/ppermute | solution.py:296
  305.4 7.8 %collective-permute-start.27 = (bf16[4,24,768]{2,1,0:T(8,128)(2,1)S(1)}, bf16[4,24,768]{2,1,0:T(8,128)(2,1)S(1)}, u32[]{:S(2)}, u32[]{:S(2)}) collective-permute-start(bf16[4,24,768]{2,1,0:T(8,128)(2,1)S(1)} %get-tuple-element.201), channel_id=1, source_target_pairs={{0,4},{1,5},{2,6},{3,7},{4,0},{5,1},{6,2},{7,3},{8,12},{9,13},{10,... | collective-permute-start | bytes 442376 | tf_op jit(solution)/shard_map/ppermute | solution.py:296
  (86 other events, 589.1 us)
Sparse Core Ops, SparseCore 0:
  11.5 101.1 all-gather.2

commit v4 on v3

--- a/solution.py
+++ b/solution.py
@@ -557,17 +557,16 @@
             proj_low[:, 4 * width :].reshape(-1, units),
         ]
     )
-    rest = lax.all_gather(rest, ("unit", "dp"), axis=0).reshape(fabric.unit, fabric.dp, -1, units)
+    rest = lax.all_gather(rest, AXES, axis=0).reshape(fabric.dp, fabric.unit, -1, units)
     count = (rest.shape[2] - 2 * tile_rows) // 2
 
-
     def tile(u, at):
-        size = (1, fabric.dp, tile_rows, units)
-        return lax.dynamic_slice(rest, (fabric.at_unit ^ u, 0, at, 0), size).reshape(width, units)
+        size = (fabric.dp, 1, tile_rows, units)
+        return lax.dynamic_slice(rest, (0, fabric.at_unit ^ u, at, 0), size).reshape(width, units)
 
     w_up, w_down = ([tile(u, at) for u in offsets] for at in (0, tile_rows))
     w_out, w_dist = (
-        rest[:, :, at : at + count].transpose(1, 0, 2, 3).reshape(width, width)
+        rest[:, :, at : at + count].reshape(width, width)
         for at in (2 * tile_rows, 2 * tile_rows + count)
     )
 

time: 367 us -> 367 us (level)
    unnamed x165 -> x175, local copies, waits for them, and re-layouts: 21.3 us -> 19.1 us
  transfers between devices with their start and end apart: 37 -> 37, of which waited for: 23 -> 27; matrix products, arithmetic and copies ran while one was open for 15% -> 15% of each run, Pallas kernels for 19% -> 19%
where the time goes in v4:
time: 367 us; the launch traced here: 363 us
  waiting for transfers between devices  99.4 us (27%)
  Pallas kernels  80.2 us (22%)
  matrix products  59.7 us (16%)
  starting transfers between devices  37.6 us (10%)
  local copies, waits for them, and re-layouts  32.1 us (9%)
  other arithmetic  31.4 us (9%)
  between operations  22.2 us (6%)
    ppermute x36, waiting for transfers between devices, swap(): return lax.ppermute(value, AXES, [(i, i ^ bit) for i in range(self.size)])  77.2 us
    ppermute x36, starting transfers between devices, swap(): return lax.ppermute(value, AXES, [(i, i ^ bit) for i in range(self.size)])  37.6 us
    pallas_call x3, Pallas kernels, attention_backward(): pl.pallas_call(partial(backward_kernel, chunk), grid_spec=pltpu.PrefetchS...  32.2 us
    dot_general x11, matrix products, dot(): return jnp.dot(left, right, preferred_element_type=f32)  30.3 us
    pallas_call x6, Pallas kernels, row_call(): pl.pallas_call(partial(kernel, steps), grid=(steps,), in_specs=[by_row(a)...  23.5 us
    pallas_call x3, Pallas kernels, attention_forward(): pl.pallas_call(partial(forward_kernel, chunk), grid_spec=pltpu.PrefetchSc...  23.1 us
    all_gather x1, waiting for transfers between devices, shards(): lax.all_gather(rest, AXES, axis=0)  22.2 us
    unnamed x175, local copies, waits for them, and re-layouts  19.1 us
  transfers between devices with their start and end apart: 37, of which 27 were waited for; matrix products, arithmetic and copies ran while one was open for 15% of the time, Pallas kernels for 19%

profile of v4, /device:TPU:0, one launch (start us, length us, event | category | flops | bytes accessed | tf_op | source)
XLA Modules:
  0.0 362.6 jit_solution(9900809603850662950)
XLA Ops:
  11.1 4.1 %collective-permute-start = (bf16[1,24,2304]{2,1,0:T(8,128)(2,1)S(1)}, bf16[1,24,2304]{2,1,0:T(8,128)(2,1)S(1)}, u32[]{:S(2)}, u32[]{:S(2)}) collective-permute-start(bf16[1,24,2304]{2,1,0:T(8,128)(2,1)S(1)} %bitcast.349), channel_id=1, source_target_pairs={{0,16},{1,17},{2,18},{3,19},{4,20},{5,21},{6,22},{7,23},{8,24},{9,... | collective-permute-start | bytes 331784 | tf_op jit(solution)/shard_map/ppermute | solution.py:296
  15.2 5.4 %collective-permute-done = bf16[1,24,2304]{2,1,0:T(8,128)(2,1)S(1)} collective-permute-done((bf16[1,24,2304]{2,1,0:T(8,128)(2,1)S(1)}, bf16[1,24,2304]{2,1,0:T(8,128)(2,1)S(1)}, u32[]{:S(2)}, u32[]{:S(2)}) %collective-permute-start) | collective-permute-done | bytes 110624 | tf_op jit(solution)/shard_map/ppermute | solution.py:296
  21.5 8.6 %collective-permute-done.1 = bf16[2,24,2304]{2,1,0:T(8,128)(2,1)S(1)} collective-permute-done((bf16[2,24,2304]{2,1,0:T(8,128)(2,1)S(1)}, bf16[2,24,2304]{2,1,0:T(8,128)(2,1)S(1)}, u32[]{:S(2)}, u32[]{:S(2)}) %collective-permute-start.1) | collective-permute-done | bytes 221216 | tf_op jit(solution)/shard_map/ppermute | solution.py:296
  33.0 4.0 %collective-permute-done.2 = bf16[4,24,768]{2,1,0:T(8,128)(2,1)S(1)} collective-permute-done((bf16[4,24,768]{2,1,0:T(8,128)(2,1)S(1)}, bf16[4,24,768]{2,1,0:T(8,128)(2,1)S(1)}, u32[]{:S(2)}, u32[]{:S(2)}) %collective-permute-start.2) | collective-permute-done | bytes 147488 | tf_op jit(solution)/shard_map/ppermute | solution.py:296
  39.4 4.3 %collective-permute-done.3 = bf16[8,24,768]{2,1,0:T(8,128)(2,1)S(1)} collective-permute-done((bf16[8,24,768]{2,1,0:T(8,128)(2,1)S(1)}, bf16[8,24,768]{2,1,0:T(8,128)(2,1)S(1)}, u32[]{:S(2)}, u32[]{:S(2)}) %collective-permute-start.3) | collective-permute-done | bytes 294944 | tf_op jit(solution)/shard_map/ppermute | solution.py:296
  44.0 10.5 %collective-permute-done.6 = bf16[8,24,1536]{2,1,0:T(8,128)(2,1)S(1)} collective-permute-done((bf16[8,24,1536]{2,1,0:T(8,128)(2,1)S(1)}, bf16[8,24,1536]{2,1,0:T(8,128)(2,1)S(1)}, u32[]{:S(2)}, u32[]{:S(2)}) %collective-permute-start.6) | collective-permute-done | bytes 589856 | tf_op jit(solution)/shard_map/ppermute | solution.py:296
  61.3 7.7 %attention_forward.3 = (bf16[1024,768]{1,0:T(8,128)(2,1)S(1)}, f32[4,1,1024]{2,1,0:T(1,128)S(1)}) custom-call(s32[12]{0:T(128)S(1)} %copy-done.36, s32[3]{0:T(128)S(1)} %bitcast.303, bf16[1024,768]{1,0:T(8,128)(2,1)S(1)} %fusion.28.q_ref.k_ref.v_ref, bf16[1024,768]{1,0:T(8,128)(2,1)S(1)} %fusion.28.q_ref.k_ref.v_ref, ...), custom_call_target="tpu_custom_call" | custom-call | flops 1000 | bytes 1000 | tf_op jit(solution)/shard_map/attention_forward/pallas_call | solution.py:142
  73.7 7.9 %attention_forward.4 = (bf16[1024,768]{1,0:T(8,128)(2,1)S(1)}, f32[4,1,1024]{2,1,0:T(1,128)S(1)}) custom-call(s32[12]{0:T(128)S(1)} %copy-done.36, s32[3]{0:T(128)S(1)} %bitcast.304, bf16[1024,768]{1,0:T(8,128)(2,1)S(1)} %fusion.30.q_ref.k_ref.v_ref, bf16[1024,768]{1,0:T(8,128)(2,1)S(1)} %fusion.30.q_ref.k_ref.v_ref, ...), custom_call_target="tpu_custom_call", output_to_operand_aliasing={{0}: (6, {})} | custom-call | flops 1000 | bytes 1000 | tf_op jit(solution)/shard_map/attention_forward/pallas_call | solution.py:142
  83.0 7.6 %attention_forward.5 = (bf16[1024,768]{1,0:T(8,128)(2,1)S(1)}, f32[4,1,1024]{2,1,0:T(1,128)S(1)}) custom-call(s32[12]{0:T(128)S(1)} %copy-done.36, s32[3]{0:T(128)S(1)} %bitcast.305, bf16[1024,768]{1,0:T(8,128)(2,1)S(1)} %fusion.29.q_ref.k_ref.v_ref, bf16[1024,768]{1,0:T(8,128)(2,1)S(1)} %fusion.29.q_ref.k_ref.v_ref, ...), custom_call_target="tpu_custom_call", output_to_operand_aliasing={{0}: (6, {})} | custom-call | flops 1000 | bytes 1000 | tf_op jit(solution)/shard_map/attention_forward/pallas_call | solution.py:142
  90.6 22.2 %all-gather.3.cloned.1.call-done = bf16[7680,768]{1,0:T(8,128)(2,1)} async-done(((bf16[240,768]{1,0:T(8,128)(2,1)}), bf16[7680,768]{1,0:T(8,128)(2,1)}) %all-gather.3.cloned.1.call-update) | async-done | bytes 11796496 | tf_op jit(solution)/shard_map/all_gather | solution.py:560
  114.6 6.7 %constant_dynamic-slice_fusion.7 = (bf16[8,1,96,768]{3,2,1,0:T(8,128)(2,1)}, bf16[8,1,96,768]{3,2,1,0:T(8,128)(2,1)S(1)}, bf16[8,1,96,768]{3,2,1,0:T(8,128)(2,1)...) fusion(bf16[8,4,240,768]{3,2,1,0:T(8,128)(2,1)} %bitcast.311, ...), kind=kLoop, calls=%fused_computation.214 | loop fusion | bytes 18874384 | tf_op jit(solution)/shard_map/dynamic_slice | solution.py:565
  124.3 3.4 multiply_convert_fusion.2
  129.2 3.7 %multiply_convert_fusion.3 = (bf16[1024,768]{1,0:T(8,128)(2,1)S(1)}, f32[1024,768]{1,0:T(8,128)}) fusion(f32[768]{0:T(1024)S(1)} %get-tuple-element.238, f32[768]{0:T(1024)S(1)} %get-tuple-element.147, bf16[1024,768]{1,0:T(8,128)(2,1)S(1)} %get-tuple-element.86, bf16[768,768]{1,0:T(8,128)(2,1)S(1)} %bitcast.337), kind=kOutput, calls=%fused_computation.45 | convolution fusion | flops 1213464576 | bytes 7477248 | tf_op jit(solution)/shard_map/dot_general | solution.py:33
  134.4 3.3 multiply_convert_fusion.1
  139.2 3.4 multiply_convert_fusion
  144.6 8.1 %head.1 = (bf16[1024,768]{1,0:T(8,128)(2,1)}, f32[1024,768]{1,0:T(8,128)S(1)}, bf16[1024,768]{1,0:T(8,128)(2,1)S(1)}, f32[8,768]{1,0:T(8,128)S(1)}, bf16[768,768]{1,0:T(8,128)(2,1)S(1)}) custom-call(f32[1024,768]{1,0:T(8,128)S(1)} %add_add_fusion.1.branch, f32[1024,768]{1,0:T(8,128)S(1)} %get-tuple-element.87.hat_one, bf16[1024,768]{1,0:T(8,128)(2,1)S(1)} %copy-done.22, ...), custom_call_target="tpu_custom_call" | custom-call | flops 1000 | bytes 1000 | tf_op jit(solution)/shard_map/head/pallas_call | solution.py:394
  187.4 3.4 add_add_fusion.d_first
  203.5 5.0 %attention_out_back.1 = (f32[1024,768]{1,0:T(8,128)S(1)}, bf16[1024,768]{1,0:T(8,128)(2,1)S(1)}, f32[8,768]{1,0:T(8,128)S(1)}, bf16[768,768]{1,0:T(8,128)(2,1)S(1)}) custom-call(f32[1024,768]{1,0:T(8,128)S(1)} %copy-done.11, f32[1024,768]{1,0:T(8,128)S(1)} %copy-done.13, f32[1024,1]{1,0:T(8,128)S(1)} %copy-done.35, ...), custom_call_target="tpu_custom_call" | custom-call | flops 1000 | bytes 1000 | tf_op jit(solution)/shard_map/attention_out_back/pallas_call | solution.py:394
  208.6 11.6 %attention_backward.3 = (bf16[1024,768]{1,0:T(8,128)(2,1)S(1)}, f32[8,256]{1,0:T(8,128)S(1)}) custom-call(s32[3]{0:T(128)S(1)} %bitcast.306, bf16[1024,768]{1,0:T(8,128)(2,1)S(1)} %copy-done.3, bf16[1024,768]{1,0:T(8,128)(2,1)S(1)} %copy-done.3, bf16[1024,768]{1,0:T(8,128)(2,1)S(1)} %copy-done.3, bf16[1024,768]{1,0:T(8,128)(2,1)S(1)} %get-tuple-element.103.do_ref, ...), custom_call_target="tpu_custom_call" | custom-call | flops 1000 | bytes 1000 | tf_op jit(solution)/shard_map/attention_backward/pallas_call | solution.py:230
  221.4 3.4 collective-permute-done.10
  239.8 10.4 %attention_backward.4 = (bf16[1024,768]{1,0:T(8,128)(2,1)S(1)}, f32[8,256]{1,0:T(8,128)S(1)}) custom-call(s32[3]{0:T(128)S(1)} %bitcast.307, bf16[1024,768]{1,0:T(8,128)(2,1)S(1)} %copy-done.1, bf16[1024,768]{1,0:T(8,128)(2,1)S(1)} %copy-done.1, bf16[1024,768]{1,0:T(8,128)(2,1)S(1)} %copy-done.1, bf16[1024,768]{1,0:T(8,128)(2,1)S(1)} %copy-done.10, ...), custom_call_target="tpu_custom_call" | custom-call | flops 1000 | bytes 1000 | tf_op jit(solution)/shard_map/attention_backward/pallas_call | solution.py:230
  260.8 10.2 %attention_backward.5 = (bf16[1024,768]{1,0:T(8,128)(2,1)S(1)}, f32[8,256]{1,0:T(8,128)S(1)}) custom-call(s32[3]{0:T(128)S(1)} %bitcast.308, bf16[1024,768]{1,0:T(8,128)(2,1)S(1)} %fusion.29.q_ref.k_ref.v_ref, bf16[1024,768]{1,0:T(8,128)(2,1)S(1)} %fusion.29.q_ref.k_ref.v_ref, bf16[1024,768]{1,0:T(8,128)(2,1)S(1)} %fusion.29.q_ref.k_ref.v_ref, ...), custom_call_target="tpu_custom_call" | custom-call | flops 1000 | bytes 1000 | tf_op jit(solution)/shard_map/attention_backward/pallas_call | solution.py:230
  285.8 10.7 %collective-permute-done.18 = bf16[1,96,1536]{2,1,0:T(8,128)(2,1)S(1)} collective-permute-done((bf16[1,96,1536]{2,1,0:T(8,128)(2,1)S(1)}, bf16[1,96,1536]{2,1,0:T(8,128)(2,1)S(1)}, u32[]{:S(2)}, u32[]{:S(2)}) %collective-permute-start.18) | collective-permute-done | bytes 294944 | tf_op jit(solution)/shard_map/ppermute | solution.py:296
  341.8 3.6 collective-permute-done.35
  (370 shorter events, 171.1 us)
Async XLA Ops:
  7.2 105.6 %all-gather.3.cloned.1.call-start = ((), (), s32[]{:S(2)}) async-start(), calls=%async_computation | async-start | bytes 12165120 | tf_op jit(solution)/shard_map/all_gather | solution.py:560
  11.1 9.5 %collective-permute-start = (bf16[1,24,2304]{2,1,0:T(8,128)(2,1)S(1)}, bf16[1,24,2304]{2,1,0:T(8,128)(2,1)S(1)}, u32[]{:S(2)}, u32[]{:S(2)}) collective-permute-start(bf16[1,24,2304]{2,1,0:T(8,128)(2,1)S(1)} %bitcast.349), channel_id=1, source_target_pairs={{0,16},{1,17},{2,18},{3,19},{4,20},{5,21},{6,22},{7,23},{8,24},{9,... | collective-permute-start | bytes 331784 | tf_op jit(solution)/shard_map/ppermute | solution.py:296
  20.7 9.4 %collective-permute-start.1 = (bf16[2,24,2304]{2,1,0:T(8,128)(2,1)S(1)}, bf16[2,24,2304]{2,1,0:T(8,128)(2,1)S(1)}, u32[]{:S(2)}, u32[]{:S(2)}) collective-permute-start(bf16[2,24,2304]{2,1,0:T(8,128)(2,1)S(1)} %pad_maximum_fusion.15), channel_id=1, source_target_pairs={{0,8},{1,9},{2,10},{3,11},{4,12},{5,13},{6,14},{7,15},{8,0},{9,1},... | collective-permute-start | bytes 663560 | tf_op jit(solution)/shard_map/ppermute | solution.py:296
  30.1 8.0 %collective-permute-start.5 = (bf16[4,24,1536]{2,1,0:T(8,128)(2,1)S(1)}, bf16[4,24,1536]{2,1,0:T(8,128)(2,1)S(1)}, u32[]{:S(2)}, u32[]{:S(2)}) collective-permute-start(bf16[4,24,1536]{2,1,0:T(8,128)(2,1)S(1)} %pad_maximum_fusion.12), channel_id=1, source_target_pairs={{0,2},{1,3},{2,0},{3,1},{4,6},{5,7},{6,4},{7,5},{8,10},{9,11},{10,... | collective-permute-start | bytes 884744 | tf_op jit(solution)/shard_map/ppermute | solution.py:296
  38.2 16.3 %collective-permute-start.6 = (bf16[8,24,1536]{2,1,0:T(8,128)(2,1)S(1)}, bf16[8,24,1536]{2,1,0:T(8,128)(2,1)S(1)}, u32[]{:S(2)}, u32[]{:S(2)}) collective-permute-start(bf16[8,24,1536]{2,1,0:T(8,128)(2,1)S(1)} %pad_maximum_fusion.9), channel_id=1, source_target_pairs={{0,4},{1,5},{2,6},{3,7},{4,0},{5,1},{6,2},{7,3},{8,12},{9,13},{10,... | collective-permute-start | bytes 1769480 | tf_op jit(solution)/shard_map/ppermute | solution.py:296
  43.9 11.8 %collective-permute-start.4 = (bf16[16,24,768]{2,1,0:T(8,128)(2,1)S(1)}, bf16[16,24,768]{2,1,0:T(8,128)(2,1)S(1)}, u32[]{:S(2)}, u32[]{:S(2)}) collective-permute-start(bf16[16,24,768]{2,1,0:T(8,128)(2,1)S(1)} %pad_maximum_fusion.8), channel_id=1, source_target_pairs={{0,1},{1,0},{2,3},{3,2},{4,5},{5,4},{6,7},{7,6},{8,9},{9,8},{10,11... | collective-permute-start | bytes 1769480 | tf_op jit(solution)/shard_map/ppermute | solution.py:296
  58.6 10.4 %collective-permute-start.7 = (bf16[16,24,1536]{2,1,0:T(8,128)(2,1)}, bf16[16,24,1536]{2,1,0:T(8,128)(2,1)}, u32[]{:S(2)}, u32[]{:S(2)}) collective-permute-start(bf16[16,24,1536]{2,1,0:T(8,128)(2,1)} %pad_maximum_fusion.7), channel_id=1, source_target_pairs={{0,1},{1,0},{2,3},{3,2},{4,5},{5,4},{6,7},{7,6},{8,9},{9,8},{10,11... | collective-permute-start | bytes 3538952 | tf_op jit(solution)/shard_map/ppermute | solution.py:296
  155.9 23.8 %collective-permute-start.8 = (bf16[16,96,768]{2,1,0:T(8,128)(2,1)S(1)}, bf16[16,96,768]{2,1,0:T(8,128)(2,1)S(1)}, u32[]{:S(2)}, u32[]{:S(2)}) collective-permute-start(bf16[16,96,768]{2,1,0:T(8,128)(2,1)S(1)} %bitcast.324), channel_id=1, source_target_pairs={{0,1},{1,0},{2,3},{3,2},{4,5},{5,4},{6,7},{7,6},{8,9},{9,8},{10,11... | collective-permute-start | bytes 7077896 | tf_op jit(solution)/shard_map/ppermute | solution.py:296
  179.7 14.8 %collective-permute-start.9 = (bf16[16,96,768]{2,1,0:T(8,128)(2,1)S(1)}, bf16[16,96,768]{2,1,0:T(8,128)(2,1)S(1)}, u32[]{:S(2)}, u32[]{:S(2)}) collective-permute-start(bf16[16,96,768]{2,1,0:T(8,128)(2,1)S(1)} %bitcast.325), channel_id=1, source_target_pairs={{0,1},{1,0},{2,3},{3,2},{4,5},{5,4},{6,7},{7,6},{8,9},{9,8},{10,11... | collective-permute-start | bytes 7077896 | tf_op jit(solution)/shard_map/ppermute | solution.py:296
  193.0 28.4 %collective-permute-start.11 = (bf16[8,96,768]{2,1,0:T(8,128)(2,1)}, bf16[8,96,768]{2,1,0:T(8,128)(2,1)}, u32[]{:S(2)}, u32[]{:S(2)}) collective-permute-start(bf16[8,96,768]{2,1,0:T(8,128)(2,1)} %get-tuple-element.175), channel_id=1, source_target_pairs={{0,4},{1,5},{2,6},{3,7},{4,0},{5,1},{6,2},{7,3},{8,12},{9,13},{10,... | collective-permute-start | bytes 3538952 | tf_op jit(solution)/shard_map/ppermute | solution.py:296
  196.7 28.2 %collective-permute-start.10 = (bf16[8,96,768]{2,1,0:T(8,128)(2,1)}, bf16[8,96,768]{2,1,0:T(8,128)(2,1)}, u32[]{:S(2)}, u32[]{:S(2)}) collective-permute-start(bf16[8,96,768]{2,1,0:T(8,128)(2,1)} %get-tuple-element.177), channel_id=1, source_target_pairs={{0,2},{1,3},{2,0},{3,1},{4,6},{5,7},{6,4},{7,5},{8,10},{9,11},{10,... | collective-permute-start | bytes 3538952 | tf_op jit(solution)/shard_map/ppermute | solution.py:296
  228.6 21.6 %collective-permute-start.14 = (bf16[16,24,2304]{2,1,0:T(8,128)(2,1)}, bf16[16,24,2304]{2,1,0:T(8,128)(2,1)}, u32[]{:S(2)}, u32[]{:S(2)}) collective-permute-start(bf16[16,24,2304]{2,1,0:T(8,128)(2,1)} %get-tuple-element.181), channel_id=1, source_target_pairs={{0,1},{1,0},{2,3},{3,2},{4,5},{5,4},{6,7},{7,6},{8,9},{9,8},{10,11... | collective-permute-start | bytes 5308424 | tf_op jit(solution)/shard_map/ppermute | solution.py:296
  231.3 18.8 %collective-permute-start.13 = (bf16[4,96,768]{2,1,0:T(8,128)(2,1)}, bf16[4,96,768]{2,1,0:T(8,128)(2,1)}, u32[]{:S(2)}, u32[]{:S(2)}) collective-permute-start(bf16[4,96,768]{2,1,0:T(8,128)(2,1)} %get-tuple-element.185), channel_id=1, source_target_pairs={{0,2},{1,3},{2,0},{3,1},{4,6},{5,7},{6,4},{7,5},{8,10},{9,11},{10,... | collective-permute-start | bytes 1769480 | tf_op jit(solution)/shard_map/ppermute | solution.py:296
  234.5 15.8 %collective-permute-start.12 = (bf16[4,96,768]{2,1,0:T(8,128)(2,1)}, bf16[4,96,768]{2,1,0:T(8,128)(2,1)}, u32[]{:S(2)}, u32[]{:S(2)}) collective-permute-start(bf16[4,96,768]{2,1,0:T(8,128)(2,1)} %get-tuple-element.187), channel_id=1, source_target_pairs={{0,4},{1,5},{2,6},{3,7},{4,0},{5,1},{6,2},{7,3},{8,12},{9,13},{10,... | collective-permute-start | bytes 1769480 | tf_op jit(solution)/shard_map/ppermute | solution.py:296
  252.3 22.2 %collective-permute-start.16 = (bf16[8,24,2304]{2,1,0:T(8,128)(2,1)S(1)}, bf16[8,24,2304]{2,1,0:T(8,128)(2,1)S(1)}, u32[]{:S(2)}, u32[]{:S(2)}) collective-permute-start(bf16[8,24,2304]{2,1,0:T(8,128)(2,1)S(1)} %get-tuple-element.179), channel_id=1, source_target_pairs={{0,2},{1,3},{2,0},{3,1},{4,6},{5,7},{6,4},{7,5},{8,10},{9,11},{10,... | collective-permute-start | bytes 2654216 | tf_op jit(solution)/shard_map/ppermute | solution.py:296
  256.2 15.9 %collective-permute-start.15 = (bf16[2,96,1536]{2,1,0:T(8,128)(2,1)S(1)}, bf16[2,96,1536]{2,1,0:T(8,128)(2,1)S(1)}, u32[]{:S(2)}, u32[]{:S(2)}) collective-permute-start(bf16[2,96,1536]{2,1,0:T(8,128)(2,1)S(1)} %pad_maximum_fusion.10), channel_id=1, source_target_pairs={{0,8},{1,9},{2,10},{3,11},{4,12},{5,13},{6,14},{7,15},{8,0},{9,1},... | collective-permute-start | bytes 1769480 | tf_op jit(solution)/shard_map/ppermute | solution.py:296
  258.9 13.2 %collective-permute-start.17 = (bf16[16,24,768]{2,1,0:T(8,128)(2,1)S(1)}, bf16[16,24,768]{2,1,0:T(8,128)(2,1)S(1)}, u32[]{:S(2)}, u32[]{:S(2)}) collective-permute-start(bf16[16,24,768]{2,1,0:T(8,128)(2,1)S(1)} %get-tuple-element.197), channel_id=1, source_target_pairs={{0,1},{1,0},{2,3},{3,2},{4,5},{5,4},{6,7},{7,6},{8,9},{9,8},{10,11... | collective-permute-start | bytes 1769480 | tf_op jit(solution)/shard_map/ppermute | solution.py:296
  276.1 20.5 %collective-permute-start.21 = (bf16[16,24,768]{2,1,0:T(8,128)(2,1)S(1)}, bf16[16,24,768]{2,1,0:T(8,128)(2,1)S(1)}, u32[]{:S(2)}, u32[]{:S(2)}) collective-permute-start(bf16[16,24,768]{2,1,0:T(8,128)(2,1)S(1)} %get-tuple-element.193), channel_id=1, source_target_pairs={{0,1},{1,0},{2,3},{3,2},{4,5},{5,4},{6,7},{7,6},{8,9},{9,8},{10,11... | collective-permute-start | bytes 1769480 | tf_op jit(solution)/shard_map/ppermute | solution.py:296
  276.5 9.4 %collective-permute-start.20 = (bf16[8,24,768]{2,1,0:T(8,128)(2,1)S(1)}, bf16[8,24,768]{2,1,0:T(8,128)(2,1)S(1)}, u32[]{:S(2)}, u32[]{:S(2)}) collective-permute-start(bf16[8,24,768]{2,1,0:T(8,128)(2,1)S(1)} %get-tuple-element.195), channel_id=1, source_target_pairs={{0,2},{1,3},{2,0},{3,1},{4,6},{5,7},{6,4},{7,5},{8,10},{9,11},{10,... | collective-permute-start | bytes 884744 | tf_op jit(solution)/shard_map/ppermute | solution.py:296
  278.8 17.7 %collective-permute-start.19 = (bf16[4,24,2304]{2,1,0:T(8,128)(2,1)S(1)}, bf16[4,24,2304]{2,1,0:T(8,128)(2,1)S(1)}, u32[]{:S(2)}, u32[]{:S(2)}) collective-permute-start(bf16[4,24,2304]{2,1,0:T(8,128)(2,1)S(1)} %get-tuple-element.189), channel_id=1, source_target_pairs={{0,4},{1,5},{2,6},{3,7},{4,0},{5,1},{6,2},{7,3},{8,12},{9,13},{10,... | collective-permute-start | bytes 1327112 | tf_op jit(solution)/shard_map/ppermute | solution.py:296
  280.8 15.8 %collective-permute-start.18 = (bf16[1,96,1536]{2,1,0:T(8,128)(2,1)S(1)}, bf16[1,96,1536]{2,1,0:T(8,128)(2,1)S(1)}, u32[]{:S(2)}, u32[]{:S(2)}) collective-permute-start(bf16[1,96,1536]{2,1,0:T(8,128)(2,1)S(1)} %add_convert_fusion.20), channel_id=1, source_target_pairs={{0,16},{1,17},{2,18},{3,19},{4,20},{5,21},{6,22},{7,23},{8,24},{9,... | collective-permute-start | bytes 884744 | tf_op jit(solution)/shard_map/ppermute | solution.py:296
  296.7 9.0 %collective-permute-start.24 = (bf16[8,24,768]{2,1,0:T(8,128)(2,1)S(1)}, bf16[8,24,768]{2,1,0:T(8,128)(2,1)S(1)}, u32[]{:S(2)}, u32[]{:S(2)}) collective-permute-start(bf16[8,24,768]{2,1,0:T(8,128)(2,1)S(1)} %get-tuple-element.191), channel_id=1, source_target_pairs={{0,2},{1,3},{2,0},{3,1},{4,6},{5,7},{6,4},{7,5},{8,10},{9,11},{10,... | collective-permute-start | bytes 884744 | tf_op jit(solution)/shard_map/ppermute | solution.py:296
  297.9 6.8 %collective-permute-start.22 = (bf16[2,24,2304]{2,1,0:T(8,128)(2,1)S(1)}, bf16[2,24,2304]{2,1,0:T(8,128)(2,1)S(1)}, u32[]{:S(2)}, u32[]{:S(2)}) collective-permute-start(bf16[2,24,2304]{2,1,0:T(8,128)(2,1)S(1)} %fusion.58), channel_id=1, source_target_pairs={{0,8},{1,9},{2,10},{3,11},{4,12},{5,13},{6,14},{7,15},{8,0},{9,1},... | collective-permute-start | bytes 663560 | tf_op jit(solution)/shard_map/ppermute | solution.py:296
  305.8 6.8 %collective-permute-start.27 = (bf16[4,24,768]{2,1,0:T(8,128)(2,1)S(1)}, bf16[4,24,768]{2,1,0:T(8,128)(2,1)S(1)}, u32[]{:S(2)}, u32[]{:S(2)}) collective-permute-start(bf16[4,24,768]{2,1,0:T(8,128)(2,1)S(1)} %get-tuple-element.201), channel_id=1, source_target_pairs={{0,4},{1,5},{2,6},{3,7},{4,0},{5,1},{6,2},{7,3},{8,12},{9,13},{10,... | collective-permute-start | bytes 442376 | tf_op jit(solution)/shard_map/ppermute | solution.py:296
  (92 other events, 605.3 us)
Sparse Core Ops, SparseCore 0:
  11.5 101.2 all-gather.2
